TPU v7x, 32 devices: a whole 2x2x4 slice. The times are simulated.
32 devices in a mesh: tm: 8 (over y, x, core), head: 4 (over z).
Axes of the slice: x: 2, y: 2, z: 4, core: 2. Of those that a mesh axis runs over, the one named last changes fastest.
Arguments:
- query_vectors: bfloat16 [8192, 4096], P('tm', 'head'), may hold values from -6 to 6
- key_vectors: bfloat16 [8192, 4096], P('tm', 'head'), may hold values from -0.125 to 0.125
- value_vectors: bfloat16 [8192, 4096], P('tm', 'head'), may hold values from -6 to 6
- grad_out: bfloat16 [8192, 4096], P('tm', 'head'), may hold values from -8 to 8
- out_weight: bfloat16 [4096, 4096], P('tm', 'head'), may hold values from -0.09375 to 0.09375
- periods: int32 [32], P('head'), may hold values from 1 to 128, as said below
- log_decay: float32 [32, 8192], P('head', 'tm'), may hold values from -0.1109375 to 0, as said below
Outputs:
- query_gradient: bfloat16 [8192, 4096], P('tm', 'head')
- key_gradient: bfloat16 [8192, 4096], P('tm', 'head')
- value_gradient: bfloat16 [8192, 4096], P('tm', 'head')
- grad_weight: float32 [4096, 4096], P('tm', 'head')
Inputs may be any that keep to these rules, and one draw needn't show every extreme that they name: `periods`: some head has period 1 and some head period 128. `log_decay`: Negative.
All inputs are finite; a program needn't handle non-finite values.
Results may differ from a plain program's by a relative error of at most 0.023.
Values may be sent and summed in bfloat16 or wider, within the bound.
No kernel may reach another device: no remote copies, remote signals or barrier semaphores. Data moves between devices by JAX's collectives and lax.ppermute only.
A program may use at most 128 MiB of HBM per device.

v0:
```python
import jax
import jax.numpy as jnp
from jax import lax
from jax.sharding import PartitionSpec as P

DK = 128
BLK = 512


def prefix(value, axis, combine, identity, reverse):
    count, place = (lax.axis_size(axis), lax.axis_index(axis))
    everything = jax.tree.map(
        lambda part, kind: lax.all_gather(part.astype(kind), axis),
        value,
        (jnp.bfloat16, jnp.bfloat16),
    )
    start = jax.tree.map(
        lambda part, zero: jnp.broadcast_to(jnp.asarray(zero, part.dtype), part.shape),
        value,
        identity,
    )

    def turn(k, before):
        at = count - 1 - k if reverse else k
        reached = at > place if reverse else at < place
        new = combine(
            before, jax.tree.map(lambda part, own: part[at].astype(own.dtype), everything, value)
        )
        return jax.tree.map(lambda a, b: jnp.where(reached, a, b), new, before)

    return lax.fori_loop(0, count, turn, start)


def block_mask(cumul, update):
    span_len = cumul.shape[1]
    causal = jnp.arange(span_len)[:, None] >= jnp.arange(span_len)[None, :]
    spread = jnp.where(causal[None], cumul[:, :, None] - cumul[:, None, :], -jnp.inf)
    return jnp.exp(spread) * update[:, None, :]


def pair_weights(query_matrix, key_matrix, value_matrix, gradient_rows, cumul, update_rows):
    decay_mask = block_mask(cumul, update_rows)
    scores = jnp.einsum(
        "thk,shk->hts", query_matrix, key_matrix, preferred_element_type=jnp.float32
    )
    reversed_blocks = jnp.einsum(
        "thv,shv->hts", gradient_rows, value_matrix, preferred_element_type=jnp.float32
    )
    return (
        (scores * decay_mask).astype(jnp.bfloat16),
        (reversed_blocks * decay_mask).astype(jnp.bfloat16),
    )


def layer_output(query_matrix, value_matrix, projection_weight, cumul, state_start):
    within = jnp.einsum(
        "hts,shv->thv", projection_weight, value_matrix, preferred_element_type=jnp.float32
    )
    carried_state = jnp.einsum(
        "qml,mla->qma",
        query_matrix,
        state_start.astype(jnp.bfloat16),
        preferred_element_type=jnp.float32,
    )
    return (within + jnp.exp(cumul).T[:, :, None] * carried_state).astype(jnp.bfloat16)


def input_grads(
    query_matrix,
    key_matrix,
    value_matrix,
    gradient_rows,
    projection_weight,
    reversed_blocks,
    cumul,
    update_rows,
    state_start,
    finish,
):
    state_reduced = state_start.astype(jnp.bfloat16)
    carry_reduced = finish.astype(jnp.bfloat16)
    incoming_gradient = jnp.exp(cumul).T[:, :, None]
    outgoing_gradient = (update_rows * jnp.exp(cumul[:, -1][:, None] - cumul)).T[:, :, None]
    query_gradient = jnp.einsum(
        "gea,agq->egq", reversed_blocks, key_matrix, preferred_element_type=jnp.float32
    ) + incoming_gradient * jnp.einsum(
        "sba,bda->sbd", gradient_rows, state_reduced, preferred_element_type=jnp.float32
    )
    key_gradient = jnp.einsum(
        "rwy,wre->yre", reversed_blocks, query_matrix, preferred_element_type=jnp.float32
    ) + outgoing_gradient * jnp.einsum(
        "wqx,qgx->wqg", value_matrix, carry_reduced, preferred_element_type=jnp.float32
    )
    value_gradient = jnp.einsum(
        "kyp,ykb->pkb", projection_weight, gradient_rows, preferred_element_type=jnp.float32
    ) + outgoing_gradient * jnp.einsum(
        "imx,mxd->imd", key_matrix, carry_reduced, preferred_element_type=jnp.float32
    )
    return (
        query_gradient.astype(jnp.bfloat16),
        key_gradient.astype(jnp.bfloat16),
        value_gradient.astype(jnp.bfloat16),
    )


def combine_carry(earlier, later):
    return (earlier[0] * later[0], later[0][:, None, None] * earlier[1] + later[1])


def per_device(query_vectors, key_vectors, value_vectors, grad_out, out_weight, periods, log_decay):
    tok_rows = query_vectors.shape[0]
    head_count = periods.shape[0]
    block_count = tok_rows // BLK
    full_grad = lax.all_gather(grad_out, "head", axis=1, tiled=True)
    columns = full_grad
    grad_mixed = jnp.dot(
        columns,
        lax.all_gather(out_weight, "tm", axis=0, tiled=True),
        preferred_element_type=jnp.float32,
    ).astype(jnp.bfloat16)
    offset = lax.axis_index("tm") * tok_rows
    positions = offset + jnp.arange(tok_rows, dtype=jnp.int32)
    update = (positions[None, :] % periods[:, None] == 0).astype(jnp.float32)
    step_log = update * periods[:, None].astype(jnp.float32) * log_decay
    cumulative = jnp.cumsum(step_log.reshape(head_count, block_count, BLK), axis=2).transpose(
        1, 0, 2
    )
    updates = update.reshape(head_count, block_count, BLK).transpose(1, 0, 2)

    def blocked(tensor):
        return tensor.reshape(block_count, BLK, head_count, DK)

    query_blocks = blocked(query_vectors)
    key_blocks = blocked(key_vectors)
    value_blocks = blocked(value_vectors)
    grad_blocks = blocked(grad_mixed)
    zero_state = jnp.zeros((head_count, DK, DK), jnp.float32)

    def forward(running, section):
        key_matrix, value_matrix, cumul, update_rows = section
        block_total = cumul[:, -1]
        factor = update_rows * jnp.exp(block_total[:, None] - cumul)
        decay_scaled = (key_matrix.astype(jnp.float32) * factor.T[:, :, None]).astype(jnp.bfloat16)
        outer_product = jnp.einsum(
            "ptz,ptb->tzb", decay_scaled, value_matrix, preferred_element_type=jnp.float32
        )
        return (jnp.exp(block_total)[:, None, None] * running + outer_product, running)

    state_local, state_starts = lax.scan(
        forward, zero_state, (key_blocks, value_blocks, cumulative, updates)
    )

    def backward(carried_in, section):
        query_matrix, gradient_rows, cumul = section
        decay_scaled = (query_matrix.astype(jnp.float32) * jnp.exp(cumul).T[:, :, None]).astype(
            jnp.bfloat16
        )
        outer_product = jnp.einsum(
            "yop,yoj->opj", decay_scaled, gradient_rows, preferred_element_type=jnp.float32
        )
        return (jnp.exp(cumul[:, -1])[:, None, None] * carried_in + outer_product, carried_in)

    grad_local, grad_ends = lax.scan(
        backward, zero_state, (query_blocks, grad_blocks, cumulative), reverse=True
    )
    totals = cumulative[:, :, -1]
    shrink = jnp.exp(jnp.sum(totals, axis=0))
    identity = (jnp.ones((head_count,), jnp.float32), zero_state)
    _, state_in = prefix((shrink, state_local), "tm", combine_carry, identity, False)
    _, grad_in = prefix((shrink, grad_local), "tm", combine_carry, identity, True)
    running_sum = jnp.cumsum(totals, axis=0)
    before = running_sum - totals
    later_sum = jnp.sum(totals, axis=0)[None] - running_sum
    starts = jnp.exp(before)[:, :, None, None] * state_in[None] + state_starts
    finishes = jnp.exp(later_sum)[:, :, None, None] * grad_in[None] + grad_ends
    sections = (
        query_blocks,
        key_blocks,
        value_blocks,
        grad_blocks,
        cumulative,
        updates,
        starts,
        finishes,
    )

    def every_output(section):
        (
            query_matrix,
            key_matrix,
            value_matrix,
            gradient_rows,
            cumul,
            update_rows,
            state_start,
            finish,
        ) = section
        projection_weight, reversed_blocks = pair_weights(
            query_matrix, key_matrix, value_matrix, gradient_rows, cumul, update_rows
        )
        mixed_block = layer_output(
            query_matrix, value_matrix, projection_weight, cumul, state_start
        )
        return (mixed_block,) + input_grads(
            query_matrix,
            key_matrix,
            value_matrix,
            gradient_rows,
            projection_weight,
            reversed_blocks,
            cumul,
            update_rows,
            state_start,
            finish,
        )

    mixed, query_gradient, key_gradient, value_gradient = lax.map(every_output, sections)
    mixed_rows = mixed.reshape(tok_rows, head_count * DK)
    columns = full_grad
    grad_weight = lax.psum_scatter(
        lax.dot_general(
            columns, mixed_rows, (((0,), (0,)), ((), ())), preferred_element_type=jnp.float32
        ).astype(jnp.bfloat16),
        "tm",
        scatter_dimension=0,
        tiled=True,
    ).astype(jnp.float32)
    return (
        query_gradient.reshape(tok_rows, head_count * DK),
        key_gradient.reshape(tok_rows, head_count * DK),
        value_gradient.reshape(tok_rows, head_count * DK),
        grad_weight,
    )


def solution(mesh):
    return jax.shard_map(
        per_device,
        mesh=mesh,
        in_specs=(
            P("tm", "head"),
            P("tm", "head"),
            P("tm", "head"),
            P("tm", "head"),
            P("tm", "head"),
            P("head"),
            P("head", "tm"),
        ),
        out_specs=(P("tm", "head"), P("tm", "head"), P("tm", "head"), P("tm", "head")),
        check_vma=False,
    )
```

profile of v0, /device:TPU:16, one launch (start us, length us, event | category | flops | bytes accessed | tf_op | source)
XLA Modules:
  0.0 471.5 jit_solution(9501568357952887732)
XLA Ops:
  16.8 5.1 %fusion.56 = f32[2,8,512]{1,2,0:T(8,128)S(1)} fusion(s32[8]{0:T(128)S(1)} %get-tuple-element.753, s32[2,512]{1,0:T(2,128)S(1)} %add_add_fusion, pred[8]{0:T(512)(128)(4,1)S(1)} %broadcast_compare_fusion), kind=kLoop, calls=%fused_computation.107 | loop fusion | flops 73728 | bytes 36904 | tf_op jit(solution)/shard_map/convert_element_type | solution.py:123
  23.1 15.9 %while.77 = (s32[]{:T(128)}, f32[8,128,128]{2,1,0:T(8,128)}, f32[2,8,128,128]{3,2,1,0:T(8,128)}, f32[2,8,512]{1,2,0:T(8,128)}, bf16[2,512,8,128]{3,2,1,0:T(8,128...) while((s32[]{:T(128)}, f32[8,128,128]{2,1,0:T(8,128)}, ...), condition=%wide.region_5.6_spmd.clone, body=%wide.region_4.5_spmd.clone.sunk | while | flops 136323072 | bytes 10879352 | solution.py:149
  41.2 3.5 copy.167
  44.8 113.8 %all-gather.8.cloned.1.call-done = bf16[1024,4096]{1,0:T(8,128)(2,1)} async-done(((bf16[1024,1024]{1,0:T(8,128)(2,1)}), bf16[1024,4096]{1,0:T(8,128)(2,1)}) %all-gather.8.cloned.1.call-update) | async-done | bytes 8388624 | tf_op jit(solution)/shard_map/all_gather | solution.py:114
  158.6 56.3 %all-gather.10.cloned.1.call-done = bf16[4096,1024]{1,0:T(8,128)(2,1)} async-done(((bf16[512,1024]{1,0:T(8,128)(2,1)}), bf16[4096,1024]{1,0:T(8,128)(2,1)}) %all-gather.10.cloned.1.call-update) | async-done | bytes 8388624 | tf_op jit(solution)/shard_map/all_gather | solution.py:118
  214.8 13.7 %convert_bitcast_fusion.1 = bf16[128,8,8,128]{3,1,2,0:T(8,128)(2,1)S(1)} fusion(bf16[1024,4096]{1,0:T(8,128)(2,1)} %all-gather.8.cloned.1.call-done, bf16[4096,1024]{1,0:T(8,128)(2,1)} %all-gather.10.cloned.1.call-done), kind=kOutput, calls=%fused_computation.99 | convolution fusion | flops 8590983168 | bytes 18874368 | tf_op jit(solution)/shard_map/dot_general | solution.py:116
  230.6 16.4 %while.79 = (s32[]{:T(128)}, f32[8,128,128]{2,1,0:T(8,128)}, f32[2,8,128,128]{3,2,1,0:T(8,128)}, f32[2,8,512]{1,2,0:T(8,128)}, bf16[2,512,8,128]{3,2,1,0:T(8,128...) while((s32[]{:T(128)}, f32[8,128,128]{2,1,0:T(8,128)}, ...), condition=%wide.region_9.10_spmd.clone, body=%wide.region_8.9_spmd.clone.sunk | while | flops 136314880 | bytes 8487620 | solution.py:163
  250.8 13.1 %all-reduce = bf16[64]{0:T(256)(128)(2,1)S(1)} all-reduce(bf16[64]{0:T(256)(128)(2,1)S(1)} %dynamic-update-slice), channel_id=2, replica_groups=mesh['tm'=8,'head'=4] {'tm'}, use_global_device_ids=true, to_apply=%add | all-reduce | flops 64 | bytes 256
  264.1 9.2 %while.78 = (s32[]{:T(128)}, f32[8,128,128]{2,1,0:T(8,128)S(1)}, s32[]{:T(128)}, bf16[8,8]{1,0:T(8,128)(2,1)S(1)}, bf16[8,8,128,128]{3,2,1,0:T(8,128)(2,1)}, /*index=5*/s32[]{:T(128)}, s32[]{:T(128)}) while((s32[]{:T(128)}, f32[8,128,128]{2,1,0:T(8,128)S(1)}, s32[]{:T(128)}, bf16[8,8]{1,0:T(8,128)(2,1)S(1)}, ...), condition=%wide.region_7.8_spmd.clone, body=%wide.region_6.7_spmd.clone.sunk | while | flops 655372 | bytes 1310913 | solution.py:31
  273.2 3.7 all-gather.14.cloned.1.call-done
  277.0 9.1 %while.80 = (s32[]{:T(128)}, f32[8,128,128]{2,1,0:T(8,128)S(1)}, s32[]{:T(128)}, bf16[8,8]{1,0:T(8,128)(2,1)S(1)}, bf16[8,8,128,128]{3,2,1,0:T(8,128)(2,1)}, /*index=5*/s32[]{:T(128)}, s32[]{:T(128)}, s32[]{:T(128)}, s32[]{:T(128)}) while((s32[]{:T(128)}, f32[8,128,128]{2,1,0:T(8,128)S(1)}, s32[]{:T(128)}, ...), condition=%wide.region_11.12_spmd.clone, body=%wide.region_10.11_spmd.clone.sunk | while | flops 655376 | bytes 1310975 | solution.py:31
  286.1 2.8 multiply_add_fusion
  288.9 87.9 %while.76 = (s32[]{:T(128)}, bf16[2,512,8,128]{3,2,1,0:T(8,128)(2,1)}, bf16[2,512,8,128]{3,2,1,0:T(8,128)(2,1)}, bf16[2,512,8,128]{3,2,1,0:T(8,128)(2,1)}, bf16[...) while((s32[]{:T(128)}, ...), condition=%wide.region_13.14_spmd, body=%wide.region_12.13_spmd.sunk | while | flops 3785629696 | bytes 145883712 | solution.py:217
  298.9 3.6 multiply_convert_fusion.4
  304.8 2.8 fusion.114
  314.0 3.6 multiply_convert_fusion.5
  327.6 2.8 constant_dynamic-update-slice_fusion.6
  342.8 3.6 multiply_convert_fusion.4
  348.8 2.8 fusion.114
  357.9 3.6 multiply_convert_fusion.5
  371.5 2.8 constant_dynamic-update-slice_fusion.6
  376.8 14.1 %convert_bitcast_fusion = bf16[4096,1024]{0,1:T(8,128)(2,1)} fusion(bf16[1024,4096]{1,0:T(8,128)(2,1)} %all-gather.8.cloned.1.call-done, bf16[128,8,8,128]{3,2,1,0:T(8,128)(2,1)} %bitcast.333), kind=kOutput, calls=%fused_computation.93 | convolution fusion | flops 8594128896 | bytes 18874368 | tf_op jit(solution)/shard_map/dot_general | solution.py:221
  398.4 64.0 %reduce-scatter.2.cloned.1.call-done = bf16[512,1024]{0,1:T(8,128)(2,1)} async-done(((bf16[4096,1024]{0,1:T(8,128)(2,1)}), bf16[512,1024]{0,1:T(8,128)(2,1)}) %reduce-scatter.2.cloned.1.call-update) | async-done | bytes 1048592 | tf_op jit(solution)/shard_map/reduce_scatter | solution.py:220
  462.4 2.6 copy.142
  (234 shorter events, 137.4 us)
Async XLA Ops:
  7.2 5.7 %copy-start.11 = (bf16[1024,1024]{1,0:T(8,128)(2,1)S(1)}, bf16[1024,1024]{1,0:T(8,128)(2,1)}, u32[]{:S(2)}) copy-start(bf16[1024,1024]{1,0:T(8,128)(2,1)} %param.18) | copy-start | bytes 6291460
  7.2 151.4 %all-gather.8.cloned.1.call-start = ((), (), s32[]{:S(2)}) async-start(), calls=%async_computation.1 | async-start | bytes 10485760 | tf_op jit(solution)/shard_map/all_gather | solution.py:114
  7.9 206.9 %all-gather.10.cloned.1.call-start = ((), (), s32[]{:S(2)}) async-start(), calls=%async_computation.2 | async-start | bytes 9437184 | tf_op jit(solution)/shard_map/all_gather | solution.py:118
  8.7 255.4 %all-gather.12.cloned.1.call-start = ((), (), s32[]{:S(2)}) async-start(), calls=%async_computation.4 | async-start | bytes 2359296 | tf_op jit(solution)/shard_map/all_gather | solution.py:13
  23.1 2.3 copy-start.6
  36.6 2.4 copy-start.7
  39.0 5.8 %copy-start.8 = (f32[2,8,512]{1,2,0:T(8,128)}, f32[2,8,512]{1,2,0:T(8,128)S(1)}, u32[]{:S(2)}) copy-start(f32[2,8,512]{1,2,0:T(8,128)S(1)} %get-tuple-element.1152) | copy-start | bytes 98308
  41.0 236.0 %all-gather.14.cloned.1.call-start = ((), (), s32[]{:S(2)}) async-start(), calls=%async_computation.5 | async-start | bytes 2359296 | tf_op jit(solution)/shard_map/all_gather | solution.py:13
  230.6 18.3 %copy-start.20 = (u32[32]{0:T(128)S(1)}, u32[32]{0:T(128)}, u32[]{:S(2)}) copy-start(u32[32]{0:T(128)} %constant.169) | copy-start | bytes 388
  248.9 213.5 %reduce-scatter.2.cloned.1.call-start = ((), (), s32[]{:S(2)}) async-start(), calls=%async_computation.3 | async-start | bytes 9437184 | tf_op jit(solution)/shard_map/reduce_scatter | solution.py:220
  288.9 4.4 copy-start
  293.4 2.8 copy-start.5
  304.8 2.8 copy-start.9
  324.2 3.3 copy-start.3
  327.6 2.8 copy-start.2
  327.6 2.8 copy-start.13
  330.4 2.5 copy-start.1
  332.9 4.4 copy-start
  337.4 2.8 copy-start.5
  348.8 2.8 copy-start.9
  368.1 3.3 copy-start.3
  371.5 2.8 copy-start.2
  371.5 2.8 copy-start.13
  374.3 2.5 copy-start.1
  (14 other events, 24.8 us)
Sparse Core Ops, SparseCore 0:
  9.6 148.9 all-gather.7
  160.5 54.3 all-gather.9
  216.7 27.8 all-gather.11
  249.0 27.9 all-gather.13
  391.0 71.2 reduce-scatter.1
where the time goes:
time: 475 us; the launch traced here: 471 us
  waiting for transfers between devices  239 us (50%)
  local copies, waits for them, and re-layouts  83.3 us (18%)
  matrix products  75.7 us (16%)
  other arithmetic  44.1 us (9%)
  between operations  14.7 us (3%)
  blocking collectives  13.1 us (3%)
    all_gather x1, waiting for transfers between devices, per_device(): full_grad = lax.all_gather(grad_out, 'head', axis=1, tiled=True)  114 us
    reduce_scatter x1, waiting for transfers between devices, per_device(): lax.psum_scatter(lax.dot_general(columns, mixed_rows, (((0,), (0,)), ((),...  64 us
    all_gather x1, waiting for transfers between devices, per_device(): lax.all_gather(out_weight, 'tm', axis=0, tiled=True)  56.3 us
    dynamic_update_slice x12, local copies, waits for them, and re-layouts, per_device(): lax.map(every_output, sections)  24.4 us
    dynamic_slice x16, local copies, waits for them, and re-layouts, per_device(): lax.scan(forward, zero_state, (key_blocks, value_blocks, cumulative, upda...  23.5 us
    unnamed x29, local copies, waits for them, and re-layouts  19 us
    select_n x16, other arithmetic, turn(): return jax.tree.map(lambda a, b: jnp.where(reached, a, b), new, before)  17.6 us
    dot_general x1, matrix products, per_device(): lax.dot_general(columns, mixed_rows, (((0,), (0,)), ((), ())), preferred_...  14.1 us
  transfers between devices with their start and end apart: 5, of which 4 were waited for; matrix products, arithmetic and copies ran while one was open for 18% of the time, Pallas kernels for 0%

commit v1 on v0

v1 whole, which is shorter than its diff:
```python
import functools
import math

import jax
import jax.numpy as jnp
from jax import lax
from jax.experimental import pallas as pl
from jax.experimental.pallas import tpu as pltpu
from jax.sharding import PartitionSpec as P

DK = 128
BLK = 512
CHUNKS = 2
LOG2E = math.log2(math.e)
FAR = 1e30
F32 = jnp.float32
BF16 = jnp.bfloat16
PARAMS = pltpu.CompilerParams(vmem_limit_bytes=48 * 1024 * 1024)


def dot(a, b, da=1, db=0):
    return lax.dot_general(a, b, (((da,), (db,)), ((), ())), preferred_element_type=F32)


def cost(flops, moved):
    return pl.CostEstimate(flops=flops, bytes_accessed=moved, transcendentals=0)


def state_kernel(col, k, v, parts, local):
    state = jnp.zeros((DK, DK), F32)
    for b in range(parts.shape[1]):
        rows = pl.ds(b * BLK, BLK)
        scaled = (k[rows, :].astype(F32) * col[0, rows, 1:2]).astype(BF16)
        part = dot(scaled, v[rows, :], 0, 0)
        parts[0, b] = part
        state = state * col[0, pl.ds(b * BLK + BLK - 1, 1), 2:3] + part
    local[0] = state


def tiles(half):
    return ((0, 0), (1, 0), (1, 1))


def mask_tile(col, row, t, s, half, diagonal):
    spread = jnp.exp2(col[0, pl.ds(t, half), 0:1] - row[0, 0:1, pl.ds(s, half)])
    if diagonal:
        shape = (half, half)
        causal = lax.broadcasted_iota(jnp.int32, shape, 0) >= lax.broadcasted_iota(
            jnp.int32, shape, 1
        )
        spread = jnp.where(causal, spread, 0.0)
    return spread


def within_kernel(col, row, q, k, v, weights, within):
    half = BLK // 2
    for b in range(weights.shape[1]):
        sums = [None, None]
        for n, (i, j) in enumerate(tiles(half)):
            t, s = b * BLK + i * half, b * BLK + j * half
            scores = dot(q[pl.ds(t, half), :], k[pl.ds(s, half), :], 1, 1)
            tile = (scores * mask_tile(col, row, t, s, half, i == j)).astype(BF16)
            weights[0, b, n] = tile
            part = dot(tile, v[pl.ds(s, half), :])
            sums[i] = part if sums[i] is None else sums[i] + part
        for i in range(2):
            within[pl.ds(b * BLK + i * half, half), :] = sums[i]


def mixed_kernel(col, q, within, parts, start, mixed, states):
    state = start[0]
    for b in range(parts.shape[1]):
        rows = pl.ds(b * BLK, BLK)
        small = state.astype(BF16)
        states[0, b] = small
        carried = dot(q[rows, :], small)
        mixed[rows, :] = (within[rows, :] + col[0, rows, 2:3] * carried).astype(BF16)
        state = state * col[0, pl.ds(b * BLK + BLK - 1, 1), 2:3] + parts[0, b]


def grad_kernel(col, q, early, last, weight, e, parts, local):
    rows_all = early[...] + dot(last[...], weight[...])
    e[...] = rows_all.astype(BF16)
    for h in range(parts.shape[0]):
        lanes = pl.ds(h * DK, DK)
        state = jnp.zeros((DK, DK), F32)
        for b in reversed(range(parts.shape[1])):
            rows = pl.ds(b * BLK, BLK)
            scaled = (q[rows, lanes].astype(F32) * col[h, rows, 2:3]).astype(BF16)
            part = dot(scaled, e[rows, lanes], 0, 0)
            parts[h, b] = part
            state = state * col[h, pl.ds(b * BLK + BLK - 1, 1), 2:3] + part
        local[h] = state


def back_kernel(col, row, q, k, v, e, weights, states, dq, dk, dv):
    half = BLK // 2
    for b in range(weights.shape[1]):
        sums = [[None, None] for _ in range(3)]

        def add(which, at, part):
            old = sums[which][at]
            sums[which][at] = part if old is None else old + part

        for n, (i, j) in enumerate(tiles(half)):
            t, s = b * BLK + i * half, b * BLK + j * half
            at_t, at_s = pl.ds(t, half), pl.ds(s, half)
            raw = dot(e[at_t, :], v[at_s, :], 1, 1)
            tile = (raw * mask_tile(col, row, t, s, half, i == j)).astype(BF16)
            add(0, i, dot(tile, k[at_s, :]))
            add(1, j, dot(tile, q[at_t, :], 0, 0))
            add(2, j, dot(weights[0, b, n], e[at_t, :], 0, 0))
        for i in range(2):
            rows = pl.ds(b * BLK + i * half, half)
            carried = dot(e[rows, :], states[0, b], 1, 1)
            dq[rows, :] = (sums[0][i] + col[0, rows, 2:3] * carried).astype(BF16)
            dk[rows, :] = sums[1][i].astype(BF16)
            dv[rows, :] = sums[2][i].astype(BF16)


def finish_kernel(col, k, v, dk_part, dv_part, parts, finish, dk, dv):
    state = finish[0]
    for b in reversed(range(parts.shape[1])):
        rows = pl.ds(b * BLK, BLK)
        small = state.astype(BF16)
        factor = col[0, rows, 1:2]
        dk[rows, :] = (dk_part[rows, :].astype(F32) + factor * dot(v[rows, :], small, 1, 1)).astype(
            BF16
        )
        dv[rows, :] = (dv_part[rows, :].astype(F32) + factor * dot(k[rows, :], small)).astype(BF16)
        state = state * col[0, pl.ds(b * BLK + BLK - 1, 1), 2:3] + parts[0, b]


def log2_of(count):
    bits = count.bit_length() - 1
    assert 1 << bits == count
    return bits


def scan_states(total, decay, reverse, decays):
    count, place = lax.axis_size("tm"), lax.axis_index("tm")
    heads = total.shape[0]
    reached, across, own = jnp.zeros_like(total), jnp.ones_like(decay), decay
    seen = []
    for bit in range(log2_of(count)):
        perm = [(i, i ^ (1 << bit)) for i in range(count)]
        sent = total.astype(BF16)
        if decays is None:
            high = own.astype(BF16)
            low = (own - high.astype(F32)).astype(BF16)
            pair = jnp.concatenate(
                [jnp.broadcast_to(x[:, None, None], (heads, 8, DK)) for x in (high, low)], axis=1
            )
            got = lax.ppermute(jnp.concatenate([sent, pair], axis=1), "tm", perm)
            other = got[:, DK, 0].astype(F32) + got[:, DK + 8, 0].astype(F32)
            got = got[:, :DK].astype(F32)
        else:
            got = lax.ppermute(sent, "tm", perm).astype(F32)
            other = decays[bit]
        seen.append(other)
        upper = (place >> bit) & 1
        takes = (upper == 1) != reverse
        reached = jnp.where(takes, reached + across[:, None, None] * got, reached)
        across = jnp.where(takes, across * other, across)
        total = jnp.where(
            takes, total + own[:, None, None] * got, got + other[:, None, None] * total
        )
        own = own * other
    return reached, seen


def block_order(size):
    return [sorted(range(size), key=lambda q: (abs(p - q), p ^ q)) for p in range(size)]


def line_gather(pieces):
    size = lax.axis_size("head")
    have = {}
    left, right = list(pieces), list(pieces)
    for step in range(1, size):
        to_left = [(p, p - 1) for p in range(1, size) if p + step - 1 < size]
        to_right = [(p, p + 1) for p in range(size - 1) if p - step + 1 >= 0]
        for c in range(len(pieces)):
            left[c] = lax.ppermute(left[c], "head", to_left)
            right[c] = lax.ppermute(right[c], "head", to_right)
            have[(step, c)] = left[c]
            have[(-step, c)] = right[c]
    for c, piece in enumerate(pieces):
        have[(0, c)] = piece
    return have


def pick(by_plane, make):
    plane = lax.axis_index("head")
    keys = sorted(set(by_plane))
    out = make(keys[0])
    for key in keys[1:]:
        here = functools.reduce(
            jnp.logical_or, [plane == p for p, own in enumerate(by_plane) if own == key]
        )
        out = jnp.where(here, make(key), out)
    return out


def reduce_block(part, targets, flips):
    count, size = lax.axis_size("tm"), lax.axis_size("head")
    group = part.shape[0]
    place = lax.axis_index("tm")
    held = part
    width = group
    while width > 1:
        width //= 2
        perm = [(i, i ^ width) for i in range(count)]
        upper = (place // width) % 2 == 1
        first, second = held[:width], held[width:]
        got = lax.ppermute(jnp.where(upper, first, second), "tm", perm)
        held = (jnp.where(upper, second, first).astype(F32) + got.astype(F32)).astype(BF16)
    held = held[0]
    out = []
    span = held.shape[1] // len(flips)
    for n, order in enumerate(flips):
        now = held[:, n * span : (n + 1) * span]
        done = 0
        for bit in order:
            perm = []
            for i in range(count):
                for p in range(size):
                    far = (i // group) ^ targets[p]
                    if far & bit and not far & done:
                        perm.append((i * size + p, (i ^ (bit * group)) * size + p))
            got = lax.ppermute(now.astype(BF16), ("tm", "head"), perm)
            now = now.astype(F32) + got.astype(F32)
            done |= bit
        out.append(now)
    return jnp.concatenate(out, axis=1) if len(out) > 1 else out[0]


def per_device(query, key, value, grad_out, out_weight, periods, log_decay):
    tok, width = query.shape
    heads = periods.shape[0]
    blocks = tok // BLK
    count, size = lax.axis_size("tm"), lax.axis_size("head")
    group = count // size
    plane = lax.axis_index("head")
    place = lax.axis_index("tm")
    sub = grad_out.shape[1] // group
    piece = sub // CHUNKS

    split = grad_out.reshape(tok, group, CHUNKS, piece)
    pieces = [split[:, :, c].reshape(tok, group * piece) for c in range(CHUNKS)]
    have = line_gather(pieces)
    full_weight = lax.all_gather(out_weight, "tm", axis=0, tiled=True)

    positions = place * tok + jnp.arange(tok, dtype=jnp.int32)
    update = positions[None, :] % periods[:, None] == 0
    step_log = jnp.where(update, periods[:, None].astype(F32) * log_decay, 0.0)
    cumul = jnp.cumsum(step_log.reshape(heads, blocks, BLK), axis=2)
    totals = cumul[:, :, -1]
    key_factor = jnp.where(
        update.reshape(heads, blocks, BLK), jnp.exp(totals[:, :, None] - cumul), 0.0
    ).reshape(heads, tok)
    cumul = cumul.reshape(heads, tok)
    scaled_log = cumul * LOG2E
    col = jnp.stack([scaled_log, key_factor, jnp.exp(cumul)], axis=2)
    row = jnp.where(update, scaled_log, FAR)[:, None, :]
    decay = jnp.exp(jnp.sum(totals, axis=1))

    half = BLK // 2
    head_rows = pl.BlockSpec((tok, DK), lambda h: (0, h))
    cols = pl.BlockSpec((1, tok, 3), lambda h: (h, 0, 0))
    rows = pl.BlockSpec((1, 1, tok), lambda h: (h, 0, 0))
    block_states = pl.BlockSpec((1, blocks, DK, DK), lambda h: (h, 0, 0, 0))
    one_state = pl.BlockSpec((1, DK, DK), lambda h: (h, 0, 0))
    tiles_spec = pl.BlockSpec((1, blocks, 3, half, half), lambda h: (h, 0, 0, 0, 0))
    shape = jax.ShapeDtypeStruct
    states_f32 = shape((heads, blocks, DK, DK), F32)
    states_bf16 = shape((heads, blocks, DK, DK), BF16)
    state_f32 = shape((heads, DK, DK), F32)
    rows_bf16 = shape((tok, width), BF16)
    pair_flops = 2 * tok * BLK * width

    fwd_parts, fwd_local = pl.pallas_call(
        state_kernel,
        grid=(heads,),
        in_specs=[cols, head_rows, head_rows],
        out_specs=[block_states, one_state],
        out_shape=[states_f32, state_f32],
        compiler_params=PARAMS,
        cost_estimate=cost(2 * tok * DK * width, 12 * tok * width),
        name="block_states",
    )(col, key, value)
    state_in, decays = scan_states(fwd_local, decay, False, None)
    weights, within = pl.pallas_call(
        within_kernel,
        grid=(heads,),
        in_specs=[cols, rows, head_rows, head_rows, head_rows],
        out_specs=[tiles_spec, head_rows],
        out_shape=[shape((heads, blocks, 3, half, half), BF16), shape((tok, width), F32)],
        compiler_params=PARAMS,
        cost_estimate=cost(3 * pair_flops, 20 * tok * width),
        name="pair_weights",
    )(col, row, query, key, value)
    mixed, states = pl.pallas_call(
        mixed_kernel,
        grid=(heads,),
        in_specs=[cols, head_rows, head_rows, block_states, one_state],
        out_specs=[head_rows, block_states],
        out_shape=[rows_bf16, states_bf16],
        compiler_params=PARAMS,
        cost_estimate=cost(2 * tok * DK * width, 12 * tok * width),
        name="mixed_rows",
    )(col, query, within, fwd_parts, state_in)

    order = block_order(size)
    weight_parts = full_weight.reshape(size, group, CHUNKS, piece, width)
    early = None
    sums = []
    bits = [1 << b for b in range(log2_of(size))]
    for s in range(size):
        targets = [order[p][s] for p in range(size)]
        at = pick(targets, lambda q: jnp.int32(q))
        final = s == size - 1
        for c in range(CHUNKS):
            block = pick([q - p for p, q in enumerate(targets)], lambda k: have[(k, c)])
            weight = lax.dynamic_slice(
                weight_parts, (at, 0, c, 0, 0), (1, group, 1, piece, width)
            ).reshape(group * piece, width)
            if final and c == CHUNKS - 1:
                last, last_weight = block, weight
            else:
                part = jnp.dot(block, weight, preferred_element_type=F32)
                early = part if early is None else early + part
            product = dot(block, mixed, 0, 0).astype(BF16).reshape(group, piece, width)
            flips = [bits[::-1], bits] if final else [bits[::-1] if s % 2 else bits]
            done = reduce_block(product, targets, flips)
            mine = pick(targets, lambda q: jnp.int32(q)) == place // group
            sums.append((c, mine, done))
    grad_weight = []
    for c in range(CHUNKS):
        out = None
        for chunk, mine, done in sums:
            if chunk == c:
                out = done.astype(F32) if out is None else jnp.where(mine, done.astype(F32), out)
        grad_weight.append(out)
    grad_weight = jnp.concatenate(grad_weight, axis=0)

    two = 2 if heads % 2 == 0 else 1
    wide = pl.BlockSpec((tok, two * DK), lambda h: (0, h))
    e, back_parts, back_local = pl.pallas_call(
        grad_kernel,
        grid=(heads // two,),
        in_specs=[
            pl.BlockSpec((two, tok, 3), lambda h: (h, 0, 0)),
            wide,
            wide,
            pl.BlockSpec(last.shape, lambda h: (0, 0)),
            pl.BlockSpec((last.shape[1], two * DK), lambda h: (0, h)),
        ],
        out_specs=[
            wide,
            pl.BlockSpec((two, blocks, DK, DK), lambda h: (h, 0, 0, 0)),
            pl.BlockSpec((two, DK, DK), lambda h: (h, 0, 0)),
        ],
        out_shape=[rows_bf16, states_f32, state_f32],
        compiler_params=PARAMS,
        cost_estimate=cost(2 * tok * last.shape[1] * width, 16 * tok * width),
        name="grad_mixed_rows",
    )(col, query, early, last, last_weight)
    grad_in, _ = scan_states(back_local, decay, True, decays)
    dq, dk_part, dv_part = pl.pallas_call(
        back_kernel,
        grid=(heads,),
        in_specs=[cols, rows] + [head_rows] * 4 + [tiles_spec, block_states],
        out_specs=[head_rows] * 3,
        out_shape=[rows_bf16] * 3,
        compiler_params=PARAMS,
        cost_estimate=cost(5 * pair_flops, 24 * tok * width),
        name="block_gradients",
    )(col, row, query, key, value, e, weights, states)
    dk, dv = pl.pallas_call(
        finish_kernel,
        grid=(heads,),
        in_specs=[cols] + [head_rows] * 4 + [block_states, one_state],
        out_specs=[head_rows] * 2,
        out_shape=[rows_bf16] * 2,
        compiler_params=PARAMS,
        cost_estimate=cost(4 * tok * DK * width, 16 * tok * width),
        name="carried_gradients",
    )(col, key, value, dk_part, dv_part, back_parts, grad_in)
    return dq, dk, dv, grad_weight


def solution(mesh):
    both = P("tm", "head")
    return jax.shard_map(
        per_device,
        mesh=mesh,
        in_specs=(both, both, both, both, both, P("head"), P("head", "tm")),
        out_specs=(both, both, both, both),
        check_vma=False,
    )
```

time: 475 us -> 426 us (0.90)
  the two profiles are of different devices: /device:TPU:16 before, /device:TPU:10 now
where the time goes in v1:
time: 426 us; the launch traced here: 418 us
  waiting for transfers between devices  121 us (28%)
  starting transfers between devices  109 us (26%)
  Pallas kernels  58.3 us (14%)
  other arithmetic  43.9 us (10%)
  matrix products  36.2 us (8%)
  local copies, waits for them, and re-layouts  34.5 us (8%)
  between operations  15.3 us (4%)
    ppermute x6, waiting for transfers between devices, line_gather(): left[c] = lax.ppermute(left[c], 'head', to_left)  76.9 us
    ppermute x20, starting transfers between devices, reduce_block(): got = lax.ppermute(now.astype(BF16), ('tm', 'head'), perm)  45.8 us
    ppermute x20, waiting for transfers between devices, reduce_block(): got = lax.ppermute(now.astype(BF16), ('tm', 'head'), perm)  36.1 us
    dot_general x7, matrix products, per_device(): part = jnp.dot(block, weight, preferred_element_type=F32)  23.8 us
    ppermute x6, starting transfers between devices, line_gather(): right[c] = lax.ppermute(right[c], 'head', to_right)  20.2 us
    ppermute x6, starting transfers between devices, line_gather(): left[c] = lax.ppermute(left[c], 'head', to_left)  18.2 us
    pallas_call x1, Pallas kernels, per_device(): pl.pallas_call(back_kernel, grid=(heads,), in_specs=[cols, rows] + [head_...  17.4 us
    ppermute x3, starting transfers between devices, scan_states(): got = lax.ppermute(sent, 'tm', perm).astype(F32)  16.1 us
  transfers between devices with their start and end apart: 47, of which 16 were waited for; matrix products, arithmetic and copies ran while one was open for 20% of the time, Pallas kernels for 12%

profile of v1, /device:TPU:10, one launch (start us, length us, event | category | flops | bytes accessed | tf_op | source)
XLA Modules:
  0.0 417.8 jit_solution(15156373857842738273)
XLA Ops:
  11.2 10.7 %slice_reduce_fusion.1 = (bf16[1024,2,256]{2,1,0:T(2,128)(2,1)S(1)}, bf16[1024,2,256]{2,1,0:T(2,128)(2,1)S(1)}) fusion(bf16[1024,2,2,256]{3,2,1,0:T(2,128)(2,1)S(1)} %reshape.426), kind=kLoop, calls=%fused_computation.6 | loop fusion | bytes 4194304 | tf_op jit(solution)/shard_map/slice | solution.py:250
  34.1 16.0 %collective-permute-done = bf16[1024,512]{1,0:T(8,128)(2,1)S(1)} collective-permute-done((bf16[1024,512]{1,0:T(8,128)(2,1)S(1)}, bf16[1024,512]{1,0:T(8,128)(2,1)S(1)}, u32[]{:S(2)}, u32[]{:S(2)}) %collective-permute-start) | collective-permute-done | bytes 1048608 | tf_op jit(solution)/shard_map/ppermute | solution.py:184
  52.6 5.3 %collective-permute-start.5 = (bf16[1024,512]{1,0:T(8,128)(2,1)}, bf16[1024,512]{1,0:T(8,128)(2,1)}, u32[]{:S(2)}, u32[]{:S(2)}) collective-permute-start(bf16[1024,512]{1,0:T(8,128)(2,1)} %collective-permute-done.1), channel_id=1, source_target_pairs={{1,2},{2,3},{5,6},{6,7},{9,10},{10,11},{13,14},{14,15},{17,18},{18... | collective-permute-start | bytes 3145736 | tf_op jit(solution)/shard_map/ppermute | solution.py:185
  57.9 14.6 %collective-permute-done.2 = bf16[1024,512]{1,0:T(8,128)(2,1)S(1)} collective-permute-done((bf16[1024,512]{1,0:T(8,128)(2,1)S(1)}, bf16[1024,512]{1,0:T(8,128)(2,1)S(1)}, u32[]{:S(2)}, u32[]{:S(2)}) %collective-permute-start.2) | collective-permute-done | bytes 1048608 | tf_op jit(solution)/shard_map/ppermute | solution.py:184
  75.0 5.4 %collective-permute-start.7 = (bf16[1024,512]{1,0:T(8,128)(2,1)S(1)}, bf16[1024,512]{1,0:T(8,128)(2,1)}, u32[]{:S(2)}, u32[]{:S(2)}) collective-permute-start(bf16[1024,512]{1,0:T(8,128)(2,1)S(1)} %collective-permute-done.3), channel_id=1, source_target_pairs={{1,2},{2,3},{5,6},{6,7},{9,10},{10,11},{13,14},{14,15},{17,18},{18... | collective-permute-start | bytes 3145736 | tf_op jit(solution)/shard_map/ppermute | solution.py:185
  83.4 11.7 %collective-permute-done.4 = bf16[1024,512]{1,0:T(8,128)(2,1)} collective-permute-done((bf16[1024,512]{1,0:T(8,128)(2,1)S(1)}, bf16[1024,512]{1,0:T(8,128)(2,1)}, u32[]{:S(2)}, u32[]{:S(2)}) %collective-permute-start.4) | collective-permute-done | bytes 1048608 | tf_op jit(solution)/shard_map/ppermute | solution.py:184
  100.6 15.9 %collective-permute-done.6 = bf16[1024,512]{1,0:T(8,128)(2,1)} collective-permute-done((bf16[1024,512]{1,0:T(8,128)(2,1)S(1)}, bf16[1024,512]{1,0:T(8,128)(2,1)}, u32[]{:S(2)}, u32[]{:S(2)}) %collective-permute-start.6) | collective-permute-done | bytes 1048608 | tf_op jit(solution)/shard_map/ppermute | solution.py:184
  127.6 6.6 %block_states.1 = (f32[8,2,128,128]{3,2,1,0:T(8,128)S(1)}, f32[8,128,128]{2,1,0:T(8,128)S(1)}) custom-call(f32[8,1024,3]{2,1,0:T(8,128)} %copy.74.col, bf16[1024,1024]{1,0:T(8,128)(2,1)S(1)} %copy-done, bf16[1024,1024]{1,0:T(8,128)(2,1)S(1)} %copy-done.2), custom_call_target="tpu_custom_call" | custom-call | flops 268435456 | bytes 12582912 | tf_op jit(solution)/shard_map/block_states/pallas_call | solution.py:282
  141.6 17.8 %collective-permute-done.10 = bf16[1024,512]{1,0:T(8,128)(2,1)} collective-permute-done((bf16[1024,512]{1,0:T(8,128)(2,1)}, bf16[1024,512]{1,0:T(8,128)(2,1)}, u32[]{:S(2)}, u32[]{:S(2)}) %collective-permute-start.10) | collective-permute-done | bytes 1048608 | tf_op jit(solution)/shard_map/ppermute | solution.py:184
  162.5 4.5 %constant_dynamic-slice_fusion = (bf16[1,2,1,256,1024]{4,3,2,1,0:T(8,128)(2,1)S(1)}, bf16[1,2,1,256,1024]{4,3,2,1,0:T(8,128)(2,1)S(1)}, bf16[1,2,1,256,1024]{4,3...) fusion(bf16[4,2,2,256,1024]{4,3,2,1,0:T(8,128)(2,1)} %bitcast.1, ...), kind=kLoop, calls=%fused_computation.154 | loop fusion | bytes 16777232 | tf_op jit(solution)/shard_map/dynamic_slice | solution.py:325
  182.0 8.9 %fusion.3.early = f32[1024,1024]{1,0:T(8,128)} fusion(f32[1024,1024]{1,0:T(8,128)} %fusion.65, f32[1024,1024]{1,0:T(8,128)} %fusion.64, f32[1024,1024]{1,0:T(8,128)S(1)} %fusion.43, f32[1024,1024]{1,0:T(8,128)S(1)} %fusion.42, f32[1024,1024]{0,1:T(8,128)S(1)} %fusion.66, f32[1024,1024]{0,1:T(8,128)} %fusion.67, bf16[1024,512]{1,0:T(8,128)(2,1)S(1)} %copy-done.26, ...), kind=kOutput, calls=%fused_computation.4 | convolution fusion | flops 1080033280 | bytes 31457280 | tf_op jit(solution)/shard_map/dot_general | solution.py:331
  190.9 7.2 %grad_mixed_rows.1 = (bf16[1024,1024]{1,0:T(8,128)(2,1)S(1)}, f32[8,2,128,128]{3,2,1,0:T(8,128)S(1)}, f32[8,128,128]{2,1,0:T(8,128)S(1)}) custom-call(f32[8,1024,3]{2,1,0:T(8,128)} %copy.74.col, bf16[1024,1024]{1,0:T(8,128)(2,1)} %q.7, f32[1024,1024]{1,0:T(8,128)} %fusion.3.early, bf16[1024,512]{1,0:T(8,128)(2,1)S(1)} %get-tuple-element.57.last, ...), custom_call_target="tpu_custom_call" | custom-call | flops 1073741824 | bytes 16777216 | tf_op jit(solution)/shard_map/grad_mixed_rows/pallas_call | solution.py:349
  209.9 10.3 %collective-permute-start.16 = (bf16[8,128,128]{2,1,0:T(8,128)(2,1)}, bf16[8,128,128]{2,1,0:T(8,128)(2,1)S(1)}, u32[]{:S(2)}, u32[]{:S(2)}) collective-permute-start(bf16[8,128,128]{2,1,0:T(8,128)(2,1)} %get-tuple-element.76), channel_id=1, source_target_pairs={{0,8},{4,12},{8,0},{12,4},{16,24},{20,28},{24,16},{28,20},{1,9},{5... | collective-permute-start | bytes 786440 | tf_op jit(solution)/shard_map/ppermute | solution.py:158
  221.2 6.3 %collective-permute-done.16 = bf16[8,128,128]{2,1,0:T(8,128)(2,1)S(1)} collective-permute-done((bf16[8,128,128]{2,1,0:T(8,128)(2,1)}, bf16[8,128,128]{2,1,0:T(8,128)(2,1)S(1)}, u32[]{:S(2)}, u32[]{:S(2)}) %collective-permute-start.16) | collective-permute-done | bytes 262176 | tf_op jit(solution)/shard_map/ppermute | solution.py:158
  231.2 5.7 %collective-permute-start.14 = (bf16[8,144,128]{2,1,0:T(8,128)(2,1)}, bf16[8,144,128]{2,1,0:T(8,128)(2,1)}, u32[]{:S(2)}, u32[]{:S(2)}) collective-permute-start(bf16[8,144,128]{2,1,0:T(8,128)(2,1)} %pad_maximum_fusion.3), channel_id=1, source_target_pairs={{0,16},{4,20},{8,24},{12,28},{16,0},{20,4},{24,8},{28,12},{1,17},{... | collective-permute-start | bytes 884744 | tf_op jit(solution)/shard_map/ppermute | solution.py:154
  236.9 5.7 %collective-permute-start.17 = (bf16[8,128,128]{2,1,0:T(8,128)(2,1)}, bf16[8,128,128]{2,1,0:T(8,128)(2,1)}, u32[]{:S(2)}, u32[]{:S(2)}) collective-permute-start(bf16[8,128,128]{2,1,0:T(8,128)(2,1)} %get-tuple-element.74), channel_id=1, source_target_pairs={{0,16},{4,20},{8,24},{12,28},{16,0},{20,4},{24,8},{28,12},{1,17},{... | collective-permute-start | bytes 786440 | tf_op jit(solution)/shard_map/ppermute | solution.py:158
  242.6 11.2 %pair_weights.1 = (bf16[8,2,3,256,256]{4,3,2,1,0:T(8,128)(2,1)}, f32[1024,1024]{1,0:T(8,128)}) custom-call(f32[8,1024,3]{2,1,0:T(8,128)} %copy.74.col, f32[8,1,1024]{2,1,0:T(1,128)S(1)} %compare_select_fusion.row, bf16[1024,1024]{1,0:T(8,128)(2,1)S(1)} %copy-done.4, bf16[1024,1024]{1,0:T(8,128)(2,1)S(1)} %copy-done, bf16[1024,1024]{1,0:T(8,128)(2,1)} %v.7), custom_call_target="tpu_custom_call" | custom-call | flops 3221225472 | bytes 20971520 | tf_op jit(solution)/shard_map/pair_weights/pallas_call | solution.py:293
  256.6 7.5 %mixed_rows.1 = (bf16[1024,1024]{1,0:T(8,128)(2,1)S(1)}, bf16[8,2,128,128]{3,2,1,0:T(8,128)(2,1)S(1)}) custom-call(f32[8,1024,3]{2,1,0:T(8,128)} %copy.74.col, bf16[1024,1024]{1,0:T(8,128)(2,1)} %q.7, f32[1024,1024]{1,0:T(8,128)} %get-tuple-element.20.within, f32[8,2,128,128]{3,2,1,0:T(8,128)S(1)} %copy-done.10, f32[8,128,128]{2,1,0:T(8,128)S(1)} %add_select_fusion.2.start), custom_call_target="tpu_custom_call" | custom-call | flops 268435456 | bytes 12582912 | tf_op jit(solution)/shard_map/mixed_rows/pallas_call | solution.py:303
  283.8 17.4 %block_gradients.1 = (bf16[1024,1024]{1,0:T(8,128)(2,1)}, bf16[1024,1024]{1,0:T(8,128)(2,1)S(1)}, bf16[1024,1024]{1,0:T(8,128)(2,1)S(1)}) custom-call(f32[8,1024,3]{2,1,0:T(8,128)} %copy.74.col, f32[8,1,1024]{2,1,0:T(1,128)S(1)} %compare_select_fusion.row, bf16[1024,1024]{1,0:T(8,128)(2,1)} %q.7, bf16[1024,1024]{1,0:T(8,128)(2,1)} %k.7, ...), custom_call_target="tpu_custom_call" | custom-call | flops 5368709120 | bytes 25165824 | tf_op jit(solution)/shard_map/block_gradients/pallas_call | solution.py:370
  305.1 8.4 %carried_gradients.1 = (bf16[1024,1024]{1,0:T(8,128)(2,1)}, bf16[1024,1024]{1,0:T(8,128)(2,1)}) custom-call(f32[8,1024,3]{2,1,0:T(8,128)} %copy.74.col, bf16[1024,1024]{1,0:T(8,128)(2,1)S(1)} %copy-done.1, bf16[1024,1024]{1,0:T(8,128)(2,1)S(1)} %copy-done.3, bf16[1024,1024]{1,0:T(8,128)(2,1)} %copy-done.7, bf16[1024,1024]{1,0:T(8,128)(2,1)} %copy-done.8, ...), custom_call_target="tpu_custom_call" | custom-call | flops 536870912 | bytes 16777216 | tf_op jit(solution)/shard_map/carried_gradients/pallas_call | solution.py:380
  325.9 4.6 %collective-permute-start.19 = (bf16[256,512]{1,0:T(8,128)(2,1)S(1)}, bf16[256,512]{1,0:T(8,128)(2,1)S(1)}, u32[]{:S(2)}, u32[]{:S(2)}) collective-permute-start(bf16[256,512]{1,0:T(8,128)(2,1)S(1)} %get-tuple-element.63), channel_id=1, source_target_pairs={{0,16},{1,17},{4,20},{5,21},{8,24},{9,25},{12,28},{13,29},{18,2},{... | collective-permute-start | bytes 786440 | tf_op jit(solution)/shard_map/ppermute | solution.py:231
  348.5 15.8 %collective-permute-done.35 = bf16[256,512]{1,0:T(8,128)(2,1)S(1)} collective-permute-done((bf16[256,512]{1,0:T(8,128)(2,1)S(1)}, bf16[256,512]{1,0:T(8,128)(2,1)S(1)}, u32[]{:S(2)}, u32[]{:S(2)}) %collective-permute-start.35) | collective-permute-done | bytes 262176 | tf_op jit(solution)/shard_map/ppermute | solution.py:231
  369.7 12.5 %collective-permute-start.28 = (bf16[256,1024]{1,0:T(8,128)(2,1)S(1)}, bf16[256,1024]{1,0:T(8,128)(2,1)S(1)}, u32[]{:S(2)}, u32[]{:S(2)}) collective-permute-start(bf16[256,1024]{1,0:T(8,128)(2,1)S(1)} %fusion.15), channel_id=1, source_target_pairs={{0,8},{4,12},{9,1},{13,5},{18,26},{22,30},{27,19},{31,23}} | collective-permute-start | bytes 1572872 | tf_op jit(solution)/shard_map/ppermute | solution.py:231
  383.9 4.6 %collective-permute-start.22 = (bf16[256,512]{1,0:T(8,128)(2,1)S(1)}, bf16[256,512]{1,0:T(8,128)(2,1)S(1)}, u32[]{:S(2)}, u32[]{:S(2)}) collective-permute-start(bf16[256,512]{1,0:T(8,128)(2,1)S(1)} %get-tuple-element.62), channel_id=1, source_target_pairs={{8,24},{9,25},{12,28},{13,29},{18,2},{19,3},{22,6},{23,7}} | collective-permute-start | bytes 786440 | tf_op jit(solution)/shard_map/ppermute | solution.py:231
  (275 shorter events, 167.9 us)
Async XLA Ops:
  7.2 155.3 %all-gather.2.cloned.1.call-start = ((), (), s32[]{:S(2)}) async-start(), calls=%async_computation | async-start | bytes 9437184 | tf_op jit(solution)/shard_map/all_gather | solution.py:252
  22.1 27.9 %collective-permute-start = (bf16[1024,512]{1,0:T(8,128)(2,1)S(1)}, bf16[1024,512]{1,0:T(8,128)(2,1)S(1)}, u32[]{:S(2)}, u32[]{:S(2)}) collective-permute-start(bf16[1024,512]{1,0:T(8,128)(2,1)S(1)} %bitcast.134), channel_id=1, source_target_pairs={{1,0},{2,1},{3,2},{5,4},{6,5},{7,6},{9,8},{10,9},{11,10},{13,12},{... | collective-permute-start | bytes 3145736 | tf_op jit(solution)/shard_map/ppermute | solution.py:184
  24.5 28.1 %collective-permute-start.1 = (bf16[1024,512]{1,0:T(8,128)(2,1)S(1)}, bf16[1024,512]{1,0:T(8,128)(2,1)}, u32[]{:S(2)}, u32[]{:S(2)}) collective-permute-start(bf16[1024,512]{1,0:T(8,128)(2,1)S(1)} %bitcast.135), channel_id=1, source_target_pairs={{0,1},{1,2},{2,3},{4,5},{5,6},{6,7},{8,9},{9,10},{10,11},{12,13},{... | collective-permute-start | bytes 3145736 | tf_op jit(solution)/shard_map/ppermute | solution.py:185
  28.3 44.3 %collective-permute-start.2 = (bf16[1024,512]{1,0:T(8,128)(2,1)S(1)}, bf16[1024,512]{1,0:T(8,128)(2,1)S(1)}, u32[]{:S(2)}, u32[]{:S(2)}) collective-permute-start(bf16[1024,512]{1,0:T(8,128)(2,1)S(1)} %bitcast.138), channel_id=1, source_target_pairs={{1,0},{2,1},{3,2},{5,4},{6,5},{7,6},{9,8},{10,9},{11,10},{13,12},{... | collective-permute-start | bytes 3145736 | tf_op jit(solution)/shard_map/ppermute | solution.py:184
  31.6 43.3 %collective-permute-start.3 = (bf16[1024,512]{1,0:T(8,128)(2,1)S(1)}, bf16[1024,512]{1,0:T(8,128)(2,1)S(1)}, u32[]{:S(2)}, u32[]{:S(2)}) collective-permute-start(bf16[1024,512]{1,0:T(8,128)(2,1)S(1)} %bitcast.139), channel_id=1, source_target_pairs={{0,1},{1,2},{2,3},{4,5},{5,6},{6,7},{8,9},{9,10},{10,11},{12,13},{... | collective-permute-start | bytes 3145736 | tf_op jit(solution)/shard_map/ppermute | solution.py:185
  50.1 45.0 %collective-permute-start.4 = (bf16[1024,512]{1,0:T(8,128)(2,1)S(1)}, bf16[1024,512]{1,0:T(8,128)(2,1)}, u32[]{:S(2)}, u32[]{:S(2)}) collective-permute-start(bf16[1024,512]{1,0:T(8,128)(2,1)S(1)} %collective-permute-done), channel_id=1, source_target_pairs={{1,0},{2,1},{5,4},{6,5},{9,8},{10,9},{13,12},{14,13},{17,16},{18,1... | collective-permute-start | bytes 3145736 | tf_op jit(solution)/shard_map/ppermute | solution.py:184
  52.6 45.9 %collective-permute-start.5 = (bf16[1024,512]{1,0:T(8,128)(2,1)}, bf16[1024,512]{1,0:T(8,128)(2,1)}, u32[]{:S(2)}, u32[]{:S(2)}) collective-permute-start(bf16[1024,512]{1,0:T(8,128)(2,1)} %collective-permute-done.1), channel_id=1, source_target_pairs={{1,2},{2,3},{5,6},{6,7},{9,10},{10,11},{13,14},{14,15},{17,18},{18... | collective-permute-start | bytes 3145736 | tf_op jit(solution)/shard_map/ppermute | solution.py:185
  72.6 43.9 %collective-permute-start.6 = (bf16[1024,512]{1,0:T(8,128)(2,1)S(1)}, bf16[1024,512]{1,0:T(8,128)(2,1)}, u32[]{:S(2)}, u32[]{:S(2)}) collective-permute-start(bf16[1024,512]{1,0:T(8,128)(2,1)S(1)} %collective-permute-done.2), channel_id=1, source_target_pairs={{1,0},{2,1},{5,4},{6,5},{9,8},{10,9},{13,12},{14,13},{17,16},{18,1... | collective-permute-start | bytes 3145736 | tf_op jit(solution)/shard_map/ppermute | solution.py:184
  75.0 46.0 %collective-permute-start.7 = (bf16[1024,512]{1,0:T(8,128)(2,1)S(1)}, bf16[1024,512]{1,0:T(8,128)(2,1)}, u32[]{:S(2)}, u32[]{:S(2)}) collective-permute-start(bf16[1024,512]{1,0:T(8,128)(2,1)S(1)} %collective-permute-done.3), channel_id=1, source_target_pairs={{1,2},{2,3},{5,6},{6,7},{9,10},{10,11},{13,14},{14,15},{17,18},{18... | collective-permute-start | bytes 3145736 | tf_op jit(solution)/shard_map/ppermute | solution.py:185
  95.1 42.9 %collective-permute-start.8 = (bf16[1024,512]{1,0:T(8,128)(2,1)}, bf16[1024,512]{1,0:T(8,128)(2,1)}, u32[]{:S(2)}, u32[]{:S(2)}) collective-permute-start(bf16[1024,512]{1,0:T(8,128)(2,1)} %collective-permute-done.4), channel_id=1, source_target_pairs={{1,0},{5,4},{9,8},{13,12},{17,16},{21,20},{25,24},{29,28}} | collective-permute-start | bytes 3145736 | tf_op jit(solution)/shard_map/ppermute | solution.py:184
  98.5 39.6 %collective-permute-start.9 = (bf16[1024,512]{1,0:T(8,128)(2,1)}, bf16[1024,512]{1,0:T(8,128)(2,1)}, u32[]{:S(2)}, u32[]{:S(2)}) collective-permute-start(bf16[1024,512]{1,0:T(8,128)(2,1)} %collective-permute-done.5), channel_id=1, source_target_pairs={{2,3},{6,7},{10,11},{14,15},{18,19},{22,23},{26,27},{30,31}} | collective-permute-start | bytes 3145736 | tf_op jit(solution)/shard_map/ppermute | solution.py:185
  116.5 42.9 %collective-permute-start.10 = (bf16[1024,512]{1,0:T(8,128)(2,1)}, bf16[1024,512]{1,0:T(8,128)(2,1)}, u32[]{:S(2)}, u32[]{:S(2)}) collective-permute-start(bf16[1024,512]{1,0:T(8,128)(2,1)} %collective-permute-done.6), channel_id=1, source_target_pairs={{1,0},{5,4},{9,8},{13,12},{17,16},{21,20},{25,24},{29,28}} | collective-permute-start | bytes 3145736 | tf_op jit(solution)/shard_map/ppermute | solution.py:184
  120.9 38.4 %collective-permute-start.11 = (bf16[1024,512]{1,0:T(8,128)(2,1)}, bf16[1024,512]{1,0:T(8,128)(2,1)}, u32[]{:S(2)}, u32[]{:S(2)}) collective-permute-start(bf16[1024,512]{1,0:T(8,128)(2,1)} %collective-permute-done.7), channel_id=1, source_target_pairs={{2,3},{6,7},{10,11},{14,15},{18,19},{22,23},{26,27},{30,31}} | collective-permute-start | bytes 3145736 | tf_op jit(solution)/shard_map/ppermute | solution.py:185
  137.0 65.0 %collective-permute-start.12 = (bf16[8,144,128]{2,1,0:T(8,128)(2,1)}, bf16[8,144,128]{2,1,0:T(8,128)(2,1)}, u32[]{:S(2)}, u32[]{:S(2)}) collective-permute-start(bf16[8,144,128]{2,1,0:T(8,128)(2,1)} %pad_maximum_fusion.1), channel_id=1, source_target_pairs={{0,4},{4,0},{8,12},{12,8},{16,20},{20,16},{24,28},{28,24},{1,5},{5... | collective-permute-start | bytes 884744 | tf_op jit(solution)/shard_map/ppermute | solution.py:154
  274.5 39.1 %collective-permute-start.23 = (bf16[1,256,1024]{2,1,0:T(8,128)(2,1)}, bf16[1,256,1024]{2,1,0:T(8,128)(2,1)}, u32[]{:S(2)}, u32[]{:S(2)}) collective-permute-start(bf16[1,256,1024]{2,1,0:T(8,128)(2,1)} %select_bitcast_fusion.6), channel_id=1, source_target_pairs={{0,4},{4,0},{8,12},{12,8},{16,20},{20,16},{24,28},{28,24},{1,5},{5... | collective-permute-start | bytes 1572872 | tf_op jit(solution)/shard_map/ppermute | solution.py:216
  278.1 38.0 %collective-permute-start.26 = (bf16[1,256,1024]{2,1,0:T(8,128)(2,1)}, bf16[1,256,1024]{2,1,0:T(8,128)(2,1)}, u32[]{:S(2)}, u32[]{:S(2)}) collective-permute-start(bf16[1,256,1024]{2,1,0:T(8,128)(2,1)} %select_bitcast_fusion.5), channel_id=1, source_target_pairs={{0,4},{4,0},{8,12},{12,8},{16,20},{20,16},{24,28},{28,24},{1,5},{5... | collective-permute-start | bytes 1572872 | tf_op jit(solution)/shard_map/ppermute | solution.py:216
  279.3 38.5 %collective-permute-start.29 = (bf16[1,256,1024]{2,1,0:T(8,128)(2,1)}, bf16[1,256,1024]{2,1,0:T(8,128)(2,1)}, u32[]{:S(2)}, u32[]{:S(2)}) collective-permute-start(bf16[1,256,1024]{2,1,0:T(8,128)(2,1)} %select_bitcast_fusion.4), channel_id=1, source_target_pairs={{0,4},{4,0},{8,12},{12,8},{16,20},{20,16},{24,28},{28,24},{1,5},{5... | collective-permute-start | bytes 1572872 | tf_op jit(solution)/shard_map/ppermute | solution.py:216
  280.3 39.0 %collective-permute-start.18 = (bf16[1,256,1024]{2,1,0:T(8,128)(2,1)}, bf16[1,256,1024]{2,1,0:T(8,128)(2,1)}, u32[]{:S(2)}, u32[]{:S(2)}) collective-permute-start(bf16[1,256,1024]{2,1,0:T(8,128)(2,1)} %select_bitcast_fusion.7), channel_id=1, source_target_pairs={{0,4},{4,0},{8,12},{12,8},{16,20},{20,16},{24,28},{28,24},{1,5},{5... | collective-permute-start | bytes 1572872 | tf_op jit(solution)/shard_map/ppermute | solution.py:216
  281.5 41.7 %collective-permute-start.37 = (bf16[1,256,1024]{2,1,0:T(8,128)(2,1)}, bf16[1,256,1024]{2,1,0:T(8,128)(2,1)}, u32[]{:S(2)}, u32[]{:S(2)}) collective-permute-start(bf16[1,256,1024]{2,1,0:T(8,128)(2,1)} %select_bitcast_fusion.2), channel_id=1, source_target_pairs={{0,4},{4,0},{8,12},{12,8},{16,20},{20,16},{24,28},{28,24},{1,5},{5... | collective-permute-start | bytes 1572872 | tf_op jit(solution)/shard_map/ppermute | solution.py:216
  319.4 47.9 %collective-permute-start.24 = (bf16[256,1024]{1,0:T(8,128)(2,1)S(1)}, bf16[256,1024]{1,0:T(8,128)(2,1)S(1)}, u32[]{:S(2)}, u32[]{:S(2)}) collective-permute-start(bf16[256,1024]{1,0:T(8,128)(2,1)S(1)} %fusion.31), channel_id=1, source_target_pairs={{2,10},{3,11},{6,14},{7,15},{8,0},{9,1},{12,4},{13,5},{18,26},{19,... | collective-permute-start | bytes 1572872 | tf_op jit(solution)/shard_map/ppermute | solution.py:231
  323.2 45.5 %collective-permute-start.27 = (bf16[256,1024]{1,0:T(8,128)(2,1)S(1)}, bf16[256,1024]{1,0:T(8,128)(2,1)S(1)}, u32[]{:S(2)}, u32[]{:S(2)}) collective-permute-start(bf16[256,1024]{1,0:T(8,128)(2,1)S(1)} %fusion.32), channel_id=1, source_target_pairs={{2,18},{3,19},{6,22},{7,23},{10,26},{11,27},{14,30},{15,31},{16,0}... | collective-permute-start | bytes 1572872 | tf_op jit(solution)/shard_map/ppermute | solution.py:231
  345.0 24.7 %collective-permute-start.30 = (bf16[256,1024]{1,0:T(8,128)(2,1)S(1)}, bf16[256,1024]{1,0:T(8,128)(2,1)S(1)}, u32[]{:S(2)}, u32[]{:S(2)}) collective-permute-start(bf16[256,1024]{1,0:T(8,128)(2,1)S(1)} %fusion.33), channel_id=1, source_target_pairs={{1,9},{3,11},{5,13},{7,15},{8,0},{10,2},{12,4},{14,6},{17,25},{19,... | collective-permute-start | bytes 1572872 | tf_op jit(solution)/shard_map/ppermute | solution.py:231
  368.8 28.3 %collective-permute-start.25 = (bf16[256,1024]{1,0:T(8,128)(2,1)S(1)}, bf16[256,1024]{1,0:T(8,128)(2,1)S(1)}, u32[]{:S(2)}, u32[]{:S(2)}) collective-permute-start(bf16[256,1024]{1,0:T(8,128)(2,1)S(1)} %fusion.14), channel_id=1, source_target_pairs={{0,16},{1,17},{4,20},{5,21},{26,10},{27,11},{30,14},{31,15}} | collective-permute-start | bytes 1572872 | tf_op jit(solution)/shard_map/ppermute | solution.py:231
  369.7 28.8 %collective-permute-start.28 = (bf16[256,1024]{1,0:T(8,128)(2,1)S(1)}, bf16[256,1024]{1,0:T(8,128)(2,1)S(1)}, u32[]{:S(2)}, u32[]{:S(2)}) collective-permute-start(bf16[256,1024]{1,0:T(8,128)(2,1)S(1)} %fusion.15), channel_id=1, source_target_pairs={{0,8},{4,12},{9,1},{13,5},{18,26},{22,30},{27,19},{31,23}} | collective-permute-start | bytes 1572872 | tf_op jit(solution)/shard_map/ppermute | solution.py:231
  (72 other events, 951.7 us)
Sparse Core Ops, SparseCore 0:
  9.9 55.5 all-gather.1

commit v2 on v1

v2 whole, which is shorter than its diff:
```python
import functools
import math

import jax
import jax.numpy as jnp
from jax import lax
from jax.experimental import pallas as pl
from jax.experimental.pallas import tpu as pltpu
from jax.sharding import PartitionSpec as P

DK = 128
BLK = 512
LOG2E = math.log2(math.e)
FAR = 1e30
F32 = jnp.float32
BF16 = jnp.bfloat16
PARAMS = pltpu.CompilerParams(vmem_limit_bytes=60 * 1024 * 1024)


def dot(a, b, da=1, db=0):
    return lax.dot_general(a, b, (((da,), (db,)), ((), ())), preferred_element_type=F32)


LIGHT = pl.CostEstimate(flops=1, bytes_accessed=1, transcendentals=0)


def factors_kernel(offset, periods, log_decay, out):
    shape = log_decay.shape
    lane = lax.broadcasted_iota(jnp.int32, shape, 1)
    period = jnp.broadcast_to(periods[...], shape)
    update = lax.rem(offset[0] + lane, period) == 0
    cumul = jnp.where(update, period.astype(F32) * log_decay[...], 0.0)
    place = lane % BLK
    step = 1
    while step < BLK:
        cumul = cumul + jnp.where(place >= step, pltpu.roll(cumul, step, 1), 0.0)
        step *= 2
    left = [cumul[:, t : t + BLK] for t in range(0, shape[1], BLK)]
    left = jnp.concatenate([x[:, BLK - 1 : BLK] - x for x in left], axis=1)
    scaled = cumul * LOG2E
    rows = (
        scaled,
        jnp.where(update, jnp.exp(left), 0.0),
        jnp.exp(cumul),
        jnp.where(update, scaled, FAR),
    )
    out[...] = jnp.zeros(out.shape, F32)
    for h in range(shape[0]):
        for r, x in enumerate(rows):
            out[h, r : r + 1, :] = x[h : h + 1, :]


def columns(factors, h=0):
    return jnp.transpose(factors[h])


def pack_decay(sent, h, decay):
    high = decay.astype(BF16)
    low = (decay - high.astype(F32)).astype(BF16)
    sent[h, DK : DK + 16, :] = jnp.broadcast_to(high, (16, DK))
    sent[h, DK + 16 : DK + 32, :] = jnp.broadcast_to(low, (16, DK))


def lanes_of(h):
    return slice(h * DK, (h + 1) * DK)


def state_kernel(factors, k, v, parts, local, own, sent):
    for h in range(parts.shape[0]):
        col, lanes = columns(factors, h), lanes_of(h)
        state = jnp.zeros((DK, DK), F32)
        decay = jnp.ones((1, 1), F32)
        for b in range(parts.shape[1]):
            at, end = b * BLK, (b + 1) * BLK
            scaled = (k[at:end, lanes].astype(F32) * col[at:end, 1:2]).astype(BF16)
            part = dot(scaled, v[at:end, lanes], 0, 0)
            parts[h, b] = part
            fade = col[end - 1 : end, 2:3]
            state = state * fade + part
            decay = decay * fade
        local[h] = state
        own[h] = jnp.broadcast_to(decay, (8, DK))
        sent[h, 0:DK, :] = state.astype(BF16)
        pack_decay(sent, h, jnp.broadcast_to(decay, (1, DK)))


def add_kernel(a, b, out):
    out[...] = (a[...].astype(F32) + b[...].astype(F32)).astype(BF16)


def total_block(refs):
    block = refs[0][...]
    for other in refs[1:]:
        block = block + other[...]
    return block


def halves_kernel(core, *refs):
    *inputs, mixed, sent, kept = refs
    total = dot(total_block(inputs), mixed[...], 0, 0).astype(BF16)

    @pl.when(pl.program_id(0) == 0)
    def _():
        sent[...] = total

    @pl.when(pl.program_id(0) == 1)
    def _():
        kept[...] = total


def rows_kernel(counts, order, *refs):
    inputs, mixed, out = refs[: sum(counts)], refs[sum(counts)], refs[-1]
    at = 0
    for n, many in enumerate(counts):
        mine = inputs[at : at + many]
        at += many

        @pl.when(pl.program_id(0) == n)
        def _(mine=mine):
            if mine:
                out[...] = dot(total_block(mine), mixed[...], 0, 0).astype(BF16)
            else:
                out[...] = jnp.zeros(out.shape, BF16)


def masks(col, row, at):
    half = BLK // 2
    out = []
    for start in (0, half):
        spread = jnp.exp2(
            col[at + start : at + BLK, 0:1] - row[:, at + start : at + start + half]
        )
        size = (BLK - start, half)
        causal = lax.broadcasted_iota(jnp.int32, size, 0) >= lax.broadcasted_iota(
            jnp.int32, size, 1
        )
        out.append(jnp.where(causal, spread, 0.0))
    return out


def within_kernel(factors, q, k, v, weights, within):
    half = BLK // 2
    for h in range(weights.shape[0]):
        col, lanes = columns(factors, h), lanes_of(h)
        for b in range(weights.shape[1]):
            at, mid, end = b * BLK, b * BLK + half, (b + 1) * BLK
            first, second = masks(col, factors[h, 3:4, :], at)
            first = (dot(q[at:end, lanes], k[at:mid, lanes], 1, 1) * first).astype(BF16)
            second = (dot(q[mid:end, lanes], k[mid:end, lanes], 1, 1) * second).astype(BF16)
            weights[h, b, 0:BLK, :] = first
            weights[h, b, BLK : BLK + half, :] = second
            part = dot(first, v[at:mid, lanes])
            within[at:mid, lanes] = part[:half]
            within[mid:end, lanes] = part[half:] + dot(second, v[mid:end, lanes])


def mixed_kernel(factors, q, within, parts, start, mixed, states):
    for h in range(parts.shape[0]):
        col, lanes = columns(factors, h), lanes_of(h)
        state = start[h]
        for b in range(parts.shape[1]):
            at, end = b * BLK, (b + 1) * BLK
            small = state.astype(BF16)
            states[h, b] = small
            carried = dot(q[at:end, lanes], small)
            total = within[at:end, lanes] + col[at:end, 2:3] * carried
            mixed[at:end, lanes] = total.astype(BF16)
            state = state * col[end - 1 : end, 2:3] + parts[h, b]


def block_products(counts, rows, blocks):
    total = None
    at = 0
    for n, many in enumerate(counts):
        block = blocks[at][...]
        for other in blocks[at + 1 : at + many]:
            block = block + other[...]
        at += many
        part = dot(block, rows(n))
        total = part if total is None else total + part
    return total


def early_kernel(counts, order, *refs):
    *inputs, out = refs
    shards, inputs = inputs[-len(counts) :], inputs[: -len(counts)]
    before, blocks = (inputs[0], inputs[1:]) if len(inputs) > sum(counts) else (None, inputs)
    total = block_products(counts, lambda n: shards[n][...], blocks)
    out[...] = total if before is None else before[...] + total


def grad_kernel(counts, order, factors, q, early, *refs):
    *blocks, weight, e, parts, local, sent = refs
    e[...] = (early[...] + block_products(counts, lambda n: weight[...], blocks)).astype(BF16)
    for h in range(parts.shape[0]):
        col, lanes = columns(factors, h), lanes_of(h)
        state = jnp.zeros((DK, DK), F32)
        for b in reversed(range(parts.shape[1])):
            at, end = b * BLK, (b + 1) * BLK
            scaled = (q[at:end, lanes].astype(F32) * col[at:end, 2:3]).astype(BF16)
            part = dot(scaled, e[at:end, lanes], 0, 0)
            parts[h, b] = part
            state = state * col[end - 1 : end, 2:3] + part
        local[h] = state
        sent[h] = state.astype(BF16)


def back_kernel(factors, q, k, v, e, weights, states, dq, dk, dv):
    half = BLK // 2
    for h in range(weights.shape[0]):
        col, lanes = columns(factors, h), lanes_of(h)
        first, second = masks(col, factors[h, 3:4, :], 0)
        first = (dot(e[:, lanes], v[0:half, lanes], 1, 1) * first).astype(BF16)
        second = (dot(e[half:BLK, lanes], v[half:BLK, lanes], 1, 1) * second).astype(BF16)
        carried = col[:, 2:3] * dot(e[:, lanes], states[h, 0], 1, 1) + dot(first, k[0:half, lanes])
        dq[0:half, lanes] = carried[:half].astype(BF16)
        more = dot(second, k[half:BLK, lanes])
        dq[half:BLK, lanes] = (carried[half:] + more).astype(BF16)
        dk[0:half, lanes] = dot(first, q[:, lanes], 0, 0).astype(BF16)
        dk[half:BLK, lanes] = dot(second, q[half:BLK, lanes], 0, 0).astype(BF16)
        dv[0:half, lanes] = dot(weights[h, 0, 0:BLK, :], e[:, lanes], 0, 0).astype(BF16)
        tail = weights[h, 0, BLK : BLK + half, :]
        dv[half:BLK, lanes] = dot(tail, e[half:BLK, lanes], 0, 0).astype(BF16)


def finish_kernel(factors, k, v, dk_part, dv_part, parts, finish, dk, dv):
    for h in range(finish.shape[0]):
        col, lanes = columns(factors, h), lanes_of(h)
        state = finish[h]
        for b in reversed(range(parts.shape[1])):
            at, end = b * BLK, (b + 1) * BLK
            small = state.astype(BF16)
            factor = col[at:end, 1:2]
            more = factor * dot(v[at:end, lanes], small, 1, 1)
            dk[at:end, lanes] = (dk_part[at:end, lanes].astype(F32) + more).astype(BF16)
            more = factor * dot(k[at:end, lanes], small)
            dv[at:end, lanes] = (dv_part[at:end, lanes].astype(F32) + more).astype(BF16)
            state = state * col[end - 1 : end, 2:3] + parts[h, b]


def log2_of(count):
    bits = count.bit_length() - 1
    assert 1 << bits == count
    return bits


def tie(value, *after):
    return lax.optimization_barrier((value,) + after)[0] if after else value


def call(kernel, *args, out, name, prefetch=0):
    return pl.pallas_call(
        kernel,
        grid_spec=pltpu.PrefetchScalarGridSpec(
            num_scalar_prefetch=prefetch,
            grid=(1,),
            in_specs=[pl.BlockSpec(x.shape, lambda *_, r=x.ndim: (0,) * r) for x in args[prefetch:]],
            out_specs=[pl.BlockSpec(x.shape, lambda *_, r=len(x.shape): (0,) * r) for x in out],
        ),
        out_shape=out,
        compiler_params=PARAMS,
        cost_estimate=LIGHT,
        name=name,
    )(*args)


def with_decay(state, decay):
    high = decay.astype(BF16)
    low = (decay - high.astype(F32)).astype(BF16)
    pair = [jnp.broadcast_to(x, x.shape[:1] + (16, DK)) for x in (high, low)]
    return jnp.concatenate([state.astype(BF16)] + pair, axis=1)


def decay_of(got):
    return got[:, DK : DK + 1, :].astype(F32) + got[:, DK + 16 : DK + 17, :].astype(F32)


class Scan:
    def __init__(self, total, own, sent, reverse, known=None):
        self.total, self.own, self.sent, self.reverse = total, own, sent, reverse
        self.first, self.known = known is None, known or {}

    def permute(self, value, mask):
        count = lax.axis_size("tm")
        return lax.ppermute(value, "tm", [(i, i ^ mask) for i in range(count)])

    def send_pair(self):
        self.got = self.permute(self.sent, 1)

    def take_pair(self, *after):
        got = tie(self.got, *after)
        if self.first:
            self.known[0] = decay_of(got)
        other = self.known[0]
        came = got[:, :DK].astype(F32)
        upper = lax.axis_index("tm") % 2 == 1
        self.takes = upper != self.reverse
        self.near, self.across = came, self.own
        here = jnp.where(self.takes, self.own, 1.0) * came
        self.pair = here + jnp.where(self.takes, 1.0, other) * self.total
        return self.pair

    def send_all(self):
        pairs = lax.axis_size("tm") // 2
        if self.first:
            sent = with_decay(self.pair, self.own * self.known[0])
        else:
            sent = self.pair.astype(BF16)
        self.all = {m: self.permute(sent, 2 * m) for m in range(1, pairs)}

    def take_all(self, *after):
        mine = lax.axis_index("tm") // 2
        got = {m: tie(x, *after) for m, x in self.all.items()}
        if self.first:
            self.known.update({m: decay_of(x) for m, x in got.items()})
        before = (lambda a, b: a > b) if self.reverse else (lambda a, b: a < b)
        state = None
        for m, x in got.items():
            weight = jnp.where(before(mine ^ m, mine), 1.0, 0.0)
            for n in got:
                if n != m:
                    between = before(mine ^ m, mine ^ n) & before(mine ^ n, mine)
                    weight = weight * jnp.where(between, self.known[n], 1.0)
            part = weight * x[:, :DK].astype(F32)
            state = part if state is None else state + part
        other = jnp.where(self.takes, self.known[0], 1.0)
        return other * state + jnp.where(self.takes, self.near, 0.0)


def block_order(size):
    return [sorted(range(size), key=lambda q: (abs(p - q), p ^ q)) for p in range(size)]


def pick(by_plane, make):
    plane = lax.axis_index("head")
    keys = sorted(set(by_plane))
    out = make(keys[0])
    for key in keys[1:]:
        here = functools.reduce(
            jnp.logical_or, [plane == p for p, own in enumerate(by_plane) if own == key]
        )
        out = jnp.where(here, make(key), out)
    return out


def line_plan(order):
    size = len(order)
    plan, names = {}, {(0, p): (0, 0, 0) for p in range(size)}
    for s in range(1, size):
        edges = {}
        for p in range(size):
            q = order[p][s]
            edges.setdefault(abs(q - p), []).append((p + (1 if q > p else -1), p))
        for distance, group in edges.items():
            split = len({source for source, _ in group}) < len(group)
            for source, p in group:
                name = (distance, s, int(split and source < p))
                names[s, p] = name
                plan.setdefault(name, []).append((source, p))
    held = {
        name: {source: names[order[source].index(order[p][name[1]]), source] for source, p in edges}
        for name, edges in plan.items()
    }
    return plan, held


class Line:
    def __init__(self, own, order):
        self.plan, self.held = line_plan(order)
        self.raw = {(0, 0, 0): own}
        self.sent = 0

    def send(self, *after):
        self.sent += 1
        for name in sorted(self.plan):
            if name[0] == self.sent:
                held = self.held[name]
                some = min(held.values())
                by_plane = [held.get(p, some) for p in range(lax.axis_size("head"))]
                value = tie(pick(by_plane, lambda key: self.raw[key]), *after)
                self.raw[name] = lax.ppermute(value, "head", self.plan[name])

    def close(self, *after):
        names = [name for name in sorted(self.plan) if name[0] == self.sent]
        tied = lax.optimization_barrier(tuple(self.raw[name] for name in names) + after)
        self.raw.update(zip(names, tied))
        return tied[0]

    def slot(self, s):
        return [self.raw[name] for name in sorted(self.raw) if name[1] == s]


def add(a, b):
    rows, width = a.shape
    spec = pl.BlockSpec((rows // 2, width), lambda n: (n, 0))
    return pl.pallas_call(
        add_kernel,
        grid=(2,),
        in_specs=[spec, spec],
        out_specs=spec,
        out_shape=jax.ShapeDtypeStruct(a.shape, BF16),
        compiler_params=PARAMS,
        cost_estimate=LIGHT,
        name="add_rows",
    )(a, b)


class Tree:
    def __init__(self, held, targets, flips):
        self.targets, self.flips = targets, flips
        span = held.shape[1] // len(flips)
        self.now = [held[:, n * span : (n + 1) * span] for n in range(len(flips))]
        self.got, self.turn, self.done = None, 0, [0] * len(flips)

    def send(self, *after):
        count, size = lax.axis_size("tm"), lax.axis_size("head")
        self.got = []
        for n, order in enumerate(self.flips):
            bit = order[self.turn]
            perm = []
            for i in range(count):
                for p in range(size):
                    far = (i // 2) ^ self.targets[p]
                    if far & bit and not far & self.done[n]:
                        perm.append((i * size + p, (i ^ (bit * 2)) * size + p))
            self.got.append(lax.ppermute(tie(self.now[n], *after), ("tm", "head"), perm))
            self.done[n] |= bit

    def take(self, *after):
        got = [tie(x, *after) for x in self.got]
        self.now = [add(x, y) for x, y in zip(self.now, got)]
        self.turn += 1
        self.got = None

    def finished(self):
        return self.turn == len(self.flips[0])


def per_device(query, key, value, grad_out, out_weight, periods, log_decay):
    tok, width = query.shape
    heads = periods.shape[0]
    blocks = tok // BLK
    count, size = lax.axis_size("tm"), lax.axis_size("head")
    group = count // size
    plane = lax.axis_index("head")
    place = lax.axis_index("tm")
    group_bits = [1 << b for b in range(log2_of(size))]
    order = block_order(size)
    assert group == 2

    line = Line(grad_out, order)
    line.send()
    full_weight = lax.all_gather(out_weight, "tm", axis=0, tiled=True)

    factors = pl.pallas_call(
        factors_kernel,
        in_specs=[
            pl.BlockSpec(memory_space=pltpu.SMEM),
            pl.BlockSpec(memory_space=pltpu.VMEM),
            pl.BlockSpec(memory_space=pltpu.VMEM),
        ],
        out_specs=pl.BlockSpec(memory_space=pltpu.VMEM),
        out_shape=jax.ShapeDtypeStruct((heads, 8, tok), F32),
        compiler_params=PARAMS,
            cost_estimate=LIGHT,
        name="factors",
    )((place * tok).astype(jnp.int32)[None], periods[:, None], log_decay)

    half = BLK // 2
    many = math.gcd(heads, 4)
    head_rows = pl.BlockSpec((tok, many * DK), lambda h: (0, h))
    head_factors = pl.BlockSpec((many, 8, tok), lambda h: (h, 0, 0))
    block_states = pl.BlockSpec((many, blocks, DK, DK), lambda h: (h, 0, 0, 0))
    one_state = pl.BlockSpec((many, DK, DK), lambda h: (h, 0, 0))
    weight_rows = BLK + half
    weights_spec = pl.BlockSpec((many, blocks, weight_rows, half), lambda h: (h, 0, 0, 0))
    shape = jax.ShapeDtypeStruct
    states_f32 = shape((heads, blocks, DK, DK), F32)
    states_bf16 = shape((heads, blocks, DK, DK), BF16)
    state_f32 = shape((heads, DK, DK), F32)
    rows_bf16 = shape((tok, width), BF16)

    small = shape((heads, 8, DK), F32)
    fwd_parts, fwd_local, fwd_own, fwd_sent = pl.pallas_call(
        state_kernel,
        grid=(heads // many,),
        in_specs=[head_factors, head_rows, head_rows],
        out_specs=[
            block_states,
            one_state,
            pl.BlockSpec((many, 8, DK), lambda h: (h, 0, 0)),
            pl.BlockSpec((many, DK + 32, DK), lambda h: (h, 0, 0)),
        ],
        out_shape=[states_f32, state_f32, small, shape((heads, DK + 32, DK), BF16)],
        compiler_params=PARAMS,
            cost_estimate=LIGHT,
        name="block_states",
    )(factors, key, value)
    scan = Scan(fwd_local, fwd_own[:, :1], fwd_sent, False)
    scan.send_pair()
    scan.take_pair()
    scan.send_all()
    weights, within = pl.pallas_call(
        within_kernel,
        grid=(heads // many,),
        in_specs=[head_factors, head_rows, head_rows, head_rows],
        out_specs=[weights_spec, head_rows],
        out_shape=[shape((heads, blocks, weight_rows, half), BF16), shape((tok, width), F32)],
        compiler_params=PARAMS,
            cost_estimate=LIGHT,
        name="pair_weights",
    )(tie(factors, scan.pair), query, key, value)
    mark = line.close(within)
    line.send(mark)
    state_in = scan.take_all(mark)
    mixed, states = pl.pallas_call(
        mixed_kernel,
        grid=(heads // many,),
        in_specs=[head_factors, head_rows, head_rows, block_states, one_state],
        out_specs=[head_rows, block_states],
        out_shape=[rows_bf16, states_bf16],
        compiler_params=PARAMS,
            cost_estimate=LIGHT,
        name="mixed_rows",
    )(factors, query, within, fwd_parts, state_in)

    mine = jnp.take(jnp.array(order, jnp.int32), plane, axis=0)

    def targets(s):
        return [order[p][s] for p in range(size)]

    core = (place % 2).astype(jnp.int32)[None]

    sub = grad_out.shape[1] // 4
    whole_mixed = pl.BlockSpec((tok, width), lambda k, i, o: (0, 0))

    def halves_of(arrays, *after):
        block = pl.BlockSpec((tok, sub), lambda k, i, o: (0, 2 * (o[0] ^ (1 - k)) + i))
        out = shape((2 * sub, width), BF16)
        return pl.pallas_call(
            halves_kernel,
            grid_spec=pltpu.PrefetchScalarGridSpec(
                num_scalar_prefetch=1,
                grid=(2, 2),
                in_specs=[block] * len(arrays) + [whole_mixed],
                out_specs=[
                    pl.BlockSpec((sub, width), lambda k, i, o: (jnp.where(k == 0, i, 1), 0)),
                    pl.BlockSpec((sub, width), lambda k, i, o: (jnp.where(k == 0, 0, i), 0)),
                ],
            ),
            out_shape=[out, out],
            compiler_params=PARAMS,
            cost_estimate=LIGHT,
            name="weight_halves",
        )(tie(core, *after), *arrays, mixed)

    def rows_of(slots, held, *after):
        arrays, specs, counts = [], [], []
        for n, s in enumerate(slots):
            mine_of = line.slot(s) if s < size - 1 else []
            counts.append(len(mine_of))
            arrays += mine_of
            specs += [
                pl.BlockSpec((tok, sub), lambda k, i, o, n=n: (0, jnp.where(k == n, i, 3 * (k > n))))
            ] * len(mine_of)
        held = [] if held is None else [held]
        place_of = jnp.stack([mine[s] for s in slots])
        return pl.pallas_call(
            functools.partial(rows_kernel, counts),
            grid_spec=pltpu.PrefetchScalarGridSpec(
                num_scalar_prefetch=1,
                grid=(len(slots), 4),
                in_specs=specs + [whole_mixed] + [pl.BlockSpec(memory_space=pl.ANY)] * len(held),
                out_specs=pl.BlockSpec((sub, width), lambda k, i, o: (o[k] * 4 + i, 0)),
            ),
            out_shape=shape((size * 4 * sub, width), BF16),
            input_output_aliases={len(arrays) + 2: 0} if held else {},
            compiler_params=PARAMS,
            cost_estimate=LIGHT,
            name="weight_rows",
        )(tie(place_of, *after), *arrays, mixed, *held)

    def swap(sent, *after):
        return lax.ppermute(tie(sent, *after), "tm", [(i, i ^ 1) for i in range(count)])

    def joined(kept, got, *after):
        return add(kept, tie(got, *after))

    two = 2 if heads % 2 == 0 else 1
    cover = two * DK
    wide = pl.BlockSpec((tok, cover), lambda n, o: (0, n))
    depth = grad_out.shape[1]

    def accumulate(before, slots, *after):
        inputs = [line.slot(s) for s in slots]
        arrays = [x for y in inputs for x in y]
        held = [] if before is None else [before]
        return pl.pallas_call(
            functools.partial(early_kernel, [len(x) for x in inputs]),
            grid_spec=pltpu.PrefetchScalarGridSpec(
                num_scalar_prefetch=1,
                grid=(width // cover,),
                in_specs=[wide] * len(held)
                + [pl.BlockSpec(x.shape, lambda n, o: (0, 0)) for x in arrays]
                + [pl.BlockSpec((depth, cover), lambda n, o, s=s: (o[s], n)) for s in slots],
                out_specs=wide,
            ),
            out_shape=shape((tok, width), F32),
            compiler_params=PARAMS,
            cost_estimate=LIGHT,
            name="early_product",
        )(tie(mine, *after), *held, *arrays, *[full_weight] * len(slots))

    slots = list(range(min(2, size - 1)))
    products = rows_of(slots, None)
    early = accumulate(None, slots, products)
    for s in range(2, size - 1):
        mark = line.close(early)
        line.send(mark)
        final = [size - 1] if s == size - 2 else []
        products = rows_of([s] + final, products, mark)
        early = accumulate(early, [s], products)
    most = lax.psum_scatter(products, "tm", scatter_dimension=0, tiled=True)
    mark = line.close(early)

    whole = line.slot(size - 1)
    pair_state = pl.BlockSpec((two, DK, DK), lambda n, o: (n, 0, 0))
    e, parts, local, sent = pl.pallas_call(
        functools.partial(grad_kernel, [len(whole)]),
        grid_spec=pltpu.PrefetchScalarGridSpec(
            num_scalar_prefetch=1,
            grid=(width // cover,),
            in_specs=[pl.BlockSpec((two, 8, tok), lambda n, o: (n, 0, 0)), wide, wide]
            + [pl.BlockSpec(x.shape, lambda n, o: (0, 0)) for x in whole]
            + [pl.BlockSpec((depth, cover), lambda n, o: (o[size - 1], n))],
            out_specs=[
                wide,
                pl.BlockSpec((two, blocks, DK, DK), lambda n, o: (n, 0, 0, 0)),
                pair_state,
                pair_state,
            ],
        ),
        out_shape=[rows_bf16, states_f32, state_f32, shape((heads, DK, DK), BF16)],
        compiler_params=PARAMS,
        cost_estimate=LIGHT,
        name="grad_mixed_rows",
    )(mine, factors, query, early, *whole, full_weight)
    back = Scan(local, fwd_own[:, :1], sent, True, scan.known)
    back.send_pair()
    sent, kept = halves_of(whole, e)
    got = swap(sent)
    back.take_pair(kept)
    back.send_all()
    held = joined(kept, got, back.pair)
    last_tree = Tree(held, targets(size - 1), [group_bits[::-1], group_bits])
    last_tree.send()
    own_rows = pl.BlockSpec((BLK, many * DK), lambda h, b: (b, h))
    dq, dk_part, dv_part = pl.pallas_call(
        back_kernel,
        grid=(heads // many, blocks),
        in_specs=[pl.BlockSpec((many, 8, BLK), lambda h, b: (h, 0, b))]
        + [own_rows] * 4
        + [
            pl.BlockSpec((many, 1, weight_rows, half), lambda h, b: (h, b, 0, 0)),
            pl.BlockSpec((many, 1, DK, DK), lambda h, b: (h, b, 0, 0)),
        ],
        out_specs=[own_rows] * 3,
        out_shape=[rows_bf16] * 3,
        compiler_params=PARAMS,
        cost_estimate=LIGHT,
        name="block_gradients",
    )(tie(factors, held), query, key, value, e, weights, states)
    grad_in = back.take_all(dq)
    for _ in group_bits[1:]:
        last_tree.take(grad_in)
        last_tree.send()
    pair_rows = pl.BlockSpec((tok, cover), lambda n: (0, n))
    dk, dv = pl.pallas_call(
        finish_kernel,
        grid=(heads // two,),
        in_specs=[pl.BlockSpec((two, 8, tok), lambda n: (n, 0, 0))]
        + [pair_rows] * 4
        + [
            pl.BlockSpec((two, blocks, DK, DK), lambda n: (n, 0, 0, 0)),
            pl.BlockSpec((two, DK, DK), lambda n: (n, 0, 0)),
        ],
        out_specs=[pair_rows] * 2,
        out_shape=[rows_bf16] * 2,
        compiler_params=PARAMS,
        cost_estimate=LIGHT,
        name="carried_gradients",
    )(factors, key, value, dk_part, dv_part, parts, tie(grad_in, last_tree.now[0]))
    done = [x.astype(F32) + tie(y, dk).astype(F32) for x, y in zip(last_tree.now, last_tree.got)]
    done = jnp.concatenate(done, axis=1)
    grad_weight = most.astype(F32) + jnp.where(mine[size - 1] == place // group, done, 0.0)
    return dq, dk, dv, grad_weight


def solution(mesh):
    both = P("tm", "head")
    return jax.shard_map(
        per_device,
        mesh=mesh,
        in_specs=(both, both, both, both, both, P("head"), P("head", "tm")),
        out_specs=(both, both, both, both),
        check_vma=False,
    )
```

time: 426 us -> 248 us (0.58)
  the two profiles are of different devices: /device:TPU:10 before, /device:TPU:16 now
where the time goes in v2:
time: 248 us; the launch traced here: 244 us
  Pallas kernels  108 us (44%)
  waiting for transfers between devices  82 us (33%)
  starting transfers between devices  23 us (9%)
  between operations  15 us (6%)
  other arithmetic  8.93 us (4%)
  local copies, waits for them, and re-layouts  7.69 us (3%)
    ppermute x5, waiting for transfers between devices, send(): self.raw[name] = lax.ppermute(value, 'head', self.plan[name])  56.8 us
    pallas_call x2, Pallas kernels, rows_of(): pl.pallas_call(functools.partial(rows_kernel, counts), grid_spec=pltpu.Pr...  20 us
    pallas_call x2, Pallas kernels, accumulate(): pl.pallas_call(functools.partial(early_kernel, [len(x) for x in inputs]),...  19 us
    ppermute x8, waiting for transfers between devices, permute(): return lax.ppermute(value, 'tm', [(i, i ^ mask) for i in range(count)])  17.3 us
    pallas_call x1, Pallas kernels, per_device(): pl.pallas_call(back_kernel, grid=(heads // many, blocks), in_specs=[pl.Bl...  12.4 us
    pallas_call x1, Pallas kernels, per_device(): pl.pallas_call(functools.partial(grad_kernel, [len(whole)]), grid_spec=pl...  10.4 us
    ppermute x5, starting transfers between devices, send(): self.raw[name] = lax.ppermute(value, 'head', self.plan[name])  10.1 us
    pallas_call x1, Pallas kernels, per_device(): pl.pallas_call(within_kernel, grid=(heads // many,), in_specs=[head_facto...  9.96 us
  transfers between devices with their start and end apart: 20, of which 11 were waited for; matrix products, arithmetic and copies ran while one was open for 4% of the time, Pallas kernels for 40%

profile of v2, /device:TPU:16, one launch (start us, length us, event | category | flops | bytes accessed | tf_op | source)
XLA Modules:
  0.0 244.4 jit_solution(4481160984473143211)
XLA Ops:
  7.9 2.4 collective-permute-start.1
  11.7 2.5 %factors.1 = f32[8,8,1024]{2,1,0:T(8,128)} custom-call(s32[1]{0:T(128)} %bitcast.offset, s32[8,1]{1,0:T(8,128)} %copy.14.periods, f32[8,1024]{1,0:T(8,128)} %log_decay.1), custom_call_target="tpu_custom_call" | custom-call | flops 1 | bytes 1 | tf_op jit(solution)/shard_map/factors/pallas_call | solution.py:455
  14.2 6.6 %block_states.1 = (f32[8,2,128,128]{3,2,1,0:T(8,128)}, f32[8,128,128]{2,1,0:T(8,128)}, f32[8,8,128]{2,1,0:T(8,128)}, bf16[8,160,128]{2,1,0:T(8,128)(2,1)}) custom-call(f32[8,8,1024]{2,1,0:T(8,128)} %factors.1, bf16[1024,1024]{1,0:T(8,128)(2,1)} %k.7, bf16[1024,1024]{1,0:T(8,128)(2,1)} %v.7), custom_call_target="tpu_custom_call" | custom-call | flops 1 | bytes 1 | tf_op jit(solution)/shard_map/block_states/pallas_call | solution.py:484
  24.6 10.0 %pair_weights.1 = (bf16[8,2,768,256]{3,2,1,0:T(8,128)(2,1)}, f32[1024,1024]{1,0:T(8,128)}) custom-call(f32[8,8,1024]{2,1,0:T(8,128)} %factors.1, bf16[1024,1024]{1,0:T(8,128)(2,1)} %q.7, bf16[1024,1024]{1,0:T(8,128)(2,1)} %k.7, bf16[1024,1024]{1,0:T(8,128)(2,1)} %v.7), custom_call_target="tpu_custom_call" | custom-call | flops 1 | bytes 1 | tf_op jit(solution)/shard_map/pair_weights/pallas_call | solution.py:503
  34.5 22.9 %collective-permute-done.1.refs_0_.refs_1_ = bf16[1024,1024]{1,0:T(8,128)(2,1)S(1)} collective-permute-done((bf16[1024,1024]{1,0:T(8,128)(2,1)}, bf16[1024,1024]{1,0:T(8,128)(2,1)S(1)}, u32[]{:S(2)}, u32[]{:S(2)}) %collective-permute-start.1) | collective-permute-done | bytes 2097184 | tf_op jit(solution)/shard_map/ppermute | solution.py:381
  57.8 3.5 %collective-permute-start.4 = (bf16[1024,1024]{1,0:T(8,128)(2,1)}, bf16[1024,1024]{1,0:T(8,128)(2,1)}, u32[]{:S(2)}, u32[]{:S(2)}) collective-permute-start(bf16[1024,1024]{1,0:T(8,128)(2,1)} %collective-permute-done.refs_1_), channel_id=1, source_target_pairs={{2,1},{1,2},{6,5},{5,6},{10,9},{9,10},{14,13},{13,14},{18,17},{17,... | collective-permute-start | bytes 6291464 | tf_op jit(solution)/shard_map/ppermute | solution.py:381
  61.3 2.6 %collective-permute-start.3 = (bf16[1024,1024]{1,0:T(8,128)(2,1)S(1)}, bf16[1024,1024]{1,0:T(8,128)(2,1)}, u32[]{:S(2)}, u32[]{:S(2)}) collective-permute-start(bf16[1024,1024]{1,0:T(8,128)(2,1)S(1)} %collective-permute-done.1.refs_0_.refs_1_), channel_id=1, source_target_pairs={{1,0},{2,3},{5,4},{6,7},{9,8},{10,11},{13,12},{14,15},{17,16},{18,... | collective-permute-start | bytes 6291464 | tf_op jit(solution)/shard_map/ppermute | solution.py:381
  68.6 6.6 %collective-permute-done.7 = bf16[8,160,128]{2,1,0:T(8,128)(2,1)S(1)} collective-permute-done((bf16[8,160,128]{2,1,0:T(8,128)(2,1)S(1)}, bf16[8,160,128]{2,1,0:T(8,128)(2,1)S(1)}, u32[]{:S(2)}, u32[]{:S(2)}) %collective-permute-start.7) | collective-permute-done | bytes 327712 | tf_op jit(solution)/shard_map/ppermute | solution.py:285
  75.2 5.4 %collective-permute-done.6 = bf16[8,160,128]{2,1,0:T(8,128)(2,1)S(1)} collective-permute-done((bf16[8,160,128]{2,1,0:T(8,128)(2,1)S(1)}, bf16[8,160,128]{2,1,0:T(8,128)(2,1)S(1)}, u32[]{:S(2)}, u32[]{:S(2)}) %collective-permute-start.6) | collective-permute-done | bytes 327712 | tf_op jit(solution)/shard_map/ppermute | solution.py:285
  83.1 5.9 %mixed_rows.1 = (bf16[1024,1024]{1,0:T(8,128)(2,1)}, bf16[8,2,128,128]{3,2,1,0:T(8,128)(2,1)}) custom-call(f32[8,8,1024]{2,1,0:T(8,128)} %factors.1, bf16[1024,1024]{1,0:T(8,128)(2,1)} %q.7, f32[1024,1024]{1,0:T(8,128)} %get-tuple-element.54.within, f32[8,2,128,128]{3,2,1,0:T(8,128)} %get-tuple-element.59.parts, f32[8,128,128]{2,1,0:T(8,128)} %fusion.2.start), custom_call_target="tpu_custom_call" | custom-call | flops 1 | bytes 1 | tf_op jit(solution)/shard_map/mixed_rows/pallas_call | solution.py:516
  89.0 11.0 %weight_rows.2.refs_3_ = bf16[4096,1024]{1,0:T(8,128)(2,1)} custom-call(s32[2]{0:T(128)} %get-tuple-element.136.order, bf16[1024,1024]{1,0:T(8,128)(2,1)} %refs_0_.3, bf16[1024,1024]{1,0:T(8,128)(2,1)} %collective-permute-done.refs_1_, bf16[1024,1024]{1,0:T(8,128)(2,1)} %get-tuple-element.63.refs_2_), custom_call_target="tpu_custom_call" | custom-call | flops 1 | bytes 1 | tf_op jit(solution)/shard_map/weight_rows/pallas_call | solution.py:568
  100.0 9.8 %early_product.2.refs_0_ = f32[1024,1024]{1,0:T(8,128)} custom-call(s32[4]{0:T(128)} %fusion.21.order, bf16[1024,1024]{1,0:T(8,128)(2,1)} %refs_0_.3, bf16[1024,1024]{1,0:T(8,128)(2,1)} %collective-permute-done.refs_1_, bf16[4096,1024]{1,0:T(8,128)(2,1)} %all-gather.2.cloned.1.call-done.refs_2_.refs_3_, ...), custom_call_target="tpu_custom_call" | custom-call | flops 1 | bytes 1 | tf_op jit(solution)/shard_map/early_product/pallas_call | solution.py:598
  109.8 9.0 %weight_rows.3 = bf16[4096,1024]{1,0:T(8,128)(2,1)} custom-call(s32[2]{0:T(128)} %get-tuple-element.66.order, bf16[1024,1024]{1,0:T(8,128)(2,1)} %copy-done, bf16[1024,1024]{1,0:T(8,128)(2,1)} %collective-permute-done.3.refs_1_.refs_2_, bf16[1024,1024]{1,0:T(8,128)(2,1)} %get-tuple-element.63.refs_2_, ...), custom_call_target="tpu_custom_call", output_to_operand_aliasing={{}: (4, {})} | custom-call | flops 1 | bytes 1 | tf_op jit(solution)/shard_map/weight_rows/pallas_call | solution.py:568
  120.4 9.2 %early_product.3.early = f32[1024,1024]{1,0:T(8,128)} custom-call(s32[4]{0:T(128)} %fusion.21.order, f32[1024,1024]{1,0:T(8,128)} %early_product.2.refs_0_, bf16[1024,1024]{1,0:T(8,128)(2,1)} %copy-done, bf16[1024,1024]{1,0:T(8,128)(2,1)} %collective-permute-done.3.refs_1_.refs_2_, bf16[4096,1024]{1,0:T(8,128)(2,1)} %all-gather.2.cloned.1.call-done.refs_2_.refs_3_), custom_call_target="tpu_custom_call" | custom-call | flops 1 | bytes 1 | tf_op jit(solution)/shard_map/early_product/pallas_call | solution.py:598
  129.6 33.5 %collective-permute-done.8.refs_1_ = bf16[1024,1024]{1,0:T(8,128)(2,1)S(1)} collective-permute-done((bf16[1024,1024]{1,0:T(8,128)(2,1)}, bf16[1024,1024]{1,0:T(8,128)(2,1)S(1)}, u32[]{:S(2)}, u32[]{:S(2)}) %collective-permute-start.8) | collective-permute-done | bytes 2097184 | tf_op jit(solution)/shard_map/ppermute | solution.py:381
  164.4 10.4 %grad_mixed_rows.1 = (bf16[1024,1024]{1,0:T(8,128)(2,1)}, f32[8,2,128,128]{3,2,1,0:T(8,128)}, f32[8,128,128]{2,1,0:T(8,128)}, bf16[8,128,128]{2,1,0:T(8,128)(2,1)}) custom-call(s32[4]{0:T(128)} %fusion.21.order, f32[8,8,1024]{2,1,0:T(8,128)} %factors.1, bf16[1024,1024]{1,0:T(8,128)(2,1)} %q.7, f32[1024,1024]{1,0:T(8,128)} %early_product.3.early, ...), custom_call_target="tpu_custom_call" | custom-call | flops 1 | bytes 1 | tf_op jit(solution)/shard_map/grad_mixed_rows/pallas_call | solution.py:628
  174.9 7.0 %weight_halves.1 = (bf16[512,1024]{1,0:T(8,128)(2,1)}, bf16[512,1024]{1,0:T(8,128)(2,1)}) custom-call(s32[1]{0:T(128)} %bitcast.2.core, bf16[1024,1024]{1,0:T(8,128)(2,1)} %collective-permute-done.4.refs_0_, bf16[1024,1024]{1,0:T(8,128)(2,1)} %copy-done.1, bf16[1024,1024]{1,0:T(8,128)(2,1)} %get-tuple-element.63.refs_2_), custom_call_target="tpu_custom_call" | custom-call | flops 1 | bytes 1 | tf_op jit(solution)/shard_map/weight_halves/pallas_call | solution.py:540
  182.4 2.2 collective-permute-done.10
  189.2 2.4 add_rows.3
  195.5 12.4 %block_gradients.1 = (bf16[1024,1024]{1,0:T(8,128)(2,1)}, bf16[1024,1024]{1,0:T(8,128)(2,1)}, bf16[1024,1024]{1,0:T(8,128)(2,1)}) custom-call(f32[8,8,1024]{2,1,0:T(8,128)} %factors.1, bf16[1024,1024]{1,0:T(8,128)(2,1)} %q.7, bf16[1024,1024]{1,0:T(8,128)(2,1)} %k.7, bf16[1024,1024]{1,0:T(8,128)(2,1)} %v.7, bf16[1024,1024]{1,0:T(8,128)(2,1)} %get-tuple-element.71.e, ...), custom_call_target="tpu_custom_call" | custom-call | flops 1 | bytes 1 | tf_op jit(solution)/shard_map/block_gradients/pallas_call | solution.py:658
  209.0 2.1 collective-permute-done.16.b
  220.5 7.7 %carried_gradients.1 = (bf16[1024,1024]{1,0:T(8,128)(2,1)}, bf16[1024,1024]{1,0:T(8,128)(2,1)}) custom-call(f32[8,8,1024]{2,1,0:T(8,128)} %factors.1, bf16[1024,1024]{1,0:T(8,128)(2,1)} %k.7, bf16[1024,1024]{1,0:T(8,128)(2,1)} %v.7, bf16[1024,1024]{1,0:T(8,128)(2,1)} %get-tuple-element.83.dk_part, bf16[1024,1024]{1,0:T(8,128)(2,1)} %get-tuple-element.84.dv_part, ...), custom_call_target="tpu_custom_call" | custom-call | flops 1 | bytes 1 | tf_op jit(solution)/shard_map/carried_gradients/pallas_call | solution.py:678
  229.1 4.2 %collective-permute-done.15 = bf16[512,512]{1,0:T(8,128)(2,1)} collective-permute-done((bf16[512,512]{1,0:T(8,128)(2,1)}, bf16[512,512]{1,0:T(8,128)(2,1)}, u32[]{:S(2)}, u32[]{:S(2)}) %collective-permute-start.15) | collective-permute-done | bytes 524320 | tf_op jit(solution)/shard_map/ppermute | solution.py:426
  234.6 2.9 %fusion = f32[512,1024]{1,0:T(8,128)} fusion(f32[512,512]{1,0:T(8,128)S(1)} %convert_add_fusion, f32[512,512]{1,0:T(8,128)S(1)} %convert_add_fusion.1, bf16[512,1024]{1,0:T(8,128)(2,1)} %reduce-scatter.2.cloned.1.call-done, pred[]{:T(512)S(6)} %eq.12), kind=kLoop, calls=%fused_computation.1 | loop fusion | flops 2097152 | bytes 5242881 | tf_op jit(solution)/shard_map/add | solution.py:695
  (79 shorter events, 37.3 us)
Async XLA Ops:
  7.2 92.8 %all-gather.2.cloned.1.call-start = ((), (), s32[]{:S(2)}) async-start(), calls=%async_computation.1 | async-start | bytes 9437184 | tf_op jit(solution)/shard_map/all_gather | solution.py:453
  7.9 226.7 %reduce-scatter.2.cloned.1.call-start = ((), (), s32[]{:S(2)}) async-start(), calls=%async_computation.2 | async-start | bytes 9437184 | tf_op jit(solution)/shard_map/reduce_scatter | solution.py:623
  7.9 49.5 %collective-permute-start.1 = (bf16[1024,1024]{1,0:T(8,128)(2,1)}, bf16[1024,1024]{1,0:T(8,128)(2,1)S(1)}, u32[]{:S(2)}, u32[]{:S(2)}) collective-permute-start(bf16[1024,1024]{1,0:T(8,128)(2,1)} %refs_0_.3), channel_id=1, source_target_pairs={{2,1},{1,2},{6,5},{5,6},{10,9},{9,10},{14,13},{13,14},{18,17},{17,... | collective-permute-start | bytes 6291464 | tf_op jit(solution)/shard_map/ppermute | solution.py:381
  10.3 47.5 %collective-permute-start = (bf16[1024,1024]{1,0:T(8,128)(2,1)}, bf16[1024,1024]{1,0:T(8,128)(2,1)}, u32[]{:S(2)}, u32[]{:S(2)}) collective-permute-start(bf16[1024,1024]{1,0:T(8,128)(2,1)} %refs_0_.3), channel_id=1, source_target_pairs={{1,0},{0,1},{3,2},{2,3},{5,4},{4,5},{7,6},{6,7},{9,8},{8,9},{11,10... | collective-permute-start | bytes 6291464 | tf_op jit(solution)/shard_map/ppermute | solution.py:381
  20.8 1.8 collective-permute-start.2
  24.6 39.3 %copy-start.10 = (s32[4,4]{1,0:T(4,128)S(1)}, s32[4,4]{1,0:T(4,128)}, u32[]{:S(2)}) copy-start(s32[4,4]{1,0:T(4,128)} %constant.70.clone..sunk.2) | copy-start | bytes 196
  57.4 31.5 %copy-start = (bf16[1024,1024]{1,0:T(8,128)(2,1)}, bf16[1024,1024]{1,0:T(8,128)(2,1)S(1)}, u32[]{:S(2)}) copy-start(bf16[1024,1024]{1,0:T(8,128)(2,1)S(1)} %collective-permute-done.1.refs_0_.refs_1_) | copy-start | bytes 6291460
  57.8 52.0 %collective-permute-start.4 = (bf16[1024,1024]{1,0:T(8,128)(2,1)}, bf16[1024,1024]{1,0:T(8,128)(2,1)}, u32[]{:S(2)}, u32[]{:S(2)}) collective-permute-start(bf16[1024,1024]{1,0:T(8,128)(2,1)} %collective-permute-done.refs_1_), channel_id=1, source_target_pairs={{2,1},{1,2},{6,5},{5,6},{10,9},{9,10},{14,13},{13,14},{18,17},{17,... | collective-permute-start | bytes 6291464 | tf_op jit(solution)/shard_map/ppermute | solution.py:381
  61.3 48.5 %collective-permute-start.3 = (bf16[1024,1024]{1,0:T(8,128)(2,1)S(1)}, bf16[1024,1024]{1,0:T(8,128)(2,1)}, u32[]{:S(2)}, u32[]{:S(2)}) collective-permute-start(bf16[1024,1024]{1,0:T(8,128)(2,1)S(1)} %collective-permute-done.1.refs_0_.refs_1_), channel_id=1, source_target_pairs={{1,0},{2,3},{5,4},{6,7},{9,8},{10,11},{13,12},{14,15},{17,16},{18,... | collective-permute-start | bytes 6291464 | tf_op jit(solution)/shard_map/ppermute | solution.py:381
  64.5 10.7 %collective-permute-start.7 = (bf16[8,160,128]{2,1,0:T(8,128)(2,1)S(1)}, bf16[8,160,128]{2,1,0:T(8,128)(2,1)S(1)}, u32[]{:S(2)}, u32[]{:S(2)}) collective-permute-start(bf16[8,160,128]{2,1,0:T(8,128)(2,1)S(1)} %pad_maximum_fusion), channel_id=1, source_target_pairs={{0,8},{4,12},{8,0},{12,4},{16,24},{20,28},{24,16},{28,20},{1,9},{5... | collective-permute-start | bytes 983048 | tf_op jit(solution)/shard_map/ppermute | solution.py:285
  66.0 14.6 %collective-permute-start.6 = (bf16[8,160,128]{2,1,0:T(8,128)(2,1)S(1)}, bf16[8,160,128]{2,1,0:T(8,128)(2,1)S(1)}, u32[]{:S(2)}, u32[]{:S(2)}) collective-permute-start(bf16[8,160,128]{2,1,0:T(8,128)(2,1)S(1)} %pad_maximum_fusion), channel_id=1, source_target_pairs={{0,24},{4,28},{8,16},{12,20},{16,8},{20,12},{24,0},{28,4},{1,25},{... | collective-permute-start | bytes 983048 | tf_op jit(solution)/shard_map/ppermute | solution.py:285
  67.5 14.4 %collective-permute-start.5 = (bf16[8,160,128]{2,1,0:T(8,128)(2,1)S(1)}, bf16[8,160,128]{2,1,0:T(8,128)(2,1)S(1)}, u32[]{:S(2)}, u32[]{:S(2)}) collective-permute-start(bf16[8,160,128]{2,1,0:T(8,128)(2,1)S(1)} %pad_maximum_fusion), channel_id=1, source_target_pairs={{0,16},{4,20},{8,24},{12,28},{16,0},{20,4},{24,8},{28,12},{1,17},{... | collective-permute-start | bytes 983048 | tf_op jit(solution)/shard_map/ppermute | solution.py:285
  118.8 44.3 %collective-permute-start.8 = (bf16[1024,1024]{1,0:T(8,128)(2,1)}, bf16[1024,1024]{1,0:T(8,128)(2,1)S(1)}, u32[]{:S(2)}, u32[]{:S(2)}) collective-permute-start(bf16[1024,1024]{1,0:T(8,128)(2,1)} %collective-permute-done.4.refs_0_), channel_id=1, source_target_pairs={{1,0},{2,3},{5,4},{6,7},{9,8},{10,11},{13,12},{14,15},{17,16},{18,... | collective-permute-start | bytes 6291464 | tf_op jit(solution)/shard_map/ppermute | solution.py:381
  181.9 6.3 %collective-permute-start.9 = (bf16[512,1024]{1,0:T(8,128)(2,1)}, bf16[512,1024]{1,0:T(8,128)(2,1)S(1)}, u32[]{:S(2)}, u32[]{:S(2)}) collective-permute-start(bf16[512,1024]{1,0:T(8,128)(2,1)} %get-tuple-element.74), channel_id=1, source_target_pairs={{0,4},{4,0},{8,12},{12,8},{16,20},{20,16},{24,28},{28,24},{1,5},{5... | collective-permute-start | bytes 3145736 | tf_op jit(solution)/shard_map/ppermute | solution.py:584
  181.9 2.7 %collective-permute-start.10 = (bf16[8,128,128]{2,1,0:T(8,128)(2,1)S(1)}, bf16[8,128,128]{2,1,0:T(8,128)(2,1)S(1)}, u32[]{:S(2)}, u32[]{:S(2)}) collective-permute-start(bf16[8,128,128]{2,1,0:T(8,128)(2,1)S(1)} %copy-done.11), channel_id=1, source_target_pairs={{0,4},{4,0},{8,12},{12,8},{16,20},{20,16},{24,28},{28,24},{1,5},{5... | collective-permute-start | bytes 786440 | tf_op jit(solution)/shard_map/ppermute | solution.py:285
  184.7 23.3 %collective-permute-start.12 = (bf16[8,128,128]{2,1,0:T(8,128)(2,1)S(1)}, bf16[8,128,128]{2,1,0:T(8,128)(2,1)S(1)}, u32[]{:S(2)}, u32[]{:S(2)}) collective-permute-start(bf16[8,128,128]{2,1,0:T(8,128)(2,1)S(1)} %fusion.3), channel_id=1, source_target_pairs={{0,16},{4,20},{8,24},{12,28},{16,0},{20,4},{24,8},{28,12},{1,17},{... | collective-permute-start | bytes 786440 | tf_op jit(solution)/shard_map/ppermute | solution.py:285
  186.0 22.0 %collective-permute-start.11 = (bf16[8,128,128]{2,1,0:T(8,128)(2,1)S(1)}, bf16[8,128,128]{2,1,0:T(8,128)(2,1)S(1)}, u32[]{:S(2)}, u32[]{:S(2)}) collective-permute-start(bf16[8,128,128]{2,1,0:T(8,128)(2,1)S(1)} %fusion.3), channel_id=1, source_target_pairs={{0,8},{4,12},{8,0},{12,4},{16,24},{20,28},{24,16},{28,20},{1,9},{5... | collective-permute-start | bytes 786440 | tf_op jit(solution)/shard_map/ppermute | solution.py:285
  187.5 20.5 %collective-permute-start.13 = (bf16[8,128,128]{2,1,0:T(8,128)(2,1)S(1)}, bf16[8,128,128]{2,1,0:T(8,128)(2,1)S(1)}, u32[]{:S(2)}, u32[]{:S(2)}) collective-permute-start(bf16[8,128,128]{2,1,0:T(8,128)(2,1)S(1)} %fusion.3), channel_id=1, source_target_pairs={{0,24},{4,28},{8,16},{12,20},{16,8},{20,12},{24,0},{28,4},{1,25},{... | collective-permute-start | bytes 786440 | tf_op jit(solution)/shard_map/ppermute | solution.py:285
  192.9 15.1 %copy-start.2 = (bf16[512,512]{1,0:T(8,128)(2,1)}, bf16[512,512]{1,0:T(8,128)(2,1)S(1)}, u32[]{:S(2)}) copy-start(bf16[512,512]{1,0:T(8,128)(2,1)S(1)} %get-tuple-element.124.a) | copy-start | bytes 1572868
  192.9 15.1 %copy-start.3 = (bf16[512,512]{1,0:T(8,128)(2,1)}, bf16[512,512]{1,0:T(8,128)(2,1)S(1)}, u32[]{:S(2)}) copy-start(bf16[512,512]{1,0:T(8,128)(2,1)S(1)} %get-tuple-element.123.a) | copy-start | bytes 1572868
  192.9 18.2 %collective-permute-start.16 = (bf16[512,512]{1,0:T(8,128)(2,1)S(1)}, bf16[512,512]{1,0:T(8,128)(2,1)S(1)}, u32[]{:S(2)}, u32[]{:S(2)}) collective-permute-start(bf16[512,512]{1,0:T(8,128)(2,1)S(1)} %get-tuple-element.123.a), channel_id=1, source_target_pairs={{0,8},{1,9},{4,12},{5,13},{10,2},{11,3},{14,6},{15,7},{16,24},{17,... | collective-permute-start | bytes 1572872 | tf_op jit(solution)/shard_map/ppermute | solution.py:426
  194.2 21.0 %collective-permute-start.14 = (bf16[512,512]{1,0:T(8,128)(2,1)S(1)}, bf16[512,512]{1,0:T(8,128)(2,1)S(1)}, u32[]{:S(2)}, u32[]{:S(2)}) collective-permute-start(bf16[512,512]{1,0:T(8,128)(2,1)S(1)} %get-tuple-element.124.a), channel_id=1, source_target_pairs={{0,16},{1,17},{4,20},{5,21},{8,24},{9,25},{12,28},{13,29},{18,2},{... | collective-permute-start | bytes 1572872 | tf_op jit(solution)/shard_map/ppermute | solution.py:426
  213.9 15.2 %collective-permute-start.17 = (bf16[512,512]{1,0:T(8,128)(2,1)}, bf16[512,512]{1,0:T(8,128)(2,1)S(1)}, u32[]{:S(2)}, u32[]{:S(2)}) collective-permute-start(bf16[512,512]{1,0:T(8,128)(2,1)} %add_rows.5), channel_id=1, source_target_pairs={{8,24},{9,25},{12,28},{13,29},{18,2},{19,3},{22,6},{23,7}} | collective-permute-start | bytes 1572872 | tf_op jit(solution)/shard_map/ppermute | solution.py:426
  218.0 15.3 %collective-permute-start.15 = (bf16[512,512]{1,0:T(8,128)(2,1)}, bf16[512,512]{1,0:T(8,128)(2,1)}, u32[]{:S(2)}, u32[]{:S(2)}) collective-permute-start(bf16[512,512]{1,0:T(8,128)(2,1)} %add_rows.4), channel_id=1, source_target_pairs={{10,2},{11,3},{14,6},{15,7},{16,24},{17,25},{20,28},{21,29}} | collective-permute-start | bytes 1572872 | tf_op jit(solution)/shard_map/ppermute | solution.py:426
  (8 other events, 38.5 us)
Sparse Core Ops, SparseCore 0:
  9.9 55.4 all-gather.1
  118.9 70.3 reduce-scatter.1

commit v3 on v2

--- a/solution.py
+++ b/solution.py
@@ -84,8 +84,15 @@
         pack_decay(sent, h, jnp.broadcast_to(decay, (1, DK)))
 
 
-def add_kernel(a, b, out):
-    out[...] = (a[...].astype(F32) + b[...].astype(F32)).astype(BF16)
+def cut_kernel(rows, out):
+    out[...] = rows[...]
+
+
+def add_kernel(*refs):
+    many = len(refs) // 3
+    for n in range(many):
+        total = refs[n][...].astype(F32) + refs[many + n][...].astype(F32)
+        refs[2 * many + n][...] = total.astype(BF16)
 
 
 def total_block(refs):
@@ -93,19 +100,6 @@
     for other in refs[1:]:
         block = block + other[...]
     return block
-
-
-def halves_kernel(core, *refs):
-    *inputs, mixed, sent, kept = refs
-    total = dot(total_block(inputs), mixed[...], 0, 0).astype(BF16)
-
-    @pl.when(pl.program_id(0) == 0)
-    def _():
-        sent[...] = total
-
-    @pl.when(pl.program_id(0) == 1)
-    def _():
-        kept[...] = total
 
 
 def rows_kernel(counts, order, *refs):
@@ -190,22 +184,20 @@
 
 
 def grad_kernel(counts, order, factors, q, early, *refs):
-    *blocks, weight, e, parts, local, sent = refs
+    *blocks, weight, later, e, parts, local, sent = refs
     e[...] = (early[...] + block_products(counts, lambda n: weight[...], blocks)).astype(BF16)
     for h in range(parts.shape[0]):
         col, lanes = columns(factors, h), lanes_of(h)
-        state = jnp.zeros((DK, DK), F32)
-        for b in reversed(range(parts.shape[1])):
-            at, end = b * BLK, (b + 1) * BLK
-            scaled = (q[at:end, lanes].astype(F32) * col[at:end, 2:3]).astype(BF16)
-            part = dot(scaled, e[at:end, lanes], 0, 0)
-            parts[h, b] = part
-            state = state * col[end - 1 : end, 2:3] + part
+        scaled = (q[:, lanes].astype(F32) * col[:, 2:3]).astype(BF16)
+        part = dot(scaled, e[:, lanes], 0, 0)
+        parts[h] = part
+        state = later[h] * col[BLK - 1 : BLK, 2:3] + part
         local[h] = state
         sent[h] = state.astype(BF16)
 
 
-def back_kernel(factors, q, k, v, e, weights, states, dq, dk, dv):
+def back_kernel(factors, q, k, v, e, weights, states, *refs):
+    dq, dk, dv = refs[-3:]
     half = BLK // 2
     for h in range(weights.shape[0]):
         col, lanes = columns(factors, h), lanes_of(h)
@@ -223,11 +215,12 @@
         dv[half:BLK, lanes] = dot(tail, e[half:BLK, lanes], 0, 0).astype(BF16)
 
 
-def finish_kernel(factors, k, v, dk_part, dv_part, parts, finish, dk, dv):
+def finish_kernel(factors, k, v, dk_part, dv_part, finish, *refs):
+    *parts, dk, dv = refs
     for h in range(finish.shape[0]):
         col, lanes = columns(factors, h), lanes_of(h)
         state = finish[h]
-        for b in reversed(range(parts.shape[1])):
+        for b in reversed(range(len(parts))):
             at, end = b * BLK, (b + 1) * BLK
             small = state.astype(BF16)
             factor = col[at:end, 1:2]
@@ -235,7 +228,7 @@
             dk[at:end, lanes] = (dk_part[at:end, lanes].astype(F32) + more).astype(BF16)
             more = factor * dot(k[at:end, lanes], small)
             dv[at:end, lanes] = (dv_part[at:end, lanes].astype(F32) + more).astype(BF16)
-            state = state * col[end - 1 : end, 2:3] + parts[h, b]
+            state = state * col[end - 1 : end, 2:3] + parts[b][h]
 
 
 def log2_of(count):
@@ -365,44 +358,85 @@
 
 
 class Line:
-    def __init__(self, own, order):
+    def __init__(self, own, order, spans):
         self.plan, self.held = line_plan(order)
         self.raw = {(0, 0, 0): own}
-        self.sent = 0
+        self.sent, self.spans = 0, spans
+        size = len(order)
+        self.cut = {name for name in self.plan if name[0] == size - 1}
+
+    def permute(self, name, value):
+        return lax.ppermute(value, "head", self.plan[name])
+
+    def operand(self, name):
+        held = self.held[name]
+        some = min(held.values())
+        by_plane = [held.get(p, some) for p in range(lax.axis_size("head"))]
+        return pick(by_plane, lambda key: self.raw[key])
 
     def send(self, *after):
         self.sent += 1
         for name in sorted(self.plan):
-            if name[0] == self.sent:
-                held = self.held[name]
-                some = min(held.values())
-                by_plane = [held.get(p, some) for p in range(lax.axis_size("head"))]
-                value = tie(pick(by_plane, lambda key: self.raw[key]), *after)
-                self.raw[name] = lax.ppermute(value, "head", self.plan[name])
+            if name[0] != self.sent:
+                continue
+            self.raw[name] = self.permute(name, tie(self.operand(name), *after))
 
     def close(self, *after):
-        names = [name for name in sorted(self.plan) if name[0] == self.sent]
-        tied = lax.optimization_barrier(tuple(self.raw[name] for name in names) + after)
-        self.raw.update(zip(names, tied))
+        keys = [k for k in self.raw if (k if len(k) == 3 else k[0])[0] == self.sent]
+        tied = lax.optimization_barrier(tuple(self.raw[key] for key in keys) + after)
+        self.raw.update(zip(keys, tied))
         return tied[0]
 
+    def send_rows(self, n, ready, *after):
+        for name in sorted(self.plan):
+            if name[0] == self.sent + 1:
+                (held,) = set(self.held[name].values())
+                start, end = self.spans[n]
+                value = tie(self.raw[held], ready)
+                out = jax.ShapeDtypeStruct((end - start, value.shape[1]), BF16)
+                part = pl.pallas_call(
+                    cut_kernel,
+                    grid=(2,),
+                    in_specs=[
+                        pl.BlockSpec(
+                            ((end - start) // 2, value.shape[1]),
+                            lambda i, at=start // (end - start): (2 * at + i, 0),
+                        )
+                    ],
+                    out_specs=pl.BlockSpec(((end - start) // 2, value.shape[1]), lambda i: (i, 0)),
+                    out_shape=out,
+                    compiler_params=PARAMS,
+                    cost_estimate=LIGHT,
+                    name="cut_rows",
+                )(value)
+                self.raw[name, n] = self.permute(name, tie(part, *after))
+
+    def newest(self, s):
+        return max(name for name in self.plan if name[1] == s)
+
     def slot(self, s):
-        return [self.raw[name] for name in sorted(self.raw) if name[1] == s]
-
-
-def add(a, b):
-    rows, width = a.shape
+        return [self.raw[key] for key in sorted(k for k in self.raw if len(k) == 3) if key[1] == s]
+
+    def last(self, n, *after):
+        at = self.spans[n][0] // (self.spans[n][1] - self.spans[n][0])
+        whole = [(x, at) for x in self.slot(max(name[1] for name in self.plan))]
+        cut = [self.raw[name, n] for name in sorted(self.cut)]
+        return whole + [(tie(x, *after), 0) for x in cut]
+
+
+def add(these, those):
+    rows, width = these[0].shape
     spec = pl.BlockSpec((rows // 2, width), lambda n: (n, 0))
     return pl.pallas_call(
         add_kernel,
         grid=(2,),
-        in_specs=[spec, spec],
-        out_specs=spec,
-        out_shape=jax.ShapeDtypeStruct(a.shape, BF16),
+        in_specs=[spec] * (2 * len(these)),
+        out_specs=[spec] * len(these),
+        out_shape=[jax.ShapeDtypeStruct(x.shape, BF16) for x in these],
         compiler_params=PARAMS,
         cost_estimate=LIGHT,
         name="add_rows",
-    )(a, b)
+    )(*these, *those)
 
 
 class Tree:
@@ -428,7 +462,7 @@
 
     def take(self, *after):
         got = [tie(x, *after) for x in self.got]
-        self.now = [add(x, y) for x, y in zip(self.now, got)]
+        self.now = add(self.now, got)
         self.turn += 1
         self.got = None
 
@@ -448,7 +482,8 @@
     order = block_order(size)
     assert group == 2
 
-    line = Line(grad_out, order)
+    spans = [(b * BLK, (b + 1) * BLK) for b in reversed(range(blocks))]
+    line = Line(grad_out, order, spans)
     line.send()
     full_weight = lax.all_gather(out_weight, "tm", axis=0, tiled=True)
 
@@ -529,30 +564,8 @@
     def targets(s):
         return [order[p][s] for p in range(size)]
 
-    core = (place % 2).astype(jnp.int32)[None]
-
     sub = grad_out.shape[1] // 4
     whole_mixed = pl.BlockSpec((tok, width), lambda k, i, o: (0, 0))
-
-    def halves_of(arrays, *after):
-        block = pl.BlockSpec((tok, sub), lambda k, i, o: (0, 2 * (o[0] ^ (1 - k)) + i))
-        out = shape((2 * sub, width), BF16)
-        return pl.pallas_call(
-            halves_kernel,
-            grid_spec=pltpu.PrefetchScalarGridSpec(
-                num_scalar_prefetch=1,
-                grid=(2, 2),
-                in_specs=[block] * len(arrays) + [whole_mixed],
-                out_specs=[
-                    pl.BlockSpec((sub, width), lambda k, i, o: (jnp.where(k == 0, i, 1), 0)),
-                    pl.BlockSpec((sub, width), lambda k, i, o: (jnp.where(k == 0, 0, i), 0)),
-                ],
-            ),
-            out_shape=[out, out],
-            compiler_params=PARAMS,
-            cost_estimate=LIGHT,
-            name="weight_halves",
-        )(tie(core, *after), *arrays, mixed)
 
     def rows_of(slots, held, *after):
         arrays, specs, counts = [], [], []
@@ -584,9 +597,9 @@
         return lax.ppermute(tie(sent, *after), "tm", [(i, i ^ 1) for i in range(count)])
 
     def joined(kept, got, *after):
-        return add(kept, tie(got, *after))
-
-    two = 2 if heads % 2 == 0 else 1
+        return add([kept], [tie(got, *after)])[0]
+
+    two = many
     cover = two * DK
     wide = pl.BlockSpec((tok, cover), lambda n, o: (0, n))
     depth = grad_out.shape[1]
@@ -612,64 +625,97 @@
         )(tie(mine, *after), *held, *arrays, *[full_weight] * len(slots))
 
     slots = list(range(min(2, size - 1)))
-    products = rows_of(slots, None)
-    early = accumulate(None, slots, products)
+    def product_of(arrays, *after):
+        block = tie(functools.reduce(jnp.add, arrays), *after)
+        return dot(block, mixed, 0, 0).astype(BF16)
+
+    products = rows_of(slots + [size - 1], None)
+    ready = products
     for s in range(2, size - 1):
-        mark = line.close(early)
-        line.send(mark)
-        final = [size - 1] if s == size - 2 else []
-        products = rows_of([s] + final, products, mark)
-        early = accumulate(early, [s], products)
+        newest = line.raw[line.newest(s)]
+        part = product_of([x for x in line.slot(s) if x is not newest], ready)
+        mark = line.close(part)
+        if s < size - 2:
+            line.send(mark)
+        else:
+            line.send_rows(0, mark, mark)
+        product = part + product_of([line.raw[line.newest(s)]], mark)
+        ready = products = lax.dynamic_update_slice(products, product, (mine[s] * depth, 0))
     most = lax.psum_scatter(products, "tm", scatter_dimension=0, tiled=True)
-    mark = line.close(early)
-
-    whole = line.slot(size - 1)
+    early = accumulate(None, range(size - 1), products)
+    later = jnp.zeros((heads, DK, DK), F32)
     pair_state = pl.BlockSpec((two, DK, DK), lambda n, o: (n, 0, 0))
-    e, parts, local, sent = pl.pallas_call(
-        functools.partial(grad_kernel, [len(whole)]),
-        grid_spec=pltpu.PrefetchScalarGridSpec(
-            num_scalar_prefetch=1,
-            grid=(width // cover,),
-            in_specs=[pl.BlockSpec((two, 8, tok), lambda n, o: (n, 0, 0)), wide, wide]
-            + [pl.BlockSpec(x.shape, lambda n, o: (0, 0)) for x in whole]
-            + [pl.BlockSpec((depth, cover), lambda n, o: (o[size - 1], n))],
-            out_specs=[
-                wide,
-                pl.BlockSpec((two, blocks, DK, DK), lambda n, o: (n, 0, 0, 0)),
-                pair_state,
-                pair_state,
-            ],
-        ),
-        out_shape=[rows_bf16, states_f32, state_f32, shape((heads, DK, DK), BF16)],
-        compiler_params=PARAMS,
-        cost_estimate=LIGHT,
-        name="grad_mixed_rows",
-    )(mine, factors, query, early, *whole, full_weight)
-    back = Scan(local, fwd_own[:, :1], sent, True, scan.known)
-    back.send_pair()
-    sent, kept = halves_of(whole, e)
-    got = swap(sent)
-    back.take_pair(kept)
-    back.send_all()
-    held = joined(kept, got, back.pair)
-    last_tree = Tree(held, targets(size - 1), [group_bits[::-1], group_bits])
-    last_tree.send()
-    own_rows = pl.BlockSpec((BLK, many * DK), lambda h, b: (b, h))
-    dq, dk_part, dv_part = pl.pallas_call(
-        back_kernel,
-        grid=(heads // many, blocks),
-        in_specs=[pl.BlockSpec((many, 8, BLK), lambda h, b: (h, 0, b))]
-        + [own_rows] * 4
-        + [
-            pl.BlockSpec((many, 1, weight_rows, half), lambda h, b: (h, b, 0, 0)),
-            pl.BlockSpec((many, 1, DK, DK), lambda h, b: (h, b, 0, 0)),
-        ],
-        out_specs=[own_rows] * 3,
-        out_shape=[rows_bf16] * 3,
-        compiler_params=PARAMS,
-        cost_estimate=LIGHT,
-        name="block_gradients",
-    )(tie(factors, held), query, key, value, e, weights, states)
+    after, filled = [early], []
+    e, parts = {}, {}
+    for n, (start, end) in enumerate(spans):
+        b = start // BLK
+        arrays = line.last(n, *after)
+        if n + 1 < blocks:
+            line.send_rows(n + 1, early, arrays[-1][0])
+        block = functools.reduce(jnp.add, [x[t * BLK : (t + 1) * BLK] for x, t in arrays])
+        queue = mine
+        if b == 0:
+            product = product + dot(block, mixed[start:end], 0, 0)
+            product = product.astype(BF16).reshape(2, -1, width)
+            first, second = product[0], product[1]
+            upper = place % 2 == 1
+            got = swap(jnp.where(upper, first, second))
+            kept = jnp.where(upper, second, first)
+            queue = tie(mine, kept)
+        e[b], parts[b], later, sent = pl.pallas_call(
+            functools.partial(grad_kernel, [len(arrays)]),
+            grid_spec=pltpu.PrefetchScalarGridSpec(
+                num_scalar_prefetch=1,
+                grid=(width // cover,),
+                in_specs=[
+                    pl.BlockSpec((two, 8, BLK), lambda n, o, b=b: (n, 0, b)),
+                    pl.BlockSpec((BLK, cover), lambda n, o, b=b: (b, n)),
+                    pl.BlockSpec((BLK, cover), lambda n, o, b=b: (b, n)),
+                ]
+                + [pl.BlockSpec((BLK, depth), lambda n, o, at=at: (at, 0)) for _, at in arrays]
+                + [pl.BlockSpec((depth, cover), lambda n, o: (o[size - 1], n)), pair_state],
+                out_specs=[pl.BlockSpec((BLK, cover), lambda n, o: (0, n))] + [pair_state] * 3,
+            ),
+            out_shape=[shape((BLK, width), BF16), state_f32, state_f32, shape((heads, DK, DK), BF16)],
+            compiler_params=PARAMS,
+            cost_estimate=LIGHT,
+            name="grad_mixed_rows",
+        )(queue, factors, query, early, *[x for x, _ in arrays], full_weight, later)
+        if b == 0:
+            back = Scan(later, fwd_own[:, :1], sent, True, scan.known)
+            back.send_pair()
+        order_after = e[b]
+        if b:
+            part = dot(tie(block, e[b]), mixed[start:end], 0, 0)
+            product = part if n == 0 else product + part
+            order_after = product
+        else:
+            held = joined(kept, got, e[b])
+            last_tree = Tree(held, targets(size - 1), [group_bits[::-1], group_bits])
+            last_tree.send()
+            order_after = back.take_pair(held)
+            back.send_all()
+        own_rows = pl.BlockSpec((BLK, many * DK), lambda h, b=b: (b, h))
+        filled = pl.pallas_call(
+            back_kernel,
+            grid=(heads // many,),
+            in_specs=[pl.BlockSpec((many, 8, BLK), lambda h, b=b: (h, 0, b))]
+            + [own_rows] * 3
+            + [
+                pl.BlockSpec((BLK, many * DK), lambda h: (0, h)),
+                pl.BlockSpec((many, 1, weight_rows, half), lambda h, b=b: (h, b, 0, 0)),
+                pl.BlockSpec((many, 1, DK, DK), lambda h, b=b: (h, b, 0, 0)),
+            ]
+            + [pl.BlockSpec(memory_space=pl.ANY)] * len(filled),
+            out_specs=[own_rows] * 3,
+            out_shape=[rows_bf16] * 3,
+            input_output_aliases={7 + m: m for m in range(len(filled))},
+            compiler_params=PARAMS,
+            cost_estimate=LIGHT,
+            name="block_gradients",
+        )(tie(factors, order_after), query, key, value, e[b], weights, states, *filled)
+        after = [filled[0], product]
+    dq, dk_part, dv_part = filled
     grad_in = back.take_all(dq)
     for _ in group_bits[1:]:
         last_tree.take(grad_in)
@@ -680,16 +726,21 @@
         grid=(heads // two,),
         in_specs=[pl.BlockSpec((two, 8, tok), lambda n: (n, 0, 0))]
         + [pair_rows] * 4
-        + [
-            pl.BlockSpec((two, blocks, DK, DK), lambda n: (n, 0, 0, 0)),
-            pl.BlockSpec((two, DK, DK), lambda n: (n, 0, 0)),
-        ],
+        + [pl.BlockSpec((two, DK, DK), lambda n: (n, 0, 0))] * (1 + blocks),
         out_specs=[pair_rows] * 2,
         out_shape=[rows_bf16] * 2,
         compiler_params=PARAMS,
         cost_estimate=LIGHT,
         name="carried_gradients",
-    )(factors, key, value, dk_part, dv_part, parts, tie(grad_in, last_tree.now[0]))
+    )(
+        factors,
+        key,
+        value,
+        dk_part,
+        dv_part,
+        tie(grad_in, last_tree.now[0]),
+        *[parts[b] for b in range(blocks)],
+    )
     done = [x.astype(F32) + tie(y, dk).astype(F32) for x, y in zip(last_tree.now, last_tree.got)]
     done = jnp.concatenate(done, axis=1)
     grad_weight = most.astype(F32) + jnp.where(mine[size - 1] == place // group, done, 0.0)

time: 248 us -> 241 us (0.972)
  waiting for transfers between devices: 82 us -> 54.8 us
  matrix products: 0 us -> 18.1 us
  starting transfers between devices: 23 us -> 32.3 us
  Pallas kernels: 108 us -> 98.9 us
  other arithmetic: 8.93 us -> 11.7 us
    ppermute x5 -> x6, waiting for transfers between devices: 56.8 us -> 23.9 us  [permute(): return lax.ppermute(value, 'head', self.plan[name])]
    dot_general x0 -> x4, matrix products: none -> 18.1 us  [dot(): lax.dot_general(a, b, (((da,), (db,)), ((), ())), preferred_element_type=...]
    ppermute x5 -> x6, starting transfers between devices: 10.1 us -> 19.5 us  [permute(): return lax.ppermute(value, 'head', self.plan[name])]
    ppermute x4, waiting for transfers between devices: 7.14 us -> 15.5 us  [send(): lax.ppermute(tie(self.now[n], *after), ('tm', 'head'), perm)]
    pallas_call x2 -> x1, Pallas kernels: 20 us -> 12.7 us  [rows_of(): pl.pallas_call(functools.partial(rows_kernel, counts), grid_spec=pltpu.Pr...]
    pallas_call x2 -> x1, Pallas kernels: 19 us -> 15.8 us  [accumulate(): pl.pallas_call(functools.partial(early_kernel, [len(x) for x in inputs]),...]
    ppermute x8, waiting for transfers between devices: 17.3 us -> 14.6 us  [permute(): return lax.ppermute(value, 'tm', [(i, i ^ mask) for i in range(count)])]
    pallas_call x6 -> x8, Pallas kernels: 36.2 us -> 38.6 us  [the longest x2 15.2 us: per_device(): pl.pallas_call(back_kernel, grid=(heads // many,), in_specs=[pl.BlockSpec...]
  transfers between devices with their start and end apart: 20 -> 21, of which waited for: 11 -> 13; matrix products, arithmetic and copies ran while one was open for 4% -> 13% of each run, Pallas kernels for 40% -> 41%
where the time goes in v3:
time: 241 us; the launch traced here: 240 us
  Pallas kernels  98.9 us (41%)
  waiting for transfers between devices  54.8 us (23%)
  starting transfers between devices  32.3 us (13%)
  matrix products  18.1 us (8%)
  between operations  15.6 us (6%)
  other arithmetic  11.7 us (5%)
  local copies, waits for them, and re-layouts  8.45 us (4%)
    ppermute x6, waiting for transfers between devices, permute(): return lax.ppermute(value, 'head', self.plan[name])  23.9 us
    ppermute x6, starting transfers between devices, permute(): return lax.ppermute(value, 'head', self.plan[name])  19.5 us
    dot_general x4, matrix products, dot(): lax.dot_general(a, b, (((da,), (db,)), ((), ())), preferred_element_type=...  18.1 us
    pallas_call x1, Pallas kernels, accumulate(): pl.pallas_call(functools.partial(early_kernel, [len(x) for x in inputs]),...  15.8 us
    ppermute x4, waiting for transfers between devices, send(): lax.ppermute(tie(self.now[n], *after), ('tm', 'head'), perm)  15.5 us
    pallas_call x2, Pallas kernels, per_device(): pl.pallas_call(back_kernel, grid=(heads // many,), in_specs=[pl.BlockSpec...  15.2 us
    ppermute x8, waiting for transfers between devices, permute(): return lax.ppermute(value, 'tm', [(i, i ^ mask) for i in range(count)])  14.6 us
    pallas_call x2, Pallas kernels, per_device(): pl.pallas_call(functools.partial(grad_kernel, [len(arrays)]), grid_spec=p...  14.4 us
  transfers between devices with their start and end apart: 21, of which 13 were waited for; matrix products, arithmetic and copies ran while one was open for 13% of the time, Pallas kernels for 41%

profile of v3, /device:TPU:16, one launch (start us, length us, event | category | flops | bytes accessed | tf_op | source)
XLA Modules:
  0.0 239.8 jit_solution(6494266579484627667)
XLA Ops:
  15.4 6.6 %block_states.1 = (f32[8,2,128,128]{3,2,1,0:T(8,128)}, f32[8,128,128]{2,1,0:T(8,128)}, f32[8,8,128]{2,1,0:T(8,128)}, bf16[8,160,128]{2,1,0:T(8,128)(2,1)}) custom-call(f32[8,8,1024]{2,1,0:T(8,128)} %factors.1, bf16[1024,1024]{1,0:T(8,128)(2,1)} %k.9, bf16[1024,1024]{1,0:T(8,128)(2,1)} %v.9), custom_call_target="tpu_custom_call" | custom-call | flops 1 | bytes 1 | tf_op jit(solution)/shard_map/block_states/pallas_call | solution.py:519
  25.8 9.9 %pair_weights.1 = (bf16[8,2,768,256]{3,2,1,0:T(8,128)(2,1)}, f32[1024,1024]{1,0:T(8,128)}) custom-call(f32[8,8,1024]{2,1,0:T(8,128)} %factors.1, bf16[1024,1024]{1,0:T(8,128)(2,1)} %q.11, bf16[1024,1024]{1,0:T(8,128)(2,1)} %k.9, bf16[1024,1024]{1,0:T(8,128)(2,1)} %v.9), custom_call_target="tpu_custom_call" | custom-call | flops 1 | bytes 1 | tf_op jit(solution)/shard_map/pair_weights/pallas_call | solution.py:538
  35.7 21.8 %collective-permute-done.1.refs_2_ = bf16[1024,1024]{1,0:T(8,128)(2,1)} collective-permute-done((bf16[1024,1024]{1,0:T(8,128)(2,1)}, bf16[1024,1024]{1,0:T(8,128)(2,1)}, u32[]{:S(2)}, u32[]{:S(2)}) %collective-permute-start.1) | collective-permute-done | bytes 2097184 | tf_op jit(solution)/shard_map/ppermute | solution.py:369
  59.0 3.5 %collective-permute-start.4 = (bf16[1024,1024]{1,0:T(8,128)(2,1)}, bf16[1024,1024]{1,0:T(8,128)(2,1)S(1)}, u32[]{:S(2)}, u32[]{:S(2)}) collective-permute-start(bf16[1024,1024]{1,0:T(8,128)(2,1)} %copy-done.2), channel_id=1, source_target_pairs={{2,1},{1,2},{6,5},{5,6},{10,9},{9,10},{14,13},{13,14},{18,17},{17,... | collective-permute-start | bytes 6291464 | tf_op jit(solution)/shard_map/ppermute | solution.py:369
  62.5 2.6 %collective-permute-start.3 = (bf16[1024,1024]{1,0:T(8,128)(2,1)}, bf16[1024,1024]{1,0:T(8,128)(2,1)}, u32[]{:S(2)}, u32[]{:S(2)}) collective-permute-start(bf16[1024,1024]{1,0:T(8,128)(2,1)} %collective-permute-done.1.refs_2_), channel_id=1, source_target_pairs={{1,0},{2,3},{5,4},{6,7},{9,8},{10,11},{13,12},{14,15},{17,16},{18,... | collective-permute-start | bytes 6291464 | tf_op jit(solution)/shard_map/ppermute | solution.py:369
  69.9 6.0 %collective-permute-done.7 = bf16[8,160,128]{2,1,0:T(8,128)(2,1)S(1)} collective-permute-done((bf16[8,160,128]{2,1,0:T(8,128)(2,1)S(1)}, bf16[8,160,128]{2,1,0:T(8,128)(2,1)S(1)}, u32[]{:S(2)}, u32[]{:S(2)}) %collective-permute-start.7) | collective-permute-done | bytes 327712 | tf_op jit(solution)/shard_map/ppermute | solution.py:278
  75.8 5.5 %collective-permute-done.6 = bf16[8,160,128]{2,1,0:T(8,128)(2,1)S(1)} collective-permute-done((bf16[8,160,128]{2,1,0:T(8,128)(2,1)S(1)}, bf16[8,160,128]{2,1,0:T(8,128)(2,1)S(1)}, u32[]{:S(2)}, u32[]{:S(2)}) %collective-permute-start.6) | collective-permute-done | bytes 327712 | tf_op jit(solution)/shard_map/ppermute | solution.py:278
  83.8 5.9 %mixed_rows.1 = (bf16[1024,1024]{1,0:T(8,128)(2,1)}, bf16[8,2,128,128]{3,2,1,0:T(8,128)(2,1)}) custom-call(f32[8,8,1024]{2,1,0:T(8,128)} %factors.1, bf16[1024,1024]{1,0:T(8,128)(2,1)} %q.11, f32[1024,1024]{1,0:T(8,128)} %get-tuple-element.66.within, f32[8,2,128,128]{3,2,1,0:T(8,128)} %get-tuple-element.71.parts, f32[8,128,128]{2,1,0:T(8,128)} %fusion.7.start), custom_call_target="tpu_custom_call" | custom-call | flops 1 | bytes 1 | tf_op jit(solution)/shard_map/mixed_rows/pallas_call | solution.py:551
  89.8 12.7 %weight_rows.1 = bf16[4096,1024]{1,0:T(8,128)(2,1)} custom-call(s32[3]{0:T(128)} %pad_add_fusion.order, bf16[1024,1024]{1,0:T(8,128)(2,1)} %refs_0_.3, bf16[1024,1024]{1,0:T(8,128)(2,1)} %copy-done.2, bf16[1024,1024]{1,0:T(8,128)(2,1)} %get-tuple-element.75.refs_2_), custom_call_target="tpu_custom_call" | custom-call | flops 1 | bytes 1 | tf_op jit(solution)/shard_map/weight_rows/pallas_call | solution.py:581
  102.5 4.8 %convolution_convert_fusion = bf16[1024,1024]{1,0:T(8,128)(2,1)S(1)} fusion(bf16[1024,1024]{1,0:T(8,128)(2,1)} %collective-permute-done.1.refs_2_, bf16[1024,1024]{1,0:T(8,128)(2,1)} %get-tuple-element.75.refs_2_), kind=kOutput, calls=%fused_computation.4 | convolution fusion | flops 2148532224 | bytes 6291456 | tf_op jit(solution)/shard_map/dot_general | solution.py:21
  107.9 5.8 %add_dynamic-update-slice_fusion = bf16[4096,1024]{1,0:T(8,128)(2,1)} fusion(bf16[4096,1024]{1,0:T(8,128)(2,1)} %weight_rows.1, s32[]{:T(128)S(6)} %select_n.213, bf16[1024,1024]{1,0:T(8,128)(2,1)S(1)} %convolution_convert_fusion, bf16[1024,1024]{1,0:T(8,128)(2,1)} %collective-permute-done.3.refs_3_, bf16[1024,1024]{1,0:T(8,128)(2,1)S(1)} %copy-done.3), kind=kOutput, calls=%fused_computation.3 | convolution fusion | flops 2152726528 | bytes 8388612 | tf_op jit(solution)/shard_map/dot_general | solution.py:21
  115.7 5.1 %collective-permute-start.8 = (bf16[512,1024]{1,0:T(8,128)(2,1)}, bf16[512,1024]{1,0:T(8,128)(2,1)}, u32[]{:S(2)}, u32[]{:S(2)}) collective-permute-start(bf16[512,1024]{1,0:T(8,128)(2,1)} %cut_rows.2), channel_id=1, source_target_pairs={{1,0},{2,3},{5,4},{6,7},{9,8},{10,11},{13,12},{14,15},{17,16},{18,... | collective-permute-start | bytes 3145736 | tf_op jit(solution)/shard_map/ppermute | solution.py:369
  121.3 15.8 %early_product.1.early = f32[1024,1024]{1,0:T(8,128)} custom-call(s32[4]{0:T(128)} %fusion.32.order, bf16[1024,1024]{1,0:T(8,128)(2,1)} %refs_0_.3, bf16[1024,1024]{1,0:T(8,128)(2,1)} %copy-done.2, bf16[1024,1024]{1,0:T(8,128)(2,1)} %collective-permute-done.1.refs_2_, bf16[1024,1024]{1,0:T(8,128)(2,1)} %collective-permute-done.3.refs_3_, ...), custom_call_target="tpu_custom_call" | custom-call | flops 1 | bytes 1 | tf_op jit(solution)/shard_map/early_product/pallas_call | solution.py:611
  140.5 4.7 %collective-permute-start.9 = (bf16[512,1024]{1,0:T(8,128)(2,1)}, bf16[512,1024]{1,0:T(8,128)(2,1)S(1)}, u32[]{:S(2)}, u32[]{:S(2)}) collective-permute-start(bf16[512,1024]{1,0:T(8,128)(2,1)} %cut_rows.3), channel_id=1, source_target_pairs={{1,0},{2,3},{5,4},{6,7},{9,8},{10,11},{13,12},{14,15},{17,16},{18,... | collective-permute-start | bytes 3145736 | tf_op jit(solution)/shard_map/ppermute | solution.py:369
  146.0 7.3 %grad_mixed_rows.2 = (bf16[512,1024]{1,0:T(8,128)(2,1)}, f32[8,128,128]{2,1,0:T(8,128)}, f32[8,128,128]{2,1,0:T(8,128)}, bf16[8,128,128]{2,1,0:T(8,128)(2,1)}) custom-call(s32[4]{0:T(128)} %fusion.32.order, f32[8,8,1024]{2,1,0:T(8,128)} %factors.1, bf16[1024,1024]{1,0:T(8,128)(2,1)} %q.11, f32[1024,1024]{1,0:T(8,128)} %early_product.1.early, ...), custom_call_target="tpu_custom_call" | custom-call | flops 1 | bytes 1 | tf_op jit(solution)/shard_map/grad_mixed_rows/pallas_call | solution.py:665
  155.2 3.3 %fusion.4 = f32[1024,1024]{1,0:T(8,128)} fusion(bf16[512,1024]{1,0:T(8,128)(2,1)S(1)} %slice_add_fusion, bf16[1024,1024]{1,0:T(8,128)(2,1)S(1)} %copy-done.4), kind=kOutput, calls=%fused_computation.10 | convolution fusion | flops 1073741824 | bytes 6291456 | tf_op jit(solution)/shard_map/dot_general | solution.py:21
  158.6 7.6 %block_gradients.2 = (bf16[1024,1024]{1,0:T(8,128)(2,1)}, bf16[1024,1024]{1,0:T(8,128)(2,1)}, bf16[1024,1024]{1,0:T(8,128)(2,1)}) custom-call(f32[8,8,1024]{2,1,0:T(8,128)} %factors.1, bf16[1024,1024]{1,0:T(8,128)(2,1)} %q.11, bf16[1024,1024]{1,0:T(8,128)(2,1)} %k.9, bf16[1024,1024]{1,0:T(8,128)(2,1)} %v.9, bf16[512,1024]{1,0:T(8,128)(2,1)} %get-tuple-element.84.e, ...), custom_call_target="tpu_custom_call" | custom-call | flops 1 | bytes 1 | tf_op jit(solution)/shard_map/block_gradients/pallas_call | solution.py:699
  166.2 4.2 %add_convert_fusion = bf16[1024,1024]{1,0:T(8,128)(2,1)S(1)} fusion(f32[1024,1024]{1,0:T(8,128)} %fusion.4, bf16[1024,1024]{1,0:T(8,128)(2,1)} %get-tuple-element.75.refs_2_, bf16[512,1024]{1,0:T(8,128)(2,1)S(1)} %collective-permute-done.9.refs_1_, bf16[1024,1024]{1,0:T(8,128)(2,1)S(1)} %copy-done.1), kind=kOutput, calls=%fused_computation | convolution fusion | flops 1076363264 | bytes 9437184 | tf_op jit(solution)/shard_map/dot_general | solution.py:21
  171.5 7.2 %grad_mixed_rows.3 = (bf16[512,1024]{1,0:T(8,128)(2,1)}, f32[8,128,128]{2,1,0:T(8,128)}, f32[8,128,128]{2,1,0:T(8,128)}, bf16[8,128,128]{2,1,0:T(8,128)(2,1)}) custom-call(s32[4]{0:T(128)} %fusion.32.order, f32[8,8,1024]{2,1,0:T(8,128)} %factors.1, bf16[1024,1024]{1,0:T(8,128)(2,1)} %q.11, f32[1024,1024]{1,0:T(8,128)} %early_product.1.early, ...), custom_call_target="tpu_custom_call" | custom-call | flops 1 | bytes 1 | tf_op jit(solution)/shard_map/grad_mixed_rows/pallas_call | solution.py:665
  190.3 7.6 %block_gradients.3 = (bf16[1024,1024]{1,0:T(8,128)(2,1)}, bf16[1024,1024]{1,0:T(8,128)(2,1)}, bf16[1024,1024]{1,0:T(8,128)(2,1)}) custom-call(f32[8,8,1024]{2,1,0:T(8,128)} %factors.1, bf16[1024,1024]{1,0:T(8,128)(2,1)} %q.11, bf16[1024,1024]{1,0:T(8,128)(2,1)} %k.9, ...), custom_call_target="tpu_custom_call", output_to_operand_aliasing={{0}: (7, {}), {1}: (8, {}), {2}: (9, {})} | custom-call | flops 1 | bytes 1 | tf_op jit(solution)/shard_map/block_gradients/pallas_call | solution.py:699
  200.2 9.2 %collective-permute-done.16.refs_3_ = bf16[512,512]{1,0:T(8,128)(2,1)S(1)} collective-permute-done((bf16[512,512]{1,0:T(8,128)(2,1)S(1)}, bf16[512,512]{1,0:T(8,128)(2,1)S(1)}, u32[]{:S(2)}, u32[]{:S(2)}) %collective-permute-start.16) | collective-permute-done | bytes 524320 | tf_op jit(solution)/shard_map/ppermute | solution.py:460
  216.6 6.8 %carried_gradients.1 = (bf16[1024,1024]{1,0:T(8,128)(2,1)}, bf16[1024,1024]{1,0:T(8,128)(2,1)}) custom-call(f32[8,8,1024]{2,1,0:T(8,128)} %factors.1, bf16[1024,1024]{1,0:T(8,128)(2,1)} %k.9, bf16[1024,1024]{1,0:T(8,128)(2,1)} %v.9, bf16[1024,1024]{1,0:T(8,128)(2,1)} %get-tuple-element.104.dk_part, bf16[1024,1024]{1,0:T(8,128)(2,1)} %get-tuple-element.105.dv_part, ...), custom_call_target="tpu_custom_call" | custom-call | flops 1 | bytes 1 | tf_op jit(solution)/shard_map/carried_gradients/pallas_call | solution.py:724
  223.4 5.0 %collective-permute-done.18 = bf16[512,512]{1,0:T(8,128)(2,1)S(1)} collective-permute-done((bf16[512,512]{1,0:T(8,128)(2,1)}, bf16[512,512]{1,0:T(8,128)(2,1)S(1)}, u32[]{:S(2)}, u32[]{:S(2)}) %collective-permute-start.18) | collective-permute-done | bytes 524320 | tf_op jit(solution)/shard_map/ppermute | solution.py:460
  230.0 2.9 %fusion = f32[512,1024]{1,0:T(8,128)} fusion(f32[512,512]{1,0:T(8,128)S(1)} %convert_add_fusion, f32[512,512]{1,0:T(8,128)S(1)} %convert_add_fusion.1, bf16[512,1024]{1,0:T(8,128)(2,1)} %reduce-scatter.2.cloned.1.call-done, pred[]{:T(512)S(6)} %eq.13), kind=kLoop, calls=%fused_computation.2 | loop fusion | flops 2097152 | bytes 5242881 | tf_op jit(solution)/shard_map/add | solution.py:746
  (95 shorter events, 52.4 us)
Async XLA Ops:
  7.2 114.2 %all-gather.2.cloned.1.call-start = ((), (), s32[]{:S(2)}) async-start(), calls=%async_computation.1 | async-start | bytes 9437184 | tf_op jit(solution)/shard_map/all_gather | solution.py:488
  7.9 222.1 %reduce-scatter.2.cloned.1.call-start = ((), (), s32[]{:S(2)}) async-start(), calls=%async_computation.2 | async-start | bytes 9437184 | tf_op jit(solution)/shard_map/reduce_scatter | solution.py:644
  7.9 49.6 %collective-permute-start.1 = (bf16[1024,1024]{1,0:T(8,128)(2,1)}, bf16[1024,1024]{1,0:T(8,128)(2,1)}, u32[]{:S(2)}, u32[]{:S(2)}) collective-permute-start(bf16[1024,1024]{1,0:T(8,128)(2,1)} %refs_0_.3), channel_id=1, source_target_pairs={{2,1},{1,2},{6,5},{5,6},{10,9},{9,10},{14,13},{13,14},{18,17},{17,... | collective-permute-start | bytes 6291464 | tf_op jit(solution)/shard_map/ppermute | solution.py:369
  10.3 47.4 %collective-permute-start = (bf16[1024,1024]{1,0:T(8,128)(2,1)}, bf16[1024,1024]{1,0:T(8,128)(2,1)S(1)}, u32[]{:S(2)}, u32[]{:S(2)}) collective-permute-start(bf16[1024,1024]{1,0:T(8,128)(2,1)} %refs_0_.3), channel_id=1, source_target_pairs={{1,0},{0,1},{3,2},{2,3},{5,4},{4,5},{7,6},{6,7},{9,8},{8,9},{11,10... | collective-permute-start | bytes 6291464 | tf_op jit(solution)/shard_map/ppermute | solution.py:369
  22.0 1.8 collective-permute-start.2
  59.0 48.4 %collective-permute-start.4 = (bf16[1024,1024]{1,0:T(8,128)(2,1)}, bf16[1024,1024]{1,0:T(8,128)(2,1)S(1)}, u32[]{:S(2)}, u32[]{:S(2)}) collective-permute-start(bf16[1024,1024]{1,0:T(8,128)(2,1)} %copy-done.2), channel_id=1, source_target_pairs={{2,1},{1,2},{6,5},{5,6},{10,9},{9,10},{14,13},{13,14},{18,17},{17,... | collective-permute-start | bytes 6291464 | tf_op jit(solution)/shard_map/ppermute | solution.py:369
  62.5 45.4 %collective-permute-start.3 = (bf16[1024,1024]{1,0:T(8,128)(2,1)}, bf16[1024,1024]{1,0:T(8,128)(2,1)}, u32[]{:S(2)}, u32[]{:S(2)}) collective-permute-start(bf16[1024,1024]{1,0:T(8,128)(2,1)} %collective-permute-done.1.refs_2_), channel_id=1, source_target_pairs={{1,0},{2,3},{5,4},{6,7},{9,8},{10,11},{13,12},{14,15},{17,16},{18,... | collective-permute-start | bytes 6291464 | tf_op jit(solution)/shard_map/ppermute | solution.py:369
  65.1 10.7 %collective-permute-start.7 = (bf16[8,160,128]{2,1,0:T(8,128)(2,1)S(1)}, bf16[8,160,128]{2,1,0:T(8,128)(2,1)S(1)}, u32[]{:S(2)}, u32[]{:S(2)}) collective-permute-start(bf16[8,160,128]{2,1,0:T(8,128)(2,1)S(1)} %pad_maximum_fusion), channel_id=1, source_target_pairs={{0,8},{4,12},{8,0},{12,4},{16,24},{20,28},{24,16},{28,20},{1,9},{5... | collective-permute-start | bytes 983048 | tf_op jit(solution)/shard_map/ppermute | solution.py:278
  66.7 14.7 %collective-permute-start.6 = (bf16[8,160,128]{2,1,0:T(8,128)(2,1)S(1)}, bf16[8,160,128]{2,1,0:T(8,128)(2,1)S(1)}, u32[]{:S(2)}, u32[]{:S(2)}) collective-permute-start(bf16[8,160,128]{2,1,0:T(8,128)(2,1)S(1)} %pad_maximum_fusion), channel_id=1, source_target_pairs={{0,24},{4,28},{8,16},{12,20},{16,8},{20,12},{24,0},{28,4},{1,25},{... | collective-permute-start | bytes 983048 | tf_op jit(solution)/shard_map/ppermute | solution.py:278
  68.2 14.5 %collective-permute-start.5 = (bf16[8,160,128]{2,1,0:T(8,128)(2,1)S(1)}, bf16[8,160,128]{2,1,0:T(8,128)(2,1)S(1)}, u32[]{:S(2)}, u32[]{:S(2)}) collective-permute-start(bf16[8,160,128]{2,1,0:T(8,128)(2,1)S(1)} %pad_maximum_fusion), channel_id=1, source_target_pairs={{0,16},{4,20},{8,24},{12,28},{16,0},{20,4},{24,8},{28,12},{1,17},{... | collective-permute-start | bytes 983048 | tf_op jit(solution)/shard_map/ppermute | solution.py:278
  115.7 24.8 %collective-permute-start.8 = (bf16[512,1024]{1,0:T(8,128)(2,1)}, bf16[512,1024]{1,0:T(8,128)(2,1)}, u32[]{:S(2)}, u32[]{:S(2)}) collective-permute-start(bf16[512,1024]{1,0:T(8,128)(2,1)} %cut_rows.2), channel_id=1, source_target_pairs={{1,0},{2,3},{5,4},{6,7},{9,8},{10,11},{13,12},{14,15},{17,16},{18,... | collective-permute-start | bytes 3145736 | tf_op jit(solution)/shard_map/ppermute | solution.py:369
  140.5 25.6 %collective-permute-start.9 = (bf16[512,1024]{1,0:T(8,128)(2,1)}, bf16[512,1024]{1,0:T(8,128)(2,1)S(1)}, u32[]{:S(2)}, u32[]{:S(2)}) collective-permute-start(bf16[512,1024]{1,0:T(8,128)(2,1)} %cut_rows.3), channel_id=1, source_target_pairs={{1,0},{2,3},{5,4},{6,7},{9,8},{10,11},{13,12},{14,15},{17,16},{18,... | collective-permute-start | bytes 3145736 | tf_op jit(solution)/shard_map/ppermute | solution.py:369
  171.5 7.7 %collective-permute-start.11 = (bf16[512,1024]{1,0:T(8,128)(2,1)S(1)}, bf16[512,1024]{1,0:T(8,128)(2,1)S(1)}, u32[]{:S(2)}, u32[]{:S(2)}) collective-permute-start(bf16[512,1024]{1,0:T(8,128)(2,1)S(1)} %get-tuple-element.147), channel_id=1, source_target_pairs={{0,4},{4,0},{8,12},{12,8},{16,20},{20,16},{24,28},{28,24},{1,5},{5... | collective-permute-start | bytes 3145736 | tf_op jit(solution)/shard_map/ppermute | solution.py:597
  178.7 4.0 %collective-permute-start.10 = (bf16[8,128,128]{2,1,0:T(8,128)(2,1)}, bf16[8,128,128]{2,1,0:T(8,128)(2,1)S(1)}, u32[]{:S(2)}, u32[]{:S(2)}) collective-permute-start(bf16[8,128,128]{2,1,0:T(8,128)(2,1)} %get-tuple-element.95), channel_id=1, source_target_pairs={{0,4},{4,0},{8,12},{12,8},{16,20},{20,16},{24,28},{28,24},{1,5},{5... | collective-permute-start | bytes 786440 | tf_op jit(solution)/shard_map/ppermute | solution.py:278
  182.8 15.1 %collective-permute-start.13 = (bf16[8,128,128]{2,1,0:T(8,128)(2,1)S(1)}, bf16[8,128,128]{2,1,0:T(8,128)(2,1)S(1)}, u32[]{:S(2)}, u32[]{:S(2)}) collective-permute-start(bf16[8,128,128]{2,1,0:T(8,128)(2,1)S(1)} %fusion.8), channel_id=1, source_target_pairs={{0,16},{4,20},{8,24},{12,28},{16,0},{20,4},{24,8},{28,12},{1,17},{... | collective-permute-start | bytes 786440 | tf_op jit(solution)/shard_map/ppermute | solution.py:278
  184.4 13.6 %collective-permute-start.12 = (bf16[8,128,128]{2,1,0:T(8,128)(2,1)S(1)}, bf16[8,128,128]{2,1,0:T(8,128)(2,1)S(1)}, u32[]{:S(2)}, u32[]{:S(2)}) collective-permute-start(bf16[8,128,128]{2,1,0:T(8,128)(2,1)S(1)} %fusion.8), channel_id=1, source_target_pairs={{0,8},{4,12},{8,0},{12,4},{16,24},{20,28},{24,16},{28,20},{1,9},{5... | collective-permute-start | bytes 786440 | tf_op jit(solution)/shard_map/ppermute | solution.py:278
  186.3 12.9 %collective-permute-start.14 = (bf16[8,128,128]{2,1,0:T(8,128)(2,1)S(1)}, bf16[8,128,128]{2,1,0:T(8,128)(2,1)S(1)}, u32[]{:S(2)}, u32[]{:S(2)}) collective-permute-start(bf16[8,128,128]{2,1,0:T(8,128)(2,1)S(1)} %fusion.8), channel_id=1, source_target_pairs={{0,24},{4,28},{8,16},{12,20},{16,8},{20,12},{24,0},{28,4},{1,25},{... | collective-permute-start | bytes 786440 | tf_op jit(solution)/shard_map/ppermute | solution.py:278
  187.6 10.2 %copy-start.6 = (bf16[512,512]{1,0:T(8,128)(2,1)}, bf16[512,512]{1,0:T(8,128)(2,1)S(1)}, u32[]{:S(2)}) copy-start(bf16[512,512]{1,0:T(8,128)(2,1)S(1)} %get-tuple-element.149.refs_1_) | copy-start | bytes 1572868
  187.7 10.2 %copy-start.7 = (bf16[512,512]{1,0:T(8,128)(2,1)}, bf16[512,512]{1,0:T(8,128)(2,1)S(1)}, u32[]{:S(2)}) copy-start(bf16[512,512]{1,0:T(8,128)(2,1)S(1)} %get-tuple-element.150.refs_0_) | copy-start | bytes 1572868
  187.7 21.7 %collective-permute-start.16 = (bf16[512,512]{1,0:T(8,128)(2,1)S(1)}, bf16[512,512]{1,0:T(8,128)(2,1)S(1)}, u32[]{:S(2)}, u32[]{:S(2)}) collective-permute-start(bf16[512,512]{1,0:T(8,128)(2,1)S(1)} %get-tuple-element.149.refs_1_), channel_id=1, source_target_pairs={{0,8},{1,9},{4,12},{5,13},{10,2},{11,3},{14,6},{15,7},{16,24},{17,... | collective-permute-start | bytes 1572872 | tf_op jit(solution)/shard_map/ppermute | solution.py:460
  189.0 20.4 %collective-permute-start.15 = (bf16[512,512]{1,0:T(8,128)(2,1)S(1)}, bf16[512,512]{1,0:T(8,128)(2,1)S(1)}, u32[]{:S(2)}, u32[]{:S(2)}) collective-permute-start(bf16[512,512]{1,0:T(8,128)(2,1)S(1)} %get-tuple-element.150.refs_0_), channel_id=1, source_target_pairs={{0,16},{1,17},{4,20},{5,21},{8,24},{9,25},{12,28},{13,29},{18,2},{... | collective-permute-start | bytes 1572872 | tf_op jit(solution)/shard_map/ppermute | solution.py:460
  213.4 15.0 %collective-permute-start.18 = (bf16[512,512]{1,0:T(8,128)(2,1)}, bf16[512,512]{1,0:T(8,128)(2,1)S(1)}, u32[]{:S(2)}, u32[]{:S(2)}) collective-permute-start(bf16[512,512]{1,0:T(8,128)(2,1)} %get-tuple-element.118), channel_id=1, source_target_pairs={{8,24},{9,25},{12,28},{13,29},{18,2},{19,3},{22,6},{23,7}} | collective-permute-start | bytes 1572872 | tf_op jit(solution)/shard_map/ppermute | solution.py:460
  214.7 15.0 %collective-permute-start.17 = (bf16[512,512]{1,0:T(8,128)(2,1)}, bf16[512,512]{1,0:T(8,128)(2,1)S(1)}, u32[]{:S(2)}, u32[]{:S(2)}) collective-permute-start(bf16[512,512]{1,0:T(8,128)(2,1)} %get-tuple-element.111), channel_id=1, source_target_pairs={{10,2},{11,3},{14,6},{15,7},{16,24},{17,25},{20,28},{21,29}} | collective-permute-start | bytes 1572872 | tf_op jit(solution)/shard_map/ppermute | solution.py:460
  216.6 13.1 %copy-start.13 = (bf16[512,512]{1,0:T(8,128)(2,1)S(1)}, bf16[512,512]{1,0:T(8,128)(2,1)}, u32[]{:S(2)}) copy-start(bf16[512,512]{1,0:T(8,128)(2,1)} %get-tuple-element.118) | copy-start | bytes 1572868
  (12 other events, 46.0 us)
Sparse Core Ops, SparseCore 0:
  9.9 55.4 all-gather.1
  113.8 72.9 reduce-scatter.1

commit v4 on v3

--- a/solution.py
+++ b/solution.py
@@ -88,11 +88,14 @@
     out[...] = rows[...]
 
 
-def add_kernel(*refs):
-    many = len(refs) // 3
+def add_kernel(cuts, *refs):
+    many = len(refs) // (2 + cuts)
     for n in range(many):
         total = refs[n][...].astype(F32) + refs[many + n][...].astype(F32)
-        refs[2 * many + n][...] = total.astype(BF16)
+        total = total.astype(BF16)
+        span = total.shape[1] // cuts
+        for m in range(cuts):
+            refs[2 * many + n * cuts + m][...] = total[:, m * span : (m + 1) * span]
 
 
 def total_block(refs):
@@ -424,15 +427,16 @@
         return whole + [(tie(x, *after), 0) for x in cut]
 
 
-def add(these, those):
+def add(these, those, cuts=1):
     rows, width = these[0].shape
     spec = pl.BlockSpec((rows // 2, width), lambda n: (n, 0))
+    part = pl.BlockSpec((rows // 2, width // cuts), lambda n: (n, 0))
     return pl.pallas_call(
-        add_kernel,
+        functools.partial(add_kernel, cuts),
         grid=(2,),
         in_specs=[spec] * (2 * len(these)),
-        out_specs=[spec] * len(these),
-        out_shape=[jax.ShapeDtypeStruct(x.shape, BF16) for x in these],
+        out_specs=[part] * (cuts * len(these)),
+        out_shape=[jax.ShapeDtypeStruct((rows, width // cuts), BF16)] * (cuts * len(these)),
         compiler_params=PARAMS,
         cost_estimate=LIGHT,
         name="add_rows",
@@ -440,10 +444,8 @@
 
 
 class Tree:
-    def __init__(self, held, targets, flips):
-        self.targets, self.flips = targets, flips
-        span = held.shape[1] // len(flips)
-        self.now = [held[:, n * span : (n + 1) * span] for n in range(len(flips))]
+    def __init__(self, parts, targets, flips):
+        self.targets, self.flips, self.now = targets, flips, list(parts)
         self.got, self.turn, self.done = None, 0, [0] * len(flips)
 
     def send(self, *after):
@@ -597,7 +599,7 @@
         return lax.ppermute(tie(sent, *after), "tm", [(i, i ^ 1) for i in range(count)])
 
     def joined(kept, got, *after):
-        return add([kept], [tie(got, *after)])[0]
+        return add([kept], [tie(got, *after)], 2)
 
     two = many
     cover = two * DK
@@ -693,7 +695,7 @@
             held = joined(kept, got, e[b])
             last_tree = Tree(held, targets(size - 1), [group_bits[::-1], group_bits])
             last_tree.send()
-            order_after = back.take_pair(held)
+            order_after = back.take_pair(held[0])
             back.send_all()
         own_rows = pl.BlockSpec((BLK, many * DK), lambda h, b=b: (b, h))
         filled = pl.pallas_call(
@@ -718,7 +720,7 @@
     dq, dk_part, dv_part = filled
     grad_in = back.take_all(dq)
     for _ in group_bits[1:]:
-        last_tree.take(grad_in)
+        last_tree.take(dq)
         last_tree.send()
     pair_rows = pl.BlockSpec((tok, cover), lambda n: (0, n))
     dk, dv = pl.pallas_call(
@@ -738,7 +740,7 @@
         value,
         dk_part,
         dv_part,
-        tie(grad_in, last_tree.now[0]),
+        grad_in,
         *[parts[b] for b in range(blocks)],
     )
     done = [x.astype(F32) + tie(y, dk).astype(F32) for x, y in zip(last_tree.now, last_tree.got)]

time: 241 us -> 235 us (0.975)
  waiting for transfers between devices: 54.8 us -> 49.6 us
    ppermute x4, waiting for transfers between devices: 15.5 us -> 5.66 us  [send(): lax.ppermute(tie(self.now[n], *after), ('tm', 'head'), perm)]
    ppermute x8, waiting for transfers between devices: 14.6 us -> 19.2 us  [permute(): return lax.ppermute(value, 'tm', [(i, i ^ mask) for i in range(count)])]
  transfers between devices with their start and end apart: 21 -> 21, of which waited for: 13 -> 13; matrix products, arithmetic and copies ran while one was open for 13% -> 13% of each run, Pallas kernels for 41% -> 42%
where the time goes in v4:
time: 235 us; the launch traced here: 234 us
  Pallas kernels  98.7 us (42%)
  waiting for transfers between devices  49.6 us (21%)
  starting transfers between devices  34.1 us (15%)
  matrix products  18.1 us (8%)
  between operations  15.6 us (7%)
  other arithmetic  11.7 us (5%)
  local copies, waits for them, and re-layouts  6.32 us (3%)
    ppermute x6, waiting for transfers between devices, permute(): return lax.ppermute(value, 'head', self.plan[name])  24 us
    ppermute x6, starting transfers between devices, permute(): return lax.ppermute(value, 'head', self.plan[name])  19.4 us
    ppermute x8, waiting for transfers between devices, permute(): return lax.ppermute(value, 'tm', [(i, i ^ mask) for i in range(count)])  19.2 us
    dot_general x4, matrix products, dot(): lax.dot_general(a, b, (((da,), (db,)), ((), ())), preferred_element_type=...  18.1 us
    pallas_call x1, Pallas kernels, accumulate(): pl.pallas_call(functools.partial(early_kernel, [len(x) for x in inputs]),...  15.7 us
    pallas_call x2, Pallas kernels, per_device(): pl.pallas_call(back_kernel, grid=(heads // many,), in_specs=[pl.BlockSpec...  15.2 us
    pallas_call x2, Pallas kernels, per_device(): pl.pallas_call(functools.partial(grad_kernel, [len(arrays)]), grid_spec=p...  14.4 us
    pallas_call x1, Pallas kernels, rows_of(): pl.pallas_call(functools.partial(rows_kernel, counts), grid_spec=pltpu.Pr...  12.8 us
  transfers between devices with their start and end apart: 21, of which 13 were waited for; matrix products, arithmetic and copies ran while one was open for 13% of the time, Pallas kernels for 42%

profile of v4, /device:TPU:16, one launch (start us, length us, event | category | flops | bytes accessed | tf_op | source)
XLA Modules:
  0.0 234.1 jit_solution(6529746052732091046)
XLA Ops:
  15.4 6.6 %block_states.1 = (f32[8,2,128,128]{3,2,1,0:T(8,128)}, f32[8,128,128]{2,1,0:T(8,128)}, f32[8,8,128]{2,1,0:T(8,128)}, bf16[8,160,128]{2,1,0:T(8,128)(2,1)}) custom-call(f32[8,8,1024]{2,1,0:T(8,128)} %factors.1, bf16[1024,1024]{1,0:T(8,128)(2,1)} %k.9, bf16[1024,1024]{1,0:T(8,128)(2,1)} %v.9), custom_call_target="tpu_custom_call" | custom-call | flops 1 | bytes 1 | tf_op jit(solution)/shard_map/block_states/pallas_call | solution.py:521
  25.8 10.0 %pair_weights.1 = (bf16[8,2,768,256]{3,2,1,0:T(8,128)(2,1)}, f32[1024,1024]{1,0:T(8,128)}) custom-call(f32[8,8,1024]{2,1,0:T(8,128)} %factors.1, bf16[1024,1024]{1,0:T(8,128)(2,1)} %q.11, bf16[1024,1024]{1,0:T(8,128)(2,1)} %k.9, bf16[1024,1024]{1,0:T(8,128)(2,1)} %v.9), custom_call_target="tpu_custom_call" | custom-call | flops 1 | bytes 1 | tf_op jit(solution)/shard_map/pair_weights/pallas_call | solution.py:540
  35.7 21.8 %collective-permute-done.1.refs_2_ = bf16[1024,1024]{1,0:T(8,128)(2,1)} collective-permute-done((bf16[1024,1024]{1,0:T(8,128)(2,1)}, bf16[1024,1024]{1,0:T(8,128)(2,1)}, u32[]{:S(2)}, u32[]{:S(2)}) %collective-permute-start.1) | collective-permute-done | bytes 2097184 | tf_op jit(solution)/shard_map/ppermute | solution.py:372
  59.0 3.5 %collective-permute-start.4 = (bf16[1024,1024]{1,0:T(8,128)(2,1)}, bf16[1024,1024]{1,0:T(8,128)(2,1)S(1)}, u32[]{:S(2)}, u32[]{:S(2)}) collective-permute-start(bf16[1024,1024]{1,0:T(8,128)(2,1)} %copy-done.2), channel_id=1, source_target_pairs={{2,1},{1,2},{6,5},{5,6},{10,9},{9,10},{14,13},{13,14},{18,17},{17,... | collective-permute-start | bytes 6291464 | tf_op jit(solution)/shard_map/ppermute | solution.py:372
  69.9 6.0 %collective-permute-done.7 = bf16[8,160,128]{2,1,0:T(8,128)(2,1)S(1)} collective-permute-done((bf16[8,160,128]{2,1,0:T(8,128)(2,1)S(1)}, bf16[8,160,128]{2,1,0:T(8,128)(2,1)S(1)}, u32[]{:S(2)}, u32[]{:S(2)}) %collective-permute-start.7) | collective-permute-done | bytes 327712 | tf_op jit(solution)/shard_map/ppermute | solution.py:281
  75.9 5.5 %collective-permute-done.6 = bf16[8,160,128]{2,1,0:T(8,128)(2,1)S(1)} collective-permute-done((bf16[8,160,128]{2,1,0:T(8,128)(2,1)S(1)}, bf16[8,160,128]{2,1,0:T(8,128)(2,1)S(1)}, u32[]{:S(2)}, u32[]{:S(2)}) %collective-permute-start.6) | collective-permute-done | bytes 327712 | tf_op jit(solution)/shard_map/ppermute | solution.py:281
  83.8 5.9 %mixed_rows.1 = (bf16[1024,1024]{1,0:T(8,128)(2,1)}, bf16[8,2,128,128]{3,2,1,0:T(8,128)(2,1)}) custom-call(f32[8,8,1024]{2,1,0:T(8,128)} %factors.1, bf16[1024,1024]{1,0:T(8,128)(2,1)} %q.11, f32[1024,1024]{1,0:T(8,128)} %get-tuple-element.67.within, f32[8,2,128,128]{3,2,1,0:T(8,128)} %get-tuple-element.72.parts, f32[8,128,128]{2,1,0:T(8,128)} %fusion.7.start), custom_call_target="tpu_custom_call" | custom-call | flops 1 | bytes 1 | tf_op jit(solution)/shard_map/mixed_rows/pallas_call | solution.py:553
  89.7 12.8 %weight_rows.1 = bf16[4096,1024]{1,0:T(8,128)(2,1)} custom-call(s32[3]{0:T(128)} %pad_add_fusion.order, bf16[1024,1024]{1,0:T(8,128)(2,1)} %refs_0_.3, bf16[1024,1024]{1,0:T(8,128)(2,1)} %copy-done.2, bf16[1024,1024]{1,0:T(8,128)(2,1)} %get-tuple-element.76.refs_2_), custom_call_target="tpu_custom_call" | custom-call | flops 1 | bytes 1 | tf_op jit(solution)/shard_map/weight_rows/pallas_call | solution.py:583
  102.5 4.8 %convolution_convert_fusion = bf16[1024,1024]{1,0:T(8,128)(2,1)S(1)} fusion(bf16[1024,1024]{1,0:T(8,128)(2,1)} %collective-permute-done.1.refs_2_, bf16[1024,1024]{1,0:T(8,128)(2,1)} %get-tuple-element.76.refs_2_), kind=kOutput, calls=%fused_computation.4 | convolution fusion | flops 2148532224 | bytes 6291456 | tf_op jit(solution)/shard_map/dot_general | solution.py:21
  107.9 5.8 %add_dynamic-update-slice_fusion = bf16[4096,1024]{1,0:T(8,128)(2,1)} fusion(bf16[4096,1024]{1,0:T(8,128)(2,1)} %weight_rows.1, s32[]{:T(128)S(6)} %select_n.213, bf16[1024,1024]{1,0:T(8,128)(2,1)S(1)} %convolution_convert_fusion, bf16[1024,1024]{1,0:T(8,128)(2,1)} %collective-permute-done.3.refs_3_, bf16[1024,1024]{1,0:T(8,128)(2,1)S(1)} %copy-done.3), kind=kOutput, calls=%fused_computation.3 | convolution fusion | flops 2152726528 | bytes 8388612 | tf_op jit(solution)/shard_map/dot_general | solution.py:21
  115.7 5.1 %collective-permute-start.8 = (bf16[512,1024]{1,0:T(8,128)(2,1)}, bf16[512,1024]{1,0:T(8,128)(2,1)}, u32[]{:S(2)}, u32[]{:S(2)}) collective-permute-start(bf16[512,1024]{1,0:T(8,128)(2,1)} %cut_rows.2), channel_id=1, source_target_pairs={{1,0},{2,3},{5,4},{6,7},{9,8},{10,11},{13,12},{14,15},{17,16},{18,... | collective-permute-start | bytes 3145736 | tf_op jit(solution)/shard_map/ppermute | solution.py:372
  121.3 15.7 %early_product.1.early = f32[1024,1024]{1,0:T(8,128)} custom-call(s32[4]{0:T(128)} %fusion.31.order, bf16[1024,1024]{1,0:T(8,128)(2,1)} %refs_0_.3, bf16[1024,1024]{1,0:T(8,128)(2,1)} %copy-done.2, bf16[1024,1024]{1,0:T(8,128)(2,1)} %collective-permute-done.1.refs_2_, bf16[1024,1024]{1,0:T(8,128)(2,1)} %collective-permute-done.3.refs_3_, ...), custom_call_target="tpu_custom_call" | custom-call | flops 1 | bytes 1 | tf_op jit(solution)/shard_map/early_product/pallas_call | solution.py:613
  140.5 4.7 %collective-permute-start.9 = (bf16[512,1024]{1,0:T(8,128)(2,1)}, bf16[512,1024]{1,0:T(8,128)(2,1)S(1)}, u32[]{:S(2)}, u32[]{:S(2)}) collective-permute-start(bf16[512,1024]{1,0:T(8,128)(2,1)} %cut_rows.3), channel_id=1, source_target_pairs={{1,0},{2,3},{5,4},{6,7},{9,8},{10,11},{13,12},{14,15},{17,16},{18,... | collective-permute-start | bytes 3145736 | tf_op jit(solution)/shard_map/ppermute | solution.py:372
  146.0 7.3 %grad_mixed_rows.2 = (bf16[512,1024]{1,0:T(8,128)(2,1)}, f32[8,128,128]{2,1,0:T(8,128)}, f32[8,128,128]{2,1,0:T(8,128)}, bf16[8,128,128]{2,1,0:T(8,128)(2,1)}) custom-call(s32[4]{0:T(128)} %fusion.31.order, f32[8,8,1024]{2,1,0:T(8,128)} %factors.1, bf16[1024,1024]{1,0:T(8,128)(2,1)} %q.11, f32[1024,1024]{1,0:T(8,128)} %early_product.1.early, ...), custom_call_target="tpu_custom_call" | custom-call | flops 1 | bytes 1 | tf_op jit(solution)/shard_map/grad_mixed_rows/pallas_call | solution.py:667
  155.2 3.3 %fusion.4 = f32[1024,1024]{1,0:T(8,128)} fusion(bf16[512,1024]{1,0:T(8,128)(2,1)S(1)} %slice_add_fusion, bf16[1024,1024]{1,0:T(8,128)(2,1)S(1)} %copy-done.4), kind=kOutput, calls=%fused_computation.10 | convolution fusion | flops 1073741824 | bytes 6291456 | tf_op jit(solution)/shard_map/dot_general | solution.py:21
  158.6 7.6 %block_gradients.2 = (bf16[1024,1024]{1,0:T(8,128)(2,1)}, bf16[1024,1024]{1,0:T(8,128)(2,1)}, bf16[1024,1024]{1,0:T(8,128)(2,1)}) custom-call(f32[8,8,1024]{2,1,0:T(8,128)} %factors.1, bf16[1024,1024]{1,0:T(8,128)(2,1)} %q.11, bf16[1024,1024]{1,0:T(8,128)(2,1)} %k.9, bf16[1024,1024]{1,0:T(8,128)(2,1)} %v.9, bf16[512,1024]{1,0:T(8,128)(2,1)} %get-tuple-element.85.e, ...), custom_call_target="tpu_custom_call" | custom-call | flops 1 | bytes 1 | tf_op jit(solution)/shard_map/block_gradients/pallas_call | solution.py:701
  166.2 4.2 %add_convert_fusion = bf16[1024,1024]{1,0:T(8,128)(2,1)S(1)} fusion(f32[1024,1024]{1,0:T(8,128)} %fusion.4, bf16[1024,1024]{1,0:T(8,128)(2,1)} %get-tuple-element.76.refs_2_, bf16[512,1024]{1,0:T(8,128)(2,1)S(1)} %collective-permute-done.9.refs_1_, bf16[1024,1024]{1,0:T(8,128)(2,1)S(1)} %copy-done.1), kind=kOutput, calls=%fused_computation | convolution fusion | flops 1076363264 | bytes 9437184 | tf_op jit(solution)/shard_map/dot_general | solution.py:21
  171.5 7.1 %grad_mixed_rows.3 = (bf16[512,1024]{1,0:T(8,128)(2,1)}, f32[8,128,128]{2,1,0:T(8,128)}, f32[8,128,128]{2,1,0:T(8,128)}, bf16[8,128,128]{2,1,0:T(8,128)(2,1)}) custom-call(s32[4]{0:T(128)} %fusion.31.order, f32[8,8,1024]{2,1,0:T(8,128)} %factors.1, bf16[1024,1024]{1,0:T(8,128)(2,1)} %q.11, f32[1024,1024]{1,0:T(8,128)} %early_product.1.early, ...), custom_call_target="tpu_custom_call" | custom-call | flops 1 | bytes 1 | tf_op jit(solution)/shard_map/grad_mixed_rows/pallas_call | solution.py:667
  189.1 2.7 %collective-permute-start.12 = (bf16[8,128,128]{2,1,0:T(8,128)(2,1)S(1)}, bf16[8,128,128]{2,1,0:T(8,128)(2,1)S(1)}, u32[]{:S(2)}, u32[]{:S(2)}) collective-permute-start(bf16[8,128,128]{2,1,0:T(8,128)(2,1)S(1)} %fusion.8), channel_id=1, source_target_pairs={{0,8},{4,12},{8,0},{12,4},{16,24},{20,28},{24,16},{28,20},{1,9},{5... | collective-permute-start | bytes 786440 | tf_op jit(solution)/shard_map/ppermute | solution.py:281
  191.8 7.6 %block_gradients.3 = (bf16[1024,1024]{1,0:T(8,128)(2,1)}, bf16[1024,1024]{1,0:T(8,128)(2,1)}, bf16[1024,1024]{1,0:T(8,128)(2,1)}) custom-call(f32[8,8,1024]{2,1,0:T(8,128)} %factors.1, bf16[1024,1024]{1,0:T(8,128)(2,1)} %q.11, bf16[1024,1024]{1,0:T(8,128)(2,1)} %k.9, ...), custom_call_target="tpu_custom_call", output_to_operand_aliasing={{0}: (7, {}), {1}: (8, {}), {2}: (9, {})} | custom-call | flops 1 | bytes 1 | tf_op jit(solution)/shard_map/block_gradients/pallas_call | solution.py:701
  206.5 4.7 %collective-permute-done.13 = bf16[8,128,128]{2,1,0:T(8,128)(2,1)S(1)} collective-permute-done((bf16[8,128,128]{2,1,0:T(8,128)(2,1)S(1)}, bf16[8,128,128]{2,1,0:T(8,128)(2,1)S(1)}, u32[]{:S(2)}, u32[]{:S(2)}) %collective-permute-start.13) | collective-permute-done | bytes 262176 | tf_op jit(solution)/shard_map/ppermute | solution.py:281
  212.3 6.8 %carried_gradients.1 = (bf16[1024,1024]{1,0:T(8,128)(2,1)}, bf16[1024,1024]{1,0:T(8,128)(2,1)}) custom-call(f32[8,8,1024]{2,1,0:T(8,128)} %factors.1, bf16[1024,1024]{1,0:T(8,128)(2,1)} %k.9, bf16[1024,1024]{1,0:T(8,128)(2,1)} %v.9, bf16[1024,1024]{1,0:T(8,128)(2,1)} %get-tuple-element.106.dk_part, bf16[1024,1024]{1,0:T(8,128)(2,1)} %get-tuple-element.107.dv_part, ...), custom_call_target="tpu_custom_call" | custom-call | flops 1 | bytes 1 | tf_op jit(solution)/shard_map/carried_gradients/pallas_call | solution.py:726
  219.1 4.9 %collective-permute-done.17 = bf16[512,512]{1,0:T(8,128)(2,1)S(1)} collective-permute-done((bf16[512,512]{1,0:T(8,128)(2,1)}, bf16[512,512]{1,0:T(8,128)(2,1)S(1)}, u32[]{:S(2)}, u32[]{:S(2)}) %collective-permute-start.17) | collective-permute-done | bytes 524320 | tf_op jit(solution)/shard_map/ppermute | solution.py:462
  224.3 2.9 %fusion = f32[512,1024]{1,0:T(8,128)} fusion(f32[512,512]{1,0:T(8,128)S(1)} %convert_add_fusion, f32[512,512]{1,0:T(8,128)S(1)} %convert_add_fusion.1, bf16[512,1024]{1,0:T(8,128)(2,1)} %reduce-scatter.2.cloned.1.call-done, pred[]{:T(512)S(6)} %eq.13), kind=kLoop, calls=%fused_computation.2 | loop fusion | flops 2097152 | bytes 5242881 | tf_op jit(solution)/shard_map/add | solution.py:748
  (92 shorter events, 51.4 us)
Async XLA Ops:
  7.2 114.2 %all-gather.2.cloned.1.call-start = ((), (), s32[]{:S(2)}) async-start(), calls=%async_computation.1 | async-start | bytes 9437184 | tf_op jit(solution)/shard_map/all_gather | solution.py:490
  7.9 216.4 %reduce-scatter.2.cloned.1.call-start = ((), (), s32[]{:S(2)}) async-start(), calls=%async_computation.2 | async-start | bytes 9437184 | tf_op jit(solution)/shard_map/reduce_scatter | solution.py:646
  7.9 49.6 %collective-permute-start.1 = (bf16[1024,1024]{1,0:T(8,128)(2,1)}, bf16[1024,1024]{1,0:T(8,128)(2,1)}, u32[]{:S(2)}, u32[]{:S(2)}) collective-permute-start(bf16[1024,1024]{1,0:T(8,128)(2,1)} %refs_0_.3), channel_id=1, source_target_pairs={{2,1},{1,2},{6,5},{5,6},{10,9},{9,10},{14,13},{13,14},{18,17},{17,... | collective-permute-start | bytes 6291464 | tf_op jit(solution)/shard_map/ppermute | solution.py:372
  10.3 47.4 %collective-permute-start = (bf16[1024,1024]{1,0:T(8,128)(2,1)}, bf16[1024,1024]{1,0:T(8,128)(2,1)S(1)}, u32[]{:S(2)}, u32[]{:S(2)}) collective-permute-start(bf16[1024,1024]{1,0:T(8,128)(2,1)} %refs_0_.3), channel_id=1, source_target_pairs={{1,0},{0,1},{3,2},{2,3},{5,4},{4,5},{7,6},{6,7},{9,8},{8,9},{11,10... | collective-permute-start | bytes 6291464 | tf_op jit(solution)/shard_map/ppermute | solution.py:372
  22.0 1.8 collective-permute-start.2
  59.0 48.4 %collective-permute-start.4 = (bf16[1024,1024]{1,0:T(8,128)(2,1)}, bf16[1024,1024]{1,0:T(8,128)(2,1)S(1)}, u32[]{:S(2)}, u32[]{:S(2)}) collective-permute-start(bf16[1024,1024]{1,0:T(8,128)(2,1)} %copy-done.2), channel_id=1, source_target_pairs={{2,1},{1,2},{6,5},{5,6},{10,9},{9,10},{14,13},{13,14},{18,17},{17,... | collective-permute-start | bytes 6291464 | tf_op jit(solution)/shard_map/ppermute | solution.py:372
  62.5 45.4 %collective-permute-start.3 = (bf16[1024,1024]{1,0:T(8,128)(2,1)}, bf16[1024,1024]{1,0:T(8,128)(2,1)}, u32[]{:S(2)}, u32[]{:S(2)}) collective-permute-start(bf16[1024,1024]{1,0:T(8,128)(2,1)} %collective-permute-done.1.refs_2_), channel_id=1, source_target_pairs={{1,0},{2,3},{5,4},{6,7},{9,8},{10,11},{13,12},{14,15},{17,16},{18,... | collective-permute-start | bytes 6291464 | tf_op jit(solution)/shard_map/ppermute | solution.py:372
  65.1 10.7 %collective-permute-start.7 = (bf16[8,160,128]{2,1,0:T(8,128)(2,1)S(1)}, bf16[8,160,128]{2,1,0:T(8,128)(2,1)S(1)}, u32[]{:S(2)}, u32[]{:S(2)}) collective-permute-start(bf16[8,160,128]{2,1,0:T(8,128)(2,1)S(1)} %pad_maximum_fusion), channel_id=1, source_target_pairs={{0,8},{4,12},{8,0},{12,4},{16,24},{20,28},{24,16},{28,20},{1,9},{5... | collective-permute-start | bytes 983048 | tf_op jit(solution)/shard_map/ppermute | solution.py:281
  66.7 14.7 %collective-permute-start.6 = (bf16[8,160,128]{2,1,0:T(8,128)(2,1)S(1)}, bf16[8,160,128]{2,1,0:T(8,128)(2,1)S(1)}, u32[]{:S(2)}, u32[]{:S(2)}) collective-permute-start(bf16[8,160,128]{2,1,0:T(8,128)(2,1)S(1)} %pad_maximum_fusion), channel_id=1, source_target_pairs={{0,24},{4,28},{8,16},{12,20},{16,8},{20,12},{24,0},{28,4},{1,25},{... | collective-permute-start | bytes 983048 | tf_op jit(solution)/shard_map/ppermute | solution.py:281
  68.2 14.5 %collective-permute-start.5 = (bf16[8,160,128]{2,1,0:T(8,128)(2,1)S(1)}, bf16[8,160,128]{2,1,0:T(8,128)(2,1)S(1)}, u32[]{:S(2)}, u32[]{:S(2)}) collective-permute-start(bf16[8,160,128]{2,1,0:T(8,128)(2,1)S(1)} %pad_maximum_fusion), channel_id=1, source_target_pairs={{0,16},{4,20},{8,24},{12,28},{16,0},{20,4},{24,8},{28,12},{1,17},{... | collective-permute-start | bytes 983048 | tf_op jit(solution)/shard_map/ppermute | solution.py:281
  115.7 24.8 %collective-permute-start.8 = (bf16[512,1024]{1,0:T(8,128)(2,1)}, bf16[512,1024]{1,0:T(8,128)(2,1)}, u32[]{:S(2)}, u32[]{:S(2)}) collective-permute-start(bf16[512,1024]{1,0:T(8,128)(2,1)} %cut_rows.2), channel_id=1, source_target_pairs={{1,0},{2,3},{5,4},{6,7},{9,8},{10,11},{13,12},{14,15},{17,16},{18,... | collective-permute-start | bytes 3145736 | tf_op jit(solution)/shard_map/ppermute | solution.py:372
  140.5 25.6 %collective-permute-start.9 = (bf16[512,1024]{1,0:T(8,128)(2,1)}, bf16[512,1024]{1,0:T(8,128)(2,1)S(1)}, u32[]{:S(2)}, u32[]{:S(2)}) collective-permute-start(bf16[512,1024]{1,0:T(8,128)(2,1)} %cut_rows.3), channel_id=1, source_target_pairs={{1,0},{2,3},{5,4},{6,7},{9,8},{10,11},{13,12},{14,15},{17,16},{18,... | collective-permute-start | bytes 3145736 | tf_op jit(solution)/shard_map/ppermute | solution.py:372
  146.0 7.3 %copy-start.1 = (bf16[1024,1024]{1,0:T(8,128)(2,1)S(1)}, bf16[1024,1024]{1,0:T(8,128)(2,1)}, u32[]{:S(2)}) copy-start(bf16[1024,1024]{1,0:T(8,128)(2,1)} %copy-done) | copy-start | bytes 6291460
  171.5 7.2 %collective-permute-start.11 = (bf16[512,1024]{1,0:T(8,128)(2,1)S(1)}, bf16[512,1024]{1,0:T(8,128)(2,1)S(1)}, u32[]{:S(2)}, u32[]{:S(2)}) collective-permute-start(bf16[512,1024]{1,0:T(8,128)(2,1)S(1)} %get-tuple-element.149), channel_id=1, source_target_pairs={{0,4},{4,0},{8,12},{12,8},{16,20},{20,16},{24,28},{28,24},{1,5},{5... | collective-permute-start | bytes 3145736 | tf_op jit(solution)/shard_map/ppermute | solution.py:599
  178.7 7.7 %copy-start.7 = (f32[8,128,128]{2,1,0:T(8,128)S(1)}, f32[8,128,128]{2,1,0:T(8,128)}, u32[]{:S(2)}) copy-start(f32[8,128,128]{2,1,0:T(8,128)} %get-tuple-element.101) | copy-start | bytes 1572868
  182.1 17.3 %collective-permute-start.16 = (bf16[512,512]{1,0:T(8,128)(2,1)}, bf16[512,512]{1,0:T(8,128)(2,1)S(1)}, u32[]{:S(2)}, u32[]{:S(2)}) collective-permute-start(bf16[512,512]{1,0:T(8,128)(2,1)} %get-tuple-element.115.refs_1_), channel_id=1, source_target_pairs={{0,8},{1,9},{4,12},{5,13},{10,2},{11,3},{14,6},{15,7},{16,24},{17,... | collective-permute-start | bytes 1572872 | tf_op jit(solution)/shard_map/ppermute | solution.py:462
  183.3 16.8 %collective-permute-start.15 = (bf16[512,512]{1,0:T(8,128)(2,1)}, bf16[512,512]{1,0:T(8,128)(2,1)S(1)}, u32[]{:S(2)}, u32[]{:S(2)}) collective-permute-start(bf16[512,512]{1,0:T(8,128)(2,1)} %get-tuple-element.99.refs_0_), channel_id=1, source_target_pairs={{0,16},{1,17},{4,20},{5,21},{8,24},{9,25},{12,28},{13,29},{18,2},{... | collective-permute-start | bytes 1572872 | tf_op jit(solution)/shard_map/ppermute | solution.py:462
  184.7 1.7 collective-permute-start.10
  186.5 24.7 %collective-permute-start.13 = (bf16[8,128,128]{2,1,0:T(8,128)(2,1)S(1)}, bf16[8,128,128]{2,1,0:T(8,128)(2,1)S(1)}, u32[]{:S(2)}, u32[]{:S(2)}) collective-permute-start(bf16[8,128,128]{2,1,0:T(8,128)(2,1)S(1)} %fusion.8), channel_id=1, source_target_pairs={{0,16},{4,20},{8,24},{12,28},{16,0},{20,4},{24,8},{28,12},{1,17},{... | collective-permute-start | bytes 786440 | tf_op jit(solution)/shard_map/ppermute | solution.py:281
  189.1 22.1 %collective-permute-start.12 = (bf16[8,128,128]{2,1,0:T(8,128)(2,1)S(1)}, bf16[8,128,128]{2,1,0:T(8,128)(2,1)S(1)}, u32[]{:S(2)}, u32[]{:S(2)}) collective-permute-start(bf16[8,128,128]{2,1,0:T(8,128)(2,1)S(1)} %fusion.8), channel_id=1, source_target_pairs={{0,8},{4,12},{8,0},{12,4},{16,24},{20,28},{24,16},{28,20},{1,9},{5... | collective-permute-start | bytes 786440 | tf_op jit(solution)/shard_map/ppermute | solution.py:281
  191.8 19.5 %collective-permute-start.14 = (bf16[8,128,128]{2,1,0:T(8,128)(2,1)S(1)}, bf16[8,128,128]{2,1,0:T(8,128)(2,1)S(1)}, u32[]{:S(2)}, u32[]{:S(2)}) collective-permute-start(bf16[8,128,128]{2,1,0:T(8,128)(2,1)S(1)} %fusion.8), channel_id=1, source_target_pairs={{0,24},{4,28},{8,16},{12,20},{16,8},{20,12},{24,0},{28,4},{1,25},{... | collective-permute-start | bytes 786440 | tf_op jit(solution)/shard_map/ppermute | solution.py:281
  203.4 20.6 %collective-permute-start.17 = (bf16[512,512]{1,0:T(8,128)(2,1)}, bf16[512,512]{1,0:T(8,128)(2,1)S(1)}, u32[]{:S(2)}, u32[]{:S(2)}) collective-permute-start(bf16[512,512]{1,0:T(8,128)(2,1)} %get-tuple-element.118), channel_id=1, source_target_pairs={{10,2},{11,3},{14,6},{15,7},{16,24},{17,25},{20,28},{21,29}} | collective-permute-start | bytes 1572872 | tf_op jit(solution)/shard_map/ppermute | solution.py:462
  204.6 19.3 %collective-permute-start.18 = (bf16[512,512]{1,0:T(8,128)(2,1)}, bf16[512,512]{1,0:T(8,128)(2,1)S(1)}, u32[]{:S(2)}, u32[]{:S(2)}) collective-permute-start(bf16[512,512]{1,0:T(8,128)(2,1)} %get-tuple-element.120), channel_id=1, source_target_pairs={{8,24},{9,25},{12,28},{13,29},{18,2},{19,3},{22,6},{23,7}} | collective-permute-start | bytes 1572872 | tf_op jit(solution)/shard_map/ppermute | solution.py:462
  212.3 11.7 %copy-start.9 = (bf16[512,512]{1,0:T(8,128)(2,1)S(1)}, bf16[512,512]{1,0:T(8,128)(2,1)}, u32[]{:S(2)}) copy-start(bf16[512,512]{1,0:T(8,128)(2,1)} %get-tuple-element.118) | copy-start | bytes 1572868
  (11 other events, 39.3 us)
Sparse Core Ops, SparseCore 0:
  9.9 55.4 all-gather.1
  113.8 72.9 reduce-scatter.1

commit v5 on v4

--- a/solution.py
+++ b/solution.py
@@ -689,7 +689,8 @@
         order_after = e[b]
         if b:
             part = dot(tie(block, e[b]), mixed[start:end], 0, 0)
-            product = part if n == 0 else product + part
+            part = part if n == 0 else product.astype(F32) + part
+            product = part.astype(BF16)
             order_after = product
         else:
             held = joined(kept, got, e[b])

time: 235 us -> 235 us (level)
  waiting for transfers between devices: 49.6 us -> 55.1 us
  starting transfers between devices: 34.1 us -> 29.8 us
    ppermute x6, waiting for transfers between devices: 24 us -> 31.2 us  [permute(): return lax.ppermute(value, 'head', self.plan[name])]
    ppermute x6, starting transfers between devices: 19.4 us -> 15.1 us  [permute(): return lax.ppermute(value, 'head', self.plan[name])]
  transfers between devices with their start and end apart: 21 -> 21, of which waited for: 13 -> 15; matrix products, arithmetic and copies ran while one was open for 13% -> 12% of each run, Pallas kernels for 42% -> 42%
where the time goes in v5:
time: 235 us; the launch traced here: 234 us
  Pallas kernels  99.3 us (42%)
  waiting for transfers between devices  55.1 us (23%)
  starting transfers between devices  29.8 us (13%)
  matrix products  17.3 us (7%)
  between operations  15.6 us (7%)
  other arithmetic  11.8 us (5%)
  local copies, waits for them, and re-layouts  5.07 us (2%)
    ppermute x6, waiting for transfers between devices, permute(): return lax.ppermute(value, 'head', self.plan[name])  31.2 us
    ppermute x8, waiting for transfers between devices, permute(): return lax.ppermute(value, 'tm', [(i, i ^ mask) for i in range(count)])  17.8 us
    dot_general x4, matrix products, dot(): lax.dot_general(a, b, (((da,), (db,)), ((), ())), preferred_element_type=...  17.3 us
    pallas_call x1, Pallas kernels, accumulate(): pl.pallas_call(functools.partial(early_kernel, [len(x) for x in inputs]),...  15.5 us
    pallas_call x2, Pallas kernels, per_device(): pl.pallas_call(back_kernel, grid=(heads // many,), in_specs=[pl.BlockSpec...  15.3 us
    pallas_call x2, Pallas kernels, per_device(): pl.pallas_call(functools.partial(grad_kernel, [len(arrays)]), grid_spec=p...  15.1 us
    ppermute x6, starting transfers between devices, permute(): return lax.ppermute(value, 'head', self.plan[name])  15.1 us
    pallas_call x1, Pallas kernels, rows_of(): pl.pallas_call(functools.partial(rows_kernel, counts), grid_spec=pltpu.Pr...  12.8 us
  transfers between devices with their start and end apart: 21, of which 15 were waited for; matrix products, arithmetic and copies ran while one was open for 12% of the time, Pallas kernels for 42%

profile of v5, /device:TPU:16, one launch (start us, length us, event | category | flops | bytes accessed | tf_op | source)
XLA Modules:
  0.0 233.9 jit_solution(900364358349102942)
XLA Ops:
  15.3 6.6 %block_states.1 = (f32[8,2,128,128]{3,2,1,0:T(8,128)}, f32[8,128,128]{2,1,0:T(8,128)}, f32[8,8,128]{2,1,0:T(8,128)}, bf16[8,160,128]{2,1,0:T(8,128)(2,1)}) custom-call(f32[8,8,1024]{2,1,0:T(8,128)} %factors.1, bf16[1024,1024]{1,0:T(8,128)(2,1)} %k.9, bf16[1024,1024]{1,0:T(8,128)(2,1)} %v.9), custom_call_target="tpu_custom_call" | custom-call | flops 1 | bytes 1 | tf_op jit(solution)/shard_map/block_states/pallas_call | solution.py:521
  25.7 10.0 %pair_weights.1 = (bf16[8,2,768,256]{3,2,1,0:T(8,128)(2,1)}, f32[1024,1024]{1,0:T(8,128)}) custom-call(f32[8,8,1024]{2,1,0:T(8,128)} %factors.1, bf16[1024,1024]{1,0:T(8,128)(2,1)} %q.11, bf16[1024,1024]{1,0:T(8,128)(2,1)} %k.9, bf16[1024,1024]{1,0:T(8,128)(2,1)} %v.9), custom_call_target="tpu_custom_call" | custom-call | flops 1 | bytes 1 | tf_op jit(solution)/shard_map/pair_weights/pallas_call | solution.py:540
  35.7 19.9 %collective-permute-done.refs_1_ = bf16[1024,1024]{1,0:T(8,128)(2,1)S(1)} collective-permute-done((bf16[1024,1024]{1,0:T(8,128)(2,1)}, bf16[1024,1024]{1,0:T(8,128)(2,1)S(1)}, u32[]{:S(2)}, u32[]{:S(2)}) %collective-permute-start) | collective-permute-done | bytes 2097184 | tf_op jit(solution)/shard_map/ppermute | solution.py:372
  55.6 3.3 %collective-permute-done.1.refs_2_ = bf16[1024,1024]{1,0:T(8,128)(2,1)} collective-permute-done((bf16[1024,1024]{1,0:T(8,128)(2,1)}, bf16[1024,1024]{1,0:T(8,128)(2,1)}, u32[]{:S(2)}, u32[]{:S(2)}) %collective-permute-start.1) | collective-permute-done | bytes 2097184 | tf_op jit(solution)/shard_map/ppermute | solution.py:372
  58.9 2.8 %collective-permute-start.3 = (bf16[1024,1024]{1,0:T(8,128)(2,1)}, bf16[1024,1024]{1,0:T(8,128)(2,1)}, u32[]{:S(2)}, u32[]{:S(2)}) collective-permute-start(bf16[1024,1024]{1,0:T(8,128)(2,1)} %collective-permute-done.1.refs_2_), channel_id=1, source_target_pairs={{1,0},{2,3},{5,4},{6,7},{9,8},{10,11},{13,12},{14,15},{17,16},{18,... | collective-permute-start | bytes 6291464 | tf_op jit(solution)/shard_map/ppermute | solution.py:372
  68.7 6.9 %collective-permute-done.6 = bf16[8,160,128]{2,1,0:T(8,128)(2,1)S(1)} collective-permute-done((bf16[8,160,128]{2,1,0:T(8,128)(2,1)S(1)}, bf16[8,160,128]{2,1,0:T(8,128)(2,1)S(1)}, u32[]{:S(2)}, u32[]{:S(2)}) %collective-permute-start.6) | collective-permute-done | bytes 327712 | tf_op jit(solution)/shard_map/ppermute | solution.py:281
  75.6 4.7 %collective-permute-done.5 = bf16[8,160,128]{2,1,0:T(8,128)(2,1)S(1)} collective-permute-done((bf16[8,160,128]{2,1,0:T(8,128)(2,1)S(1)}, bf16[8,160,128]{2,1,0:T(8,128)(2,1)S(1)}, u32[]{:S(2)}, u32[]{:S(2)}) %collective-permute-start.5) | collective-permute-done | bytes 327712 | tf_op jit(solution)/shard_map/ppermute | solution.py:281
  81.4 5.9 %mixed_rows.1 = (bf16[1024,1024]{1,0:T(8,128)(2,1)}, bf16[8,2,128,128]{3,2,1,0:T(8,128)(2,1)}) custom-call(f32[8,8,1024]{2,1,0:T(8,128)} %factors.1, bf16[1024,1024]{1,0:T(8,128)(2,1)} %q.11, f32[1024,1024]{1,0:T(8,128)} %get-tuple-element.67.within, f32[8,2,128,128]{3,2,1,0:T(8,128)} %get-tuple-element.72.parts, f32[8,128,128]{2,1,0:T(8,128)} %fusion.6.start), custom_call_target="tpu_custom_call" | custom-call | flops 1 | bytes 1 | tf_op jit(solution)/shard_map/mixed_rows/pallas_call | solution.py:553
  87.3 12.8 %weight_rows.1 = bf16[4096,1024]{1,0:T(8,128)(2,1)} custom-call(s32[3]{0:T(128)} %pad_add_fusion.order, bf16[1024,1024]{1,0:T(8,128)(2,1)} %refs_0_.3, bf16[1024,1024]{1,0:T(8,128)(2,1)} %copy-done.2, bf16[1024,1024]{1,0:T(8,128)(2,1)} %get-tuple-element.76.refs_2_), custom_call_target="tpu_custom_call" | custom-call | flops 1 | bytes 1 | tf_op jit(solution)/shard_map/weight_rows/pallas_call | solution.py:583
  100.1 4.8 %convolution_convert_fusion.1 = bf16[1024,1024]{1,0:T(8,128)(2,1)S(1)} fusion(bf16[1024,1024]{1,0:T(8,128)(2,1)} %collective-permute-done.1.refs_2_, bf16[1024,1024]{1,0:T(8,128)(2,1)} %get-tuple-element.76.refs_2_), kind=kOutput, calls=%fused_computation.5 | convolution fusion | flops 2148532224 | bytes 6291456 | tf_op jit(solution)/shard_map/dot_general | solution.py:21
  104.9 5.2 %collective-permute-done.4.rows.refs_0_ = bf16[1024,1024]{1,0:T(8,128)(2,1)S(1)} collective-permute-done((bf16[1024,1024]{1,0:T(8,128)(2,1)}, bf16[1024,1024]{1,0:T(8,128)(2,1)S(1)}, u32[]{:S(2)}, u32[]{:S(2)}) %collective-permute-start.4) | collective-permute-done | bytes 2097184 | tf_op jit(solution)/shard_map/ppermute | solution.py:372
  110.1 6.2 %add_dynamic-update-slice_fusion = bf16[4096,1024]{1,0:T(8,128)(2,1)} fusion(bf16[4096,1024]{1,0:T(8,128)(2,1)} %weight_rows.1, s32[]{:T(128)S(6)} %select_n.213, bf16[1024,1024]{1,0:T(8,128)(2,1)S(1)} %convolution_convert_fusion.1, bf16[1024,1024]{1,0:T(8,128)(2,1)} %collective-permute-done.3.refs_3_, bf16[1024,1024]{1,0:T(8,128)(2,1)S(1)} %copy-done.4), kind=kOutput, calls=%fused_computation.3 | convolution fusion | flops 2152726528 | bytes 8388612 | tf_op jit(solution)/shard_map/dot_general | solution.py:21
  120.4 15.5 %early_product.1.early = f32[1024,1024]{1,0:T(8,128)} custom-call(s32[4]{0:T(128)} %fusion.30.order, bf16[1024,1024]{1,0:T(8,128)(2,1)} %refs_0_.3, bf16[1024,1024]{1,0:T(8,128)(2,1)} %copy-done.2, bf16[1024,1024]{1,0:T(8,128)(2,1)} %collective-permute-done.1.refs_2_, bf16[1024,1024]{1,0:T(8,128)(2,1)} %collective-permute-done.3.refs_3_, ...), custom_call_target="tpu_custom_call" | custom-call | flops 1 | bytes 1 | tf_op jit(solution)/shard_map/early_product/pallas_call | solution.py:613
  137.9 2.8 %collective-permute-done.8.refs_1_ = bf16[512,1024]{1,0:T(8,128)(2,1)S(1)} collective-permute-done((bf16[512,1024]{1,0:T(8,128)(2,1)}, bf16[512,1024]{1,0:T(8,128)(2,1)S(1)}, u32[]{:S(2)}, u32[]{:S(2)}) %collective-permute-start.8) | collective-permute-done | bytes 1048608 | tf_op jit(solution)/shard_map/ppermute | solution.py:372
  140.7 5.3 %collective-permute-start.9 = (bf16[512,1024]{1,0:T(8,128)(2,1)}, bf16[512,1024]{1,0:T(8,128)(2,1)}, u32[]{:S(2)}, u32[]{:S(2)}) collective-permute-start(bf16[512,1024]{1,0:T(8,128)(2,1)} %cut_rows.3), channel_id=1, source_target_pairs={{1,0},{2,3},{5,4},{6,7},{9,8},{10,11},{13,12},{14,15},{17,16},{18,... | collective-permute-start | bytes 3145736 | tf_op jit(solution)/shard_map/ppermute | solution.py:372
  146.8 7.4 %grad_mixed_rows.2 = (bf16[512,1024]{1,0:T(8,128)(2,1)}, f32[8,128,128]{2,1,0:T(8,128)}, f32[8,128,128]{2,1,0:T(8,128)}, bf16[8,128,128]{2,1,0:T(8,128)(2,1)}) custom-call(s32[4]{0:T(128)} %fusion.30.order, f32[8,8,1024]{2,1,0:T(8,128)} %factors.1, bf16[1024,1024]{1,0:T(8,128)(2,1)} %q.11, f32[1024,1024]{1,0:T(8,128)} %early_product.1.early, ...), custom_call_target="tpu_custom_call" | custom-call | flops 1 | bytes 1 | tf_op jit(solution)/shard_map/grad_mixed_rows/pallas_call | solution.py:667
  156.2 2.6 %convolution_convert_fusion = bf16[1024,1024]{1,0:T(8,128)(2,1)} fusion(bf16[512,1024]{1,0:T(8,128)(2,1)S(1)} %slice_add_fusion, bf16[1024,1024]{1,0:T(8,128)(2,1)S(1)} %copy-done.5), kind=kOutput, calls=%fused_computation.4 | convolution fusion | flops 1074790400 | bytes 4194304 | tf_op jit(solution)/shard_map/dot_general | solution.py:21
  158.8 7.7 %block_gradients.2 = (bf16[1024,1024]{1,0:T(8,128)(2,1)}, bf16[1024,1024]{1,0:T(8,128)(2,1)}, bf16[1024,1024]{1,0:T(8,128)(2,1)}) custom-call(f32[8,8,1024]{2,1,0:T(8,128)} %factors.1, bf16[1024,1024]{1,0:T(8,128)(2,1)} %q.11, bf16[1024,1024]{1,0:T(8,128)(2,1)} %k.9, bf16[1024,1024]{1,0:T(8,128)(2,1)} %v.9, bf16[512,1024]{1,0:T(8,128)(2,1)} %get-tuple-element.85.e, ...), custom_call_target="tpu_custom_call" | custom-call | flops 1 | bytes 1 | tf_op jit(solution)/shard_map/block_gradients/pallas_call | solution.py:702
  166.4 3.7 %add_convert_fusion = bf16[1024,1024]{1,0:T(8,128)(2,1)S(1)} fusion(bf16[1024,1024]{1,0:T(8,128)(2,1)} %convolution_convert_fusion, bf16[1024,1024]{1,0:T(8,128)(2,1)} %get-tuple-element.76.refs_2_, bf16[512,1024]{1,0:T(8,128)(2,1)} %collective-permute-done.9.refs_1_, bf16[1024,1024]{1,0:T(8,128)(2,1)S(1)} %copy-done.1), kind=kOutput, calls=%fused_computation | convolution fusion | flops 1077411840 | bytes 7340032 | tf_op jit(solution)/shard_map/dot_general | solution.py:21
  171.3 7.7 %grad_mixed_rows.3 = (bf16[512,1024]{1,0:T(8,128)(2,1)}, f32[8,128,128]{2,1,0:T(8,128)}, f32[8,128,128]{2,1,0:T(8,128)}, bf16[8,128,128]{2,1,0:T(8,128)(2,1)}) custom-call(s32[4]{0:T(128)} %fusion.30.order, f32[8,8,1024]{2,1,0:T(8,128)} %factors.1, bf16[1024,1024]{1,0:T(8,128)(2,1)} %q.11, f32[1024,1024]{1,0:T(8,128)} %early_product.1.early, ...), custom_call_target="tpu_custom_call" | custom-call | flops 1 | bytes 1 | tf_op jit(solution)/shard_map/grad_mixed_rows/pallas_call | solution.py:667
  186.8 4.7 %collective-permute-start.14 = (bf16[8,128,128]{2,1,0:T(8,128)(2,1)S(1)}, bf16[8,128,128]{2,1,0:T(8,128)(2,1)S(1)}, u32[]{:S(2)}, u32[]{:S(2)}) collective-permute-start(bf16[8,128,128]{2,1,0:T(8,128)(2,1)S(1)} %fusion.7), channel_id=1, source_target_pairs={{0,24},{4,28},{8,16},{12,20},{16,8},{20,12},{24,0},{28,4},{1,25},{... | collective-permute-start | bytes 786440 | tf_op jit(solution)/shard_map/ppermute | solution.py:281
  192.2 7.6 %block_gradients.3 = (bf16[1024,1024]{1,0:T(8,128)(2,1)}, bf16[1024,1024]{1,0:T(8,128)(2,1)}, bf16[1024,1024]{1,0:T(8,128)(2,1)}) custom-call(f32[8,8,1024]{2,1,0:T(8,128)} %factors.1, bf16[1024,1024]{1,0:T(8,128)(2,1)} %q.11, bf16[1024,1024]{1,0:T(8,128)(2,1)} %k.9, ...), custom_call_target="tpu_custom_call", output_to_operand_aliasing={{0}: (7, {}), {1}: (8, {}), {2}: (9, {})} | custom-call | flops 1 | bytes 1 | tf_op jit(solution)/shard_map/block_gradients/pallas_call | solution.py:702
  212.4 6.8 %carried_gradients.1 = (bf16[1024,1024]{1,0:T(8,128)(2,1)}, bf16[1024,1024]{1,0:T(8,128)(2,1)}) custom-call(f32[8,8,1024]{2,1,0:T(8,128)} %factors.1, bf16[1024,1024]{1,0:T(8,128)(2,1)} %k.9, bf16[1024,1024]{1,0:T(8,128)(2,1)} %v.9, bf16[1024,1024]{1,0:T(8,128)(2,1)} %get-tuple-element.106.dk_part, bf16[1024,1024]{1,0:T(8,128)(2,1)} %get-tuple-element.107.dv_part, ...), custom_call_target="tpu_custom_call" | custom-call | flops 1 | bytes 1 | tf_op jit(solution)/shard_map/carried_gradients/pallas_call | solution.py:727
  224.2 2.9 %fusion = f32[512,1024]{1,0:T(8,128)} fusion(f32[512,512]{1,0:T(8,128)S(1)} %convert_add_fusion, f32[512,512]{1,0:T(8,128)S(1)} %convert_add_fusion.1, bf16[512,1024]{1,0:T(8,128)(2,1)} %reduce-scatter.2.cloned.1.call-done, pred[]{:T(512)S(6)} %eq.13), kind=kLoop, calls=%fused_computation.2 | loop fusion | flops 2097152 | bytes 5242881 | tf_op jit(solution)/shard_map/add | solution.py:749
  (92 shorter events, 54.6 us)
Async XLA Ops:
  7.2 113.2 %all-gather.2.cloned.1.call-start = ((), (), s32[]{:S(2)}) async-start(), calls=%async_computation.1 | async-start | bytes 9437184 | tf_op jit(solution)/shard_map/all_gather | solution.py:490
  7.9 216.3 %reduce-scatter.2.cloned.1.call-start = ((), (), s32[]{:S(2)}) async-start(), calls=%async_computation.2 | async-start | bytes 9437184 | tf_op jit(solution)/shard_map/reduce_scatter | solution.py:646
  7.9 47.6 %collective-permute-start = (bf16[1024,1024]{1,0:T(8,128)(2,1)}, bf16[1024,1024]{1,0:T(8,128)(2,1)S(1)}, u32[]{:S(2)}, u32[]{:S(2)}) collective-permute-start(bf16[1024,1024]{1,0:T(8,128)(2,1)} %refs_0_.3), channel_id=1, source_target_pairs={{1,0},{0,1},{3,2},{2,3},{5,4},{4,5},{7,6},{6,7},{9,8},{8,9},{11,10... | collective-permute-start | bytes 6291464 | tf_op jit(solution)/shard_map/ppermute | solution.py:372
  9.6 49.3 %collective-permute-start.1 = (bf16[1024,1024]{1,0:T(8,128)(2,1)}, bf16[1024,1024]{1,0:T(8,128)(2,1)}, u32[]{:S(2)}, u32[]{:S(2)}) collective-permute-start(bf16[1024,1024]{1,0:T(8,128)(2,1)} %refs_0_.3), channel_id=1, source_target_pairs={{2,1},{1,2},{6,5},{5,6},{10,9},{9,10},{14,13},{13,14},{18,17},{17,... | collective-permute-start | bytes 6291464 | tf_op jit(solution)/shard_map/ppermute | solution.py:372
  21.9 1.8 collective-permute-start.2
  58.9 46.0 %collective-permute-start.3 = (bf16[1024,1024]{1,0:T(8,128)(2,1)}, bf16[1024,1024]{1,0:T(8,128)(2,1)}, u32[]{:S(2)}, u32[]{:S(2)}) collective-permute-start(bf16[1024,1024]{1,0:T(8,128)(2,1)} %collective-permute-done.1.refs_2_), channel_id=1, source_target_pairs={{1,0},{2,3},{5,4},{6,7},{9,8},{10,11},{13,12},{14,15},{17,16},{18,... | collective-permute-start | bytes 6291464 | tf_op jit(solution)/shard_map/ppermute | solution.py:372
  61.7 48.4 %collective-permute-start.4 = (bf16[1024,1024]{1,0:T(8,128)(2,1)}, bf16[1024,1024]{1,0:T(8,128)(2,1)S(1)}, u32[]{:S(2)}, u32[]{:S(2)}) collective-permute-start(bf16[1024,1024]{1,0:T(8,128)(2,1)} %copy-done.2), channel_id=1, source_target_pairs={{2,1},{1,2},{6,5},{5,6},{10,9},{9,10},{14,13},{13,14},{18,17},{17,... | collective-permute-start | bytes 6291464 | tf_op jit(solution)/shard_map/ppermute | solution.py:372
  63.9 11.7 %collective-permute-start.6 = (bf16[8,160,128]{2,1,0:T(8,128)(2,1)S(1)}, bf16[8,160,128]{2,1,0:T(8,128)(2,1)S(1)}, u32[]{:S(2)}, u32[]{:S(2)}) collective-permute-start(bf16[8,160,128]{2,1,0:T(8,128)(2,1)S(1)} %pad_maximum_fusion), channel_id=1, source_target_pairs={{0,24},{4,28},{8,16},{12,20},{16,8},{20,12},{24,0},{28,4},{1,25},{... | collective-permute-start | bytes 983048 | tf_op jit(solution)/shard_map/ppermute | solution.py:281
  66.4 13.8 %collective-permute-start.5 = (bf16[8,160,128]{2,1,0:T(8,128)(2,1)S(1)}, bf16[8,160,128]{2,1,0:T(8,128)(2,1)S(1)}, u32[]{:S(2)}, u32[]{:S(2)}) collective-permute-start(bf16[8,160,128]{2,1,0:T(8,128)(2,1)S(1)} %pad_maximum_fusion), channel_id=1, source_target_pairs={{0,16},{4,20},{8,24},{12,28},{16,0},{20,4},{24,8},{28,12},{1,17},{... | collective-permute-start | bytes 983048 | tf_op jit(solution)/shard_map/ppermute | solution.py:281
  66.9 13.4 %collective-permute-start.7 = (bf16[8,160,128]{2,1,0:T(8,128)(2,1)S(1)}, bf16[8,160,128]{2,1,0:T(8,128)(2,1)S(1)}, u32[]{:S(2)}, u32[]{:S(2)}) collective-permute-start(bf16[8,160,128]{2,1,0:T(8,128)(2,1)S(1)} %pad_maximum_fusion), channel_id=1, source_target_pairs={{0,8},{4,12},{8,0},{12,4},{16,24},{20,28},{24,16},{28,20},{1,9},{5... | collective-permute-start | bytes 983048 | tf_op jit(solution)/shard_map/ppermute | solution.py:281
  100.1 10.0 %copy-start.4 = (bf16[1024,1024]{1,0:T(8,128)(2,1)S(1)}, bf16[1024,1024]{1,0:T(8,128)(2,1)}, u32[]{:S(2)}) copy-start(bf16[1024,1024]{1,0:T(8,128)(2,1)} %get-tuple-element.76.refs_2_) | copy-start | bytes 6291460
  118.4 22.3 %collective-permute-start.8 = (bf16[512,1024]{1,0:T(8,128)(2,1)}, bf16[512,1024]{1,0:T(8,128)(2,1)S(1)}, u32[]{:S(2)}, u32[]{:S(2)}) collective-permute-start(bf16[512,1024]{1,0:T(8,128)(2,1)} %cut_rows.2), channel_id=1, source_target_pairs={{1,0},{2,3},{5,4},{6,7},{9,8},{10,11},{13,12},{14,15},{17,16},{18,... | collective-permute-start | bytes 3145736 | tf_op jit(solution)/shard_map/ppermute | solution.py:372
  140.7 25.7 %collective-permute-start.9 = (bf16[512,1024]{1,0:T(8,128)(2,1)}, bf16[512,1024]{1,0:T(8,128)(2,1)}, u32[]{:S(2)}, u32[]{:S(2)}) collective-permute-start(bf16[512,1024]{1,0:T(8,128)(2,1)} %cut_rows.3), channel_id=1, source_target_pairs={{1,0},{2,3},{5,4},{6,7},{9,8},{10,11},{13,12},{14,15},{17,16},{18,... | collective-permute-start | bytes 3145736 | tf_op jit(solution)/shard_map/ppermute | solution.py:372
  171.3 7.7 %collective-permute-start.11 = (bf16[512,1024]{1,0:T(8,128)(2,1)S(1)}, bf16[512,1024]{1,0:T(8,128)(2,1)S(1)}, u32[]{:S(2)}, u32[]{:S(2)}) collective-permute-start(bf16[512,1024]{1,0:T(8,128)(2,1)S(1)} %get-tuple-element.149), channel_id=1, source_target_pairs={{0,4},{4,0},{8,12},{12,8},{16,20},{20,16},{24,28},{28,24},{1,5},{5... | collective-permute-start | bytes 3145736 | tf_op jit(solution)/shard_map/ppermute | solution.py:599
  179.0 7.7 %copy-start.7 = (f32[8,128,128]{2,1,0:T(8,128)S(1)}, f32[8,128,128]{2,1,0:T(8,128)}, u32[]{:S(2)}) copy-start(f32[8,128,128]{2,1,0:T(8,128)} %get-tuple-element.101) | copy-start | bytes 1572868
  182.4 17.4 %collective-permute-start.15 = (bf16[512,512]{1,0:T(8,128)(2,1)}, bf16[512,512]{1,0:T(8,128)(2,1)S(1)}, u32[]{:S(2)}, u32[]{:S(2)}) collective-permute-start(bf16[512,512]{1,0:T(8,128)(2,1)} %get-tuple-element.99.refs_0_), channel_id=1, source_target_pairs={{0,16},{1,17},{4,20},{5,21},{8,24},{9,25},{12,28},{13,29},{18,2},{... | collective-permute-start | bytes 1572872 | tf_op jit(solution)/shard_map/ppermute | solution.py:462
  183.7 16.8 %collective-permute-start.16 = (bf16[512,512]{1,0:T(8,128)(2,1)}, bf16[512,512]{1,0:T(8,128)(2,1)S(1)}, u32[]{:S(2)}, u32[]{:S(2)}) collective-permute-start(bf16[512,512]{1,0:T(8,128)(2,1)} %get-tuple-element.115.refs_1_), channel_id=1, source_target_pairs={{0,8},{1,9},{4,12},{5,13},{10,2},{11,3},{14,6},{15,7},{16,24},{17,... | collective-permute-start | bytes 1572872 | tf_op jit(solution)/shard_map/ppermute | solution.py:462
  185.0 1.7 collective-permute-start.10
  186.8 21.5 %collective-permute-start.14 = (bf16[8,128,128]{2,1,0:T(8,128)(2,1)S(1)}, bf16[8,128,128]{2,1,0:T(8,128)(2,1)S(1)}, u32[]{:S(2)}, u32[]{:S(2)}) collective-permute-start(bf16[8,128,128]{2,1,0:T(8,128)(2,1)S(1)} %fusion.7), channel_id=1, source_target_pairs={{0,24},{4,28},{8,16},{12,20},{16,8},{20,12},{24,0},{28,4},{1,25},{... | collective-permute-start | bytes 786440 | tf_op jit(solution)/shard_map/ppermute | solution.py:281
  191.5 18.9 %collective-permute-start.13 = (bf16[8,128,128]{2,1,0:T(8,128)(2,1)S(1)}, bf16[8,128,128]{2,1,0:T(8,128)(2,1)S(1)}, u32[]{:S(2)}, u32[]{:S(2)}) collective-permute-start(bf16[8,128,128]{2,1,0:T(8,128)(2,1)S(1)} %fusion.7), channel_id=1, source_target_pairs={{0,16},{4,20},{8,24},{12,28},{16,0},{20,4},{24,8},{28,12},{1,17},{... | collective-permute-start | bytes 786440 | tf_op jit(solution)/shard_map/ppermute | solution.py:281
  191.5 19.8 %collective-permute-start.12 = (bf16[8,128,128]{2,1,0:T(8,128)(2,1)S(1)}, bf16[8,128,128]{2,1,0:T(8,128)(2,1)S(1)}, u32[]{:S(2)}, u32[]{:S(2)}) collective-permute-start(bf16[8,128,128]{2,1,0:T(8,128)(2,1)S(1)} %fusion.7), channel_id=1, source_target_pairs={{0,8},{4,12},{8,0},{12,4},{16,24},{20,28},{24,16},{28,20},{1,9},{5... | collective-permute-start | bytes 786440 | tf_op jit(solution)/shard_map/ppermute | solution.py:281
  203.7 17.6 %collective-permute-start.18 = (bf16[512,512]{1,0:T(8,128)(2,1)}, bf16[512,512]{1,0:T(8,128)(2,1)S(1)}, u32[]{:S(2)}, u32[]{:S(2)}) collective-permute-start(bf16[512,512]{1,0:T(8,128)(2,1)} %get-tuple-element.120), channel_id=1, source_target_pairs={{8,24},{9,25},{12,28},{13,29},{18,2},{19,3},{22,6},{23,7}} | collective-permute-start | bytes 1572872 | tf_op jit(solution)/shard_map/ppermute | solution.py:462
  205.0 18.8 %collective-permute-start.17 = (bf16[512,512]{1,0:T(8,128)(2,1)}, bf16[512,512]{1,0:T(8,128)(2,1)S(1)}, u32[]{:S(2)}, u32[]{:S(2)}) collective-permute-start(bf16[512,512]{1,0:T(8,128)(2,1)} %get-tuple-element.118), channel_id=1, source_target_pairs={{10,2},{11,3},{14,6},{15,7},{16,24},{17,25},{20,28},{21,29}} | collective-permute-start | bytes 1572872 | tf_op jit(solution)/shard_map/ppermute | solution.py:462
  212.3 11.5 %copy-start.9 = (bf16[512,512]{1,0:T(8,128)(2,1)S(1)}, bf16[512,512]{1,0:T(8,128)(2,1)}, u32[]{:S(2)}) copy-start(bf16[512,512]{1,0:T(8,128)(2,1)} %get-tuple-element.120) | copy-start | bytes 1572868
  (11 other events, 45.0 us)
Sparse Core Ops, SparseCore 0:
  9.9 55.4 all-gather.1
  116.5 71.2 reduce-scatter.1
